TPU v7x, 128 devices: a whole 4x4x4 slice. The times are simulated.
128 devices in a mesh: space: 16 (over y, z), freq: 8 (over x, core).
Axes of the slice: x: 4, y: 4, z: 4, core: 2. Of those that a mesh axis runs over, the one named last changes fastest.
Arguments:
- source: float32 [2, 16, 128, 32768], P(None, None, 'space', 'freq'), may hold values from -6 to 6
- angles: float32 [4, 16, 128, 32768], P(None, None, 'space', 'freq'), may hold values from -3.140625 to 3.140625
- cheb_tables: float32 [4, 4, 2, 2, 16, 16], replicated, may hold values from -1 to 1
- switch_kernel: float32 [2, 16, 16], replicated, may hold values from -1 to 1
- box_class: int32 [4, 128], replicated, may hold values from 0 to 3
Outputs:
- spectrum: float32 [2, 16, 128, 32768], P(None, None, 'space', 'freq')
All inputs are finite; a program needn't handle non-finite values.
Results may differ from a plain program's by a relative error of at most 0.0003.
Values sent between devices are 32-bit elements; how exact they have to be, the bound alone decides.
No kernel may reach another device: no remote copies, remote signals or barrier semaphores. Data moves between devices by JAX's collectives and lax.ppermute only.
A program may use at most 256 MiB of HBM per device.

v0:
```python
import jax
import jax.numpy as jnp
from jax import lax
from jax.sharding import PartitionSpec as P

LEVELS = 4
NCLASS = 4


def swapped(array, axis, distance):
    return lax.ppermute(array, axis, [(i, i ^ 1 << distance) for i in range(lax.axis_size(axis))])


def rotate(values, phases):
    cosine = jnp.cos(phases)
    sine_part = jnp.sin(phases)
    return jnp.stack(
        [cosine * values[0] - sine_part * values[1], sine_part * values[0] + cosine * values[1]]
    )


def apply_boxes(weight, values):
    return jnp.einsum("pts,cspf->ctpf", weight, values, precision=lax.Precision.HIGHEST)


def apply_kernel(kernel, values):
    full_shape = values.shape
    flattened = values.reshape(2, full_shape[1], -1)
    real_part = jnp.dot(kernel[0], flattened[0], precision=lax.Precision.HIGHEST) - jnp.dot(
        kernel[1], flattened[1], precision=lax.Precision.HIGHEST
    )
    imag_part = jnp.dot(kernel[0], flattened[1], precision=lax.Precision.HIGHEST) + jnp.dot(
        kernel[1], flattened[0], precision=lax.Precision.HIGHEST
    )
    return jnp.stack([real_part, imag_part]).reshape(full_shape)


def box_tables(table_level, classes_level, first_box, box_count, own_half):
    local_classes = lax.dynamic_slice_in_dim(classes_level, first_box, box_count)
    onehot = (local_classes[:, None] == jnp.arange(NCLASS)[None, :]).astype(jnp.float32)
    chosen = jnp.where(own_half == 1, table_level[:, 1], table_level[:, 0])
    return jnp.einsum("pk,kjts->pjts", onehot, chosen, precision=lax.Precision.HIGHEST)


def level_update(current, phases, table_level, classes_level, level_number):
    bit_count = lax.axis_size("space").bit_length() - 1
    partner_bit = level_number % bit_count
    device_index = lax.axis_index("space")
    box_count = current.shape[2]
    own_half = device_index >> partner_bit & 1
    rotated = rotate(current, phases)
    own_tables = box_tables(
        table_level, classes_level, device_index * box_count, box_count, own_half
    )
    w_self = jnp.where(own_half == 1, own_tables[:, 1], own_tables[:, 0])
    w_other = jnp.where(own_half == 1, own_tables[:, 0], own_tables[:, 1])
    partner = swapped(rotated, "space", partner_bit)
    return apply_boxes(w_self, rotated) + apply_boxes(w_other, partner)


def switch_level(current, switch_kernel):
    full_shape = current.shape
    freq_count = lax.axis_size("freq")
    blocks = current.reshape(
        full_shape[0], full_shape[1], full_shape[2], freq_count, full_shape[3] // freq_count
    )
    regrouped = lax.all_to_all(
        apply_kernel(switch_kernel, blocks), "freq", split_axis=3, concat_axis=3, tiled=True
    )
    return regrouped.reshape(full_shape)


def on_device(source, angles, cheb_tables, switch_kernel, box_class):
    current = source
    for level_number in range(LEVELS):
        current = level_update(
            current,
            angles[level_number],
            cheb_tables[level_number],
            box_class[level_number],
            level_number,
        )
        if level_number == LEVELS // 2 - 1:
            current = switch_level(current, switch_kernel)
    return current


def solution(mesh):
    in_specs = (P(None, None, "space", "freq"), P(None, None, "space", "freq"), P(), P(), P())
    out_specs = P(None, None, "space", "freq")
    return jax.shard_map(
        on_device, mesh=mesh, in_specs=in_specs, out_specs=out_specs, check_vma=False
    )
```

profile of v0, /device:TPU:0, one launch (start us, length us, event | category | flops | bytes accessed | tf_op | source)
XLA Modules:
  0.0 522.9 jit_solution(3343470328594196291)
XLA Ops:
  0.0 6.5 %fusion.54 = (f32[1,16,8,4096]{3,2,1,0:T(8,128)}, f32[1,16,8,4096]{3,2,1,0:T(8,128)}, f32[1,16,8,4096]{3,2,1,0:T(8,128)}, f32[1,16,8,4096]{3,2,1,0:T(8,128)S(1)}) fusion(f32[4,16,8,4096]{3,2,1,0:T(8,128)} %param.6), kind=kLoop, calls=%fused_computation.101 | loop fusion | bytes 16777216 | tf_op jit(solution)/shard_map/slice | solution.py:78
  6.5 0.0 copy-done.4
  6.5 0.5 fusion.57
  6.9 9.0 %multiply_subtract_fusion.3 = (f32[1,16,8,4096]{3,1,0,2:T(8,128)S(1)}, f32[1,16,8,4096]{3,1,0,2:T(8,128)S(1)}) fusion(f32[1,16,8,4096]{3,2,1,0:T(8,128)S(1)} %get-tuple-element.22, f32[1,16,8,4096]{3,2,1,0:T(8,128)S(1)} %get-tuple-element.21, f32[1,16,8,4096]{3,2,1,0:T(8,128)S(1)} %get-tuple-element.8), kind=kLoop, calls=%fused_computation.22 | loop fusion | flops 3145728 | bytes 10485760 | tf_op jit(solution)/shard_map/sub | solution.py:18
  15.9 0.0 copy-start
  15.9 0.0 copy-start.7
  15.9 0.0 copy-start.5
  16.0 2.3 pad_maximum_fusion
  18.3 0.4 copy-done
  18.6 2.2 collective-permute-start
  20.8 0.0 copy-done.7
  20.8 0.1 fusion.50
  20.9 0.0 copy-done.5
  21.0 0.3 fusion.26
  21.3 5.6 %fusion.18 = f32[8,2,4096,16]{2,3,1,0:T(8,128)S(1)} fusion(f32[8,16,16,1]{2,0,1,3:T(8,128)S(1)} %get-tuple-element.34, f32[1,16,8,4096]{3,1,0,2:T(8,128)} %copy-done, f32[1,16,8,4096]{3,1,0,2:T(8,128)S(1)} %get-tuple-element.15), kind=kOutput, calls=%fused_computation.53 | convolution fusion | flops 202375168 | bytes 8396800 | tf_op jit(solution)/shard_map/pts,cspf->ctpf/dot_general | solution.py:23
  26.9 84.8 %collective-permute-done = f32[2,16,8,4096]{3,1,0,2:T(8,128)} collective-permute-done((f32[2,16,8,4096]{3,1,0,2:T(8,128)}, f32[2,16,8,4096]{3,1,0,2:T(8,128)}, u32[]{:S(2)}, u32[]{:S(2)}) %collective-permute-start) | collective-permute-done | bytes 4194336 | tf_op jit(solution)/shard_map/ppermute | solution.py:11
  111.7 5.7 %fusion.3 = f32[2,16,8,4096]{3,1,0,2:T(8,128)S(1)} fusion(f32[8,2,4096,16]{2,3,1,0:T(8,128)S(1)} %fusion.18, f32[2,16,8,4096]{3,1,0,2:T(8,128)} %collective-permute-done, f32[8,16,16,1]{2,0,1,3:T(8,128)S(1)} %get-tuple-element.33), kind=kOutput, calls=%fused_computation.9 | convolution fusion | flops 202375168 | bytes 12591104 | tf_op jit(solution)/shard_map/pts,cspf->ctpf/dot_general | solution.py:23
  117.4 0.0 copy-done.3
  117.4 8.3 %multiply_subtract_fusion.2 = (f32[1,16,8,4096]{3,1,0,2:T(8,128)S(1)}, f32[1,16,8,4096]{3,1,0,2:T(8,128)S(1)}) fusion(f32[2,16,8,4096]{3,1,0,2:T(8,128)S(1)} %fusion.3, f32[1,16,8,4096]{3,2,1,0:T(8,128)S(1)} %copy-done.3), kind=kLoop, calls=%fused_computation.20 | loop fusion | flops 3145728 | bytes 10485760 | tf_op jit(solution)/shard_map/sub | solution.py:18
  125.7 0.3 pad_maximum_fusion.1
  126.0 4.2 collective-permute-start.1
  130.2 0.3 fusion.24
  130.5 4.0 fusion.15
  134.5 85.4 %collective-permute-done.1 = f32[2,16,8,4096]{3,1,0,2:T(8,128)S(1)} collective-permute-done((f32[2,16,8,4096]{3,1,0,2:T(8,128)S(1)}, f32[2,16,8,4096]{3,1,0,2:T(8,128)S(1)}, u32[]{:S(2)}, u32[]{:S(2)}) %collective-permute-start.1) | collective-permute-done | bytes 4194336 | tf_op jit(solution)/shard_map/ppermute | solution.py:11
  219.9 4.0 fusion.2
  223.9 0.3 fusion.56
  224.2 0.2 copy.109
  224.4 0.0 copy-start.6
  224.4 0.2 copy.110
  224.6 0.5 copy-done.6
  225.1 1.9 fusion.32
  227.0 2.1 fusion.30
  229.2 1.9 convolution_subtract_fusion
  231.1 1.2 copy.111
  232.3 1.2 copy.64
  233.5 1.9 convolution_add_fusion
  235.5 1.2 copy.112
  236.7 1.2 copy.65
  237.9 0.6 pad_maximum_fusion.2
  238.5 54.6 %all_to_all.5 = f32[2,16,8,8,512]{4,2,1,0,3:T(8,128)S(1)} all-to-all(f32[2,16,8,8,512]{4,2,1,0,3:T(8,128)S(1)} %pad_maximum_fusion.2), channel_id=1, replica_groups=mesh['space'=16,'freq'=8] {'freq'}, dimensions={3} | all-to-all | bytes 8388608 | tf_op jit(solution)/shard_map/all_to_all | solution.py:67
  293.2 2.0 fusion.55
  295.2 1.2 copy.66
  296.4 1.6 squeeze.26
  297.9 2.8 copy.67
  300.7 1.5 squeeze.27
  302.3 9.7 %multiply_subtract_fusion.1 = (f32[1,16,8,4096]{3,1,0,2:T(8,128)S(1)}, f32[1,16,8,4096]{3,1,0,2:T(8,128)S(1)}) fusion(f32[1,16,8,4096]{3,1,0,2:T(8,128)} %squeeze.27, f32[1,16,8,4096]{3,1,0,2:T(8,128)} %squeeze.26, f32[1,16,8,4096]{3,2,1,0:T(8,128)} %get-tuple-element.7), kind=kLoop, calls=%fused_computation.18 | loop fusion | flops 3145728 | bytes 10485760 | tf_op jit(solution)/shard_map/sub | solution.py:18
  311.9 0.0 copy-start.1
  311.9 2.5 pad_maximum_fusion.3
  314.4 0.2 copy-done.1
  314.6 1.6 collective-permute-start.2
  316.2 0.1 fusion.52
  316.3 0.3 fusion.22
  316.6 5.6 %fusion.12 = f32[8,2,4096,16]{2,3,1,0:T(8,128)S(1)} fusion(f32[8,16,16,1]{2,0,1,3:T(8,128)S(1)} %get-tuple-element.30, f32[1,16,8,4096]{3,1,0,2:T(8,128)} %copy-done.1, f32[1,16,8,4096]{3,1,0,2:T(8,128)S(1)} %get-tuple-element.11), kind=kOutput, calls=%fused_computation.47 | convolution fusion | flops 202375168 | bytes 8396800 | tf_op jit(solution)/shard_map/pts,cspf->ctpf/dot_general | solution.py:23
  322.2 84.7 %collective-permute-done.2 = f32[2,16,8,4096]{3,1,0,2:T(8,128)} collective-permute-done((f32[2,16,8,4096]{3,1,0,2:T(8,128)}, f32[2,16,8,4096]{3,1,0,2:T(8,128)}, u32[]{:S(2)}, u32[]{:S(2)}) %collective-permute-start.2) | collective-permute-done | bytes 4194336 | tf_op jit(solution)/shard_map/ppermute | solution.py:11
  406.9 5.7 %fusion.1 = f32[2,16,8,4096]{3,1,0,2:T(8,128)S(1)} fusion(f32[8,2,4096,16]{2,3,1,0:T(8,128)S(1)} %fusion.12, f32[2,16,8,4096]{3,1,0,2:T(8,128)} %collective-permute-done.2, f32[8,16,16,1]{2,0,1,3:T(8,128)S(1)} %get-tuple-element.29), kind=kOutput, calls=%fused_computation.5 | convolution fusion | flops 202375168 | bytes 12591104 | tf_op jit(solution)/shard_map/pts,cspf->ctpf/dot_general | solution.py:23
  412.6 0.0 copy-done.2
  412.6 8.3 %multiply_subtract_fusion = (f32[1,16,8,4096]{3,1,0,2:T(8,128)S(1)}, f32[1,16,8,4096]{3,1,0,2:T(8,128)S(1)}) fusion(f32[2,16,8,4096]{3,1,0,2:T(8,128)S(1)} %fusion.1, f32[1,16,8,4096]{3,2,1,0:T(8,128)S(1)} %copy-done.2), kind=kLoop, calls=%fused_computation.16 | loop fusion | flops 3145728 | bytes 10485760 | tf_op jit(solution)/shard_map/sub | solution.py:18
  420.9 0.3 pad_maximum_fusion.4
  421.2 3.5 collective-permute-start.3
  424.7 0.3 fusion.20
  425.0 4.0 fusion.9
  429.0 85.1 %collective-permute-done.3 = f32[2,16,8,4096]{3,1,0,2:T(8,128)S(1)} collective-permute-done((f32[2,16,8,4096]{3,1,0,2:T(8,128)S(1)}, f32[2,16,8,4096]{3,1,0,2:T(8,128)S(1)}, u32[]{:S(2)}, u32[]{:S(2)}) %collective-permute-start.3) | collective-permute-done | bytes 4194336 | tf_op jit(solution)/shard_map/ppermute | solution.py:11
  514.0 4.0 fusion
  518.1 4.4 copy.74
  (11 shorter events, 0.1 us)
Async XLA Ops:
  0.0 6.5 %copy-start.4 = (f32[2,16,8,4096]{3,2,1,0:T(8,128)S(1)}, f32[2,16,8,4096]{3,2,1,0:T(8,128)}, u32[]{:S(2)}) copy-start(f32[2,16,8,4096]{3,2,1,0:T(8,128)} %param.5) | copy-start | bytes 12582916
  15.9 2.7 copy-start
  15.9 4.9 copy-start.7
  15.9 5.0 copy-start.5
  18.6 93.1 %collective-permute-start = (f32[2,16,8,4096]{3,1,0,2:T(8,128)}, f32[2,16,8,4096]{3,1,0,2:T(8,128)}, u32[]{:S(2)}, u32[]{:S(2)}) collective-permute-start(f32[2,16,8,4096]{3,1,0,2:T(8,128)} %pad_maximum_fusion), channel_id=1, source_target_pairs={{0,8},{8,0},{16,24},{24,16},{32,40},{40,32},{48,56},{56,48},{64,72... | collective-permute-start | bytes 12582920 | tf_op jit(solution)/shard_map/ppermute | solution.py:11
  111.7 5.7 %copy-start.3 = (f32[1,16,8,4096]{3,2,1,0:T(8,128)S(1)}, f32[1,16,8,4096]{3,2,1,0:T(8,128)}, u32[]{:S(2)}) copy-start(f32[1,16,8,4096]{3,2,1,0:T(8,128)} %get-tuple-element.6) | copy-start | bytes 6291460
  126.0 93.9 %collective-permute-start.1 = (f32[2,16,8,4096]{3,1,0,2:T(8,128)S(1)}, f32[2,16,8,4096]{3,1,0,2:T(8,128)S(1)}, u32[]{:S(2)}, u32[]{:S(2)}) collective-permute-start(f32[2,16,8,4096]{3,1,0,2:T(8,128)S(1)} %pad_maximum_fusion.1), channel_id=1, source_target_pairs={{0,16},{8,24},{16,0},{24,8},{32,48},{40,56},{48,32},{56,40},{64,80... | collective-permute-start | bytes 12582920 | tf_op jit(solution)/shard_map/ppermute | solution.py:11
  224.4 0.7 copy-start.6
  311.9 2.7 copy-start.1
  314.6 92.3 %collective-permute-start.2 = (f32[2,16,8,4096]{3,1,0,2:T(8,128)}, f32[2,16,8,4096]{3,1,0,2:T(8,128)}, u32[]{:S(2)}, u32[]{:S(2)}) collective-permute-start(f32[2,16,8,4096]{3,1,0,2:T(8,128)} %pad_maximum_fusion.3), channel_id=1, source_target_pairs={{0,32},{8,40},{16,48},{24,56},{32,0},{40,8},{48,16},{56,24},{64,96... | collective-permute-start | bytes 12582920 | tf_op jit(solution)/shard_map/ppermute | solution.py:11
  406.9 5.7 %copy-start.2 = (f32[1,16,8,4096]{3,2,1,0:T(8,128)S(1)}, f32[1,16,8,4096]{3,2,1,0:T(8,128)}, u32[]{:S(2)}) copy-start(f32[1,16,8,4096]{3,2,1,0:T(8,128)} %get-tuple-element.5) | copy-start | bytes 6291460
  421.2 92.9 %collective-permute-start.3 = (f32[2,16,8,4096]{3,1,0,2:T(8,128)S(1)}, f32[2,16,8,4096]{3,1,0,2:T(8,128)S(1)}, u32[]{:S(2)}, u32[]{:S(2)}) collective-permute-start(f32[2,16,8,4096]{3,1,0,2:T(8,128)S(1)} %pad_maximum_fusion.4), channel_id=1, source_target_pairs={{0,64},{8,72},{16,80},{24,88},{32,96},{40,104},{48,112},{56,120},{... | collective-permute-start | bytes 12582920 | tf_op jit(solution)/shard_map/ppermute | solution.py:11
where the time goes:
time: 531 us; the launch traced here: 523 us
  waiting for transfers between devices  340 us (64%)
  blocking collectives  54.6 us (10%)
  matrix products  47.5 us (9%)
  other arithmetic  41.3 us (8%)
  local copies, waits for them, and re-layouts  27.3 us (5%)
  starting transfers between devices  11.5 us (2%)
    ppermute x4, waiting for transfers between devices, swapped(): lax.ppermute(array, axis, [(i, i ^ 1 << distance) for i in range(lax.axis...  340 us
    all_to_all x1, blocking collectives, switch_level(): lax.all_to_all(apply_kernel(switch_kernel, blocks), 'freq', split_axis=3,...  54.6 us
    dot_general x8, matrix products, apply_boxes(): jnp.einsum('pts,cspf->ctpf', weight, values, precision=lax.Precision.HIGH...  38.6 us
    sub x4, other arithmetic, rotate(): cosine * values[0] - sine_part * values[1]  35.3 us
    ppermute x4, starting transfers between devices, swapped(): lax.ppermute(array, axis, [(i, i ^ 1 << distance) for i in range(lax.axis...  11.5 us
  transfers between devices with their start and end apart: 4, of which 4 were waited for; matrix products, arithmetic and copies ran while one was open for 4% of the time, Pallas kernels for 0%

commit v1 on v0

v1 whole, which is shorter than its diff:
```python
import functools

import jax
import jax.numpy as jnp
from jax import lax
from jax.experimental import pallas as pl
from jax.experimental.pallas import tpu as pltpu
from jax.sharding import PartitionSpec as P

NCLASS = 4
PTS = 16
BOX = 8
FL = 4096
CH = 2
Q = 4
HIGHEST = lax.Precision.HIGHEST
SIN = (1.0, -0.04166664555668831, 0.0005208156653679907, -3.095163492616848e-06, 1.0176427700514523e-08)
COS = (0.9999999403953552, -0.1249997615814209, 0.002603973727673292, -2.1646354070981033e-05, 9.044205739883182e-08)
VMEM = 56 * 1024 * 1024


def poly(coefs, u):
    r = coefs[-1]
    for c in coefs[-2::-1]:
        r = r * u + c
    return r


def turn(re, im, a):
    u = a * a
    s2 = a * poly(SIN, u)
    sine = s2 * poly(COS, u)
    cosine = 1.0 - 0.5 * (s2 * s2)
    return cosine * re - sine * im, sine * re + cosine * im


def split3(x):
    hi = x.astype(jnp.bfloat16)
    lo = (x - hi.astype(jnp.float32)).astype(jnp.bfloat16)
    return jnp.concatenate([hi, lo, hi], axis=0)


def mm(w, x):
    return jnp.dot(w, split3(x), preferred_element_type=jnp.float32)


def first_kernel(k, zr, s0, s1, s2, s3, a0, a1, a2, a3, o0, o1, o2, o3):
    for s, a, o in ((s0, a0, o0), (s1, a1, o1), (s2, a2, o2), (s3, a3, o3)):
        for j in range(Q):
            rows = pl.ds(Q * k + j, PTS, stride=BOX)
            re, im = turn(s[0, rows, :], s[1, rows, :], a[0, rows, :])
            here = slice(PTS * j, PTS * (j + 1))
            o[0, here, :] = re
            o[1, here, :] = im
            o[2, here, :] = a[1, rows, :]


def first(k, z, source, angles):
    rows = PTS * BOX
    src = [pl.BlockSpec((2, rows, 128), lambda d, zr, e=e: (0, 0, d * Q + (zr[0] ^ e))) for e in range(Q)]
    ang = [pl.BlockSpec((2, rows, 128), lambda d, zr, e=e: (0, 0, d * Q + (zr[0] ^ e))) for e in range(Q)]
    return pl.pallas_call(
        functools.partial(first_kernel, k),
        grid_spec=pltpu.PrefetchScalarGridSpec(
            num_scalar_prefetch=1,
            grid=(8,),
            in_specs=src + ang,
            out_specs=[pl.BlockSpec((3, Q * PTS, 128), lambda d, zr: (0, 0, d))] * Q,
        ),
        out_shape=[jax.ShapeDtypeStruct((3, Q * PTS, 1024), jnp.float32)] * Q,
        compiler_params=pltpu.CompilerParams(vmem_limit_bytes=VMEM),
        cost_estimate=pl.CostEstimate(flops=20_000_000, bytes_accessed=11_000_000, transcendentals=0),
        name="first",
    )(z, *[source] * Q, *[angles] * Q)


def share_kernel(yr, a0, a1, a2, a3, o0, o1, o2, o3):
    for e, o in enumerate((o0, o1, o2, o3)):
        for k in range(CH):
            for l in range(2):
                for i, a in enumerate((a0, a1, a2, a3)):
                    o[k, l, :, 128 * i : 128 * i + 128] = a[l, pl.ds(Q * k + (yr[0] ^ e), PTS, stride=BOX), :]


def share(y, angles):
    return pl.pallas_call(
        share_kernel,
        grid_spec=pltpu.PrefetchScalarGridSpec(
            num_scalar_prefetch=1,
            grid=(8,),
            in_specs=[pl.BlockSpec((2, PTS * BOX, 128), lambda d, yr, i=i: (1, 0, 4 * d + i)) for i in range(4)],
            out_specs=[pl.BlockSpec((CH, 2, PTS, 512), lambda d, yr: (0, 0, 0, d))] * Q,
        ),
        out_shape=[jax.ShapeDtypeStruct((CH, 2, PTS, FL), jnp.float32)] * Q,
        compiler_params=pltpu.CompilerParams(vmem_limit_bytes=VMEM),
        cost_estimate=pl.CostEstimate(flops=1_000_000, bytes_accessed=8_400_000, transcendentals=0),
        name="share",
    )(y, *[angles] * 4)


def early_kernel(zr, r0, r1, r2, r3, w0, w1, o):
    r = (r0, r1, r2, r3)
    z = zr[0]
    x = [[None] * Q for _ in range(Q)]
    for q in range(2):
        for g in range(2):
            part = []
            for c in range(2):
                rows = jnp.concatenate([r[2 * q + i][c, 32 * g : 32 * g + 32, :] for i in range(2)], axis=0)
                part.append(mm(w0[q, g], rows))
            for i in range(2):
                e = 2 * q + i
                here = slice(32 * i, 32 * i + 32)
                re, im = turn(part[0][here], part[1][here], r[e][2, 32 * g : 32 * g + 32, :])
                for n in range(2):
                    x[e][2 * g + n] = (re[PTS * n : PTS * n + PTS], im[PTS * n : PTS * n + PTS])
    for j in range(Q):
        for m in range(2):
            rows = jnp.concatenate([*x[m][j], *x[m + 2][j]], axis=0)
            out = mm(w1[j, m], rows)
            for i in range(2):
                for c in range(2):
                    piece = out[32 * i + PTS * c : 32 * i + PTS * c + PTS]
                    for b in range(2):
                        o[j, z ^ (m + 2 * i), b, c] = piece[:, 128 * b : 128 * b + 128]


def early(z, parts, w0, w1):
    return pl.pallas_call(
        early_kernel,
        grid_spec=pltpu.PrefetchScalarGridSpec(
            num_scalar_prefetch=1,
            grid=(4,),
            in_specs=[pl.BlockSpec((3, Q * PTS, 256), lambda d, zr: (0, 0, d))] * Q
            + [
                pl.BlockSpec((2, 2, 64, 192), lambda d, zr: (0, 0, 0, 0)),
                pl.BlockSpec((Q, 2, 64, 192), lambda d, zr: (0, 0, 0, 0)),
            ],
            out_specs=pl.BlockSpec((Q, Q, 2, 2, PTS, 128), lambda d, zr: (0, 0, d, 0, 0, 0)),
        ),
        out_shape=jax.ShapeDtypeStruct((Q, Q, 8, 2, PTS, 128), jnp.float32),
        compiler_params=pltpu.CompilerParams(vmem_limit_bytes=VMEM),
        cost_estimate=pl.CostEstimate(flops=400_000_000, bytes_accessed=5_000_000, transcendentals=0),
        name="early",
    )(z, *parts, w0, w1)


def late_kernel(yr, x, a0, a1, a2, a3, w2, w3, o0, o1, o2, o3):
    y = yr[0]
    angles = [jnp.concatenate([a[0, l] for a in (a0, a1, a2, a3)], axis=0) for l in range(2)]
    pair = []
    for c in range(2):
        pair.append(
            jnp.concatenate(
                [jnp.concatenate([x[y ^ e, t, 0, c] for t in range(Q)], axis=1) for e in range(Q)], axis=0
            )
        )
    for l, w in enumerate((w2, w3)):
        pair = [mm(w[...], v) for v in turn(*pair, angles[l])]
    for e, o in enumerate((o0, o1, o2, o3)):
        for c in range(2):
            o[c] = pair[c][PTS * e : PTS * e + PTS]


def late(k, y, x, angles, w2, w3):
    return pl.pallas_call(
        late_kernel,
        grid_spec=pltpu.PrefetchScalarGridSpec(
            num_scalar_prefetch=1,
            grid=(8,),
            in_specs=[pl.BlockSpec((Q, Q, 1, 2, PTS, 128), lambda d, yr: (0, 0, d, 0, 0, 0))]
            + [pl.BlockSpec((1, 2, PTS, 512), lambda d, yr: (k, 0, 0, d))] * Q
            + [pl.BlockSpec((64, 192), lambda d, yr: (0, 0))] * 2,
            out_specs=[pl.BlockSpec((2, PTS, 512), lambda d, yr: (0, 0, d))] * Q,
        ),
        out_shape=[jax.ShapeDtypeStruct((2, PTS, FL), jnp.float32)] * Q,
        compiler_params=pltpu.CompilerParams(vmem_limit_bytes=VMEM),
        cost_estimate=pl.CostEstimate(flops=400_000_000, bytes_accessed=5_000_000, transcendentals=0),
        name="late",
    )(y, x, *angles, w2, w3)


def last_kernel(yr, *refs):
    o, room = refs[-2:]
    for c in range(2):
        for i in range(4):
            lanes = slice(128 * i, 128 * i + 128)
            for k in range(CH):
                for e in range(Q):
                    room[c, i, pl.ds(Q * k + (yr[0] ^ e), PTS, stride=BOX), :] = refs[Q * k + e][c, :, lanes]
            o[c, :, lanes] = room[c, i]


def last(y, parts):
    return pl.pallas_call(
        last_kernel,
        grid_spec=pltpu.PrefetchScalarGridSpec(
            num_scalar_prefetch=1,
            grid=(8,),
            in_specs=[pl.BlockSpec((2, PTS, 512), lambda d, yr: (0, 0, d))] * (CH * Q),
            out_specs=pl.BlockSpec((2, PTS * BOX, 512), lambda d, yr: (0, 0, d)),
            scratch_shapes=[pltpu.VMEM((2, 4, PTS * BOX, 128), jnp.float32)],
        ),
        out_shape=jax.ShapeDtypeStruct((2, PTS * BOX, FL), jnp.float32),
        compiler_params=pltpu.CompilerParams(vmem_limit_bytes=VMEM),
        cost_estimate=pl.CostEstimate(flops=1_000_000, bytes_accessed=8_400_000, transcendentals=0),
        name="last",
    )(y, *parts)


def pick(onehot, options):
    shape = onehot.shape + options.shape[1:]
    mask = onehot.reshape(onehot.shape + (1,) * (options.ndim - 1))
    return jnp.sum(jnp.where(mask, jnp.broadcast_to(options, shape), 0.0), axis=onehot.ndim - 1)


def halves(tables, classes, half):
    chosen = pick(classes[..., None] == jnp.arange(NCLASS), tables)
    upper = (half == 1)[:, None, None, None]
    own, other = chosen[:, :, 0, 0], chosen[:, :, 0, 1]
    own = jnp.where(upper, chosen[:, :, 1, 1], own)
    other = jnp.where(upper, chosen[:, :, 1, 0], other)
    return own, other


def two_parts(w):
    hi = lax.reduce_precision(w, 8, 7)
    lo = w - hi
    return jnp.concatenate([hi, hi, lo], axis=-1).astype(jnp.bfloat16)


def weights(cheb_tables, switch_kernel, box_class, y, z):
    near = jnp.arange(Q)
    byplace = box_class.reshape(4, Q, Q, BOX)
    mine_y = lax.dynamic_index_in_dim(byplace, y, 1, False)
    mine_z = lax.dynamic_index_in_dim(byplace, z, 2, False)
    by_z = pick((z ^ near)[:, None] == near, mine_y.transpose(1, 0, 2)).astype(jnp.int32)
    by_y = pick((y ^ near)[:, None] == near, mine_z.transpose(1, 0, 2)).astype(jnp.int32)
    eye = jnp.eye(2, dtype=jnp.float32)
    k0, k1 = switch_kernel[0], switch_kernel[1]
    kc = jnp.stack([jnp.stack([k0, -k1]), jnp.stack([k1, k0])])

    own, other = halves(cheb_tables[0], by_z[:, 0], (z ^ near) & 1)
    own, other = (v.reshape(2, 2, CH, 2, 2, PTS, PTS) for v in (own, other))
    w0 = jnp.einsum("qikgnts,ij,nm->kqgintjms", own, eye, eye, precision=HIGHEST)
    w0 += jnp.einsum("qikgnts,ij,nm->kqgintjms", other, 1 - eye, eye, precision=HIGHEST)
    w0 = w0.reshape(CH, 2, 2, 64, 64)

    own, other = halves(cheb_tables[1], by_z[:, 1], ((z ^ near) >> 1) & 1)
    own, other = (
        jnp.einsum("cdtu,pus->pctds", kc, v.reshape(32, PTS, PTS), precision=HIGHEST).reshape(
            2, 2, CH, Q, 2, PTS, 2, PTS
        )
        for v in (own, other)
    )
    w1 = jnp.einsum("imkjctds,ih->kjmicthds", own, eye, precision=HIGHEST)
    w1 += jnp.einsum("imkjctds,ih->kjmicthds", other, 1 - eye, precision=HIGHEST)
    w1 = w1.reshape(CH, Q, 2, 64, 64)

    late_w = []
    for l in (2, 3):
        own, other = halves(cheb_tables[l], by_y[:, l], ((y ^ near) >> (l - 2)) & 1)
        at = (y == near)[None, None]
        own, other = (
            jnp.sum(jnp.where(at[..., None, None], v.reshape(Q, CH, Q, PTS, PTS), 0.0), axis=2) for v in (own, other)
        )
        same = jnp.eye(Q, dtype=jnp.float32)
        swap = (near[:, None] ^ (l - 1) == near).astype(jnp.float32)
        w = jnp.einsum("ekts,eh->keths", own, same, precision=HIGHEST)
        w += jnp.einsum("ekts,eh->keths", other, swap, precision=HIGHEST)
        late_w.append(two_parts(w.reshape(CH, 64, 64)))
    return two_parts(w0), two_parts(w1), late_w[0], late_w[1]


def exchange(parts, stride):
    count = lax.axis_size("space")
    return [parts[0]] + [
        lax.ppermute(parts[e], "space", [(i, i ^ (stride * e)) for i in range(count)]) for e in range(1, Q)
    ]


def on_device(source, angles, cheb_tables, switch_kernel, box_class):
    place = lax.axis_index("space")
    y, z = place // Q, place % Q
    yr, zr = y.reshape(1).astype(jnp.int32), z.reshape(1).astype(jnp.int32)
    source = source.reshape(2, PTS * BOX, FL)
    angles = angles.reshape(4, PTS * BOX, FL)

    sent_a = first(0, zr, source, angles)
    sent_a, (source, angles) = lax.optimization_barrier((sent_a, (source, angles)))
    here_a = exchange(sent_a, 1)
    late_angles = exchange(share(yr, angles), Q)
    sent_b = first(1, zr, source, angles)
    sent_b, cheb_tables, switch_kernel, box_class = lax.optimization_barrier(
        (sent_b, cheb_tables, switch_kernel, box_class)
    )
    w0, w1, w2, w3 = weights(cheb_tables, switch_kernel, box_class, y, z)
    here_a, sent_b = lax.optimization_barrier((here_a, sent_b))
    here_b = exchange(sent_b, 1)

    result = []
    for k, here in enumerate((here_a, here_b)):
        mixed = early(zr, here, w0[k], w1[k])
        moved = lax.all_to_all(mixed.reshape(128, 2, PTS, 128), ("space", "freq"), 0, 0, tiled=True)
        done = late(k, yr, moved.reshape(Q, Q, 8, 2, PTS, 128), late_angles, w2[k], w3[k])
        result += exchange(done, Q)
    return last(yr, result).reshape(2, PTS, BOX, FL)


def solution(mesh):
    in_specs = (P(None, None, "space", "freq"), P(None, None, "space", "freq"), P(), P(), P())
    out_specs = P(None, None, "space", "freq")
    return jax.shard_map(
        on_device, mesh=mesh, in_specs=in_specs, out_specs=out_specs, check_vma=False
    )
```

time: 531 us -> 221 us (0.42)
  waiting for transfers between devices: 340 us -> 89.5 us
  Pallas kernels: 0 us -> 55.1 us
  blocking collectives: 54.6 us -> 0 us
  matrix products: 47.5 us -> 1.11 us
  starting transfers between devices: 11.5 us -> 40.9 us
  other arithmetic: 41.3 us -> 13 us
  local copies, waits for them, and re-layouts: 27.3 us -> 18.1 us
    ppermute x4 -> x15, waiting for transfers between devices: 340 us -> 78.5 us  [exchange(): lax.ppermute(parts[e], 'space', [(i, i ^ stride * e) for i in range(count)])]
    pallas_call x0 -> x8, Pallas kernels: none -> 55.1 us  [the longest x2 15.4 us: late(): pl.pallas_call(late_kernel, grid_spec=pltpu.PrefetchScalarGridSpec(num_sc...]
    all_to_all x1 -> x0, blocking collectives: 54.6 us -> none  [switch_level(): lax.all_to_all(apply_kernel(switch_kernel, blocks), 'freq', split_axis=3,...]
    dot_general x16 -> x2, matrix products: 47.5 us -> 1.11 us  [weights(): jnp.einsum('cdtu,pus->pctds', kc, v.reshape(32, PTS, PTS), precision=HIGH...]
    sub x4 -> x1, other arithmetic: 35.3 us -> 0.01 us  [weights(): 1 - eye]
    ppermute x4 -> x15, starting transfers between devices: 11.5 us -> 26.3 us  [exchange(): lax.ppermute(parts[e], 'space', [(i, i ^ stride * e) for i in range(count)])]
    all_to_all x0 -> x2, starting transfers between devices: none -> 14.6 us  [on_device(): lax.all_to_all(mixed.reshape(128, 2, PTS, 128), ('space', 'freq'), 0, 0,...]
    all_to_all x0 -> x2, waiting for transfers between devices: none -> 11 us  [on_device(): lax.all_to_all(mixed.reshape(128, 2, PTS, 128), ('space', 'freq'), 0, 0,...]
  transfers between devices with their start and end apart: 4 -> 17, of which waited for: 4 -> 9; matrix products, arithmetic and copies ran while one was open for 4% -> 13% of each run, Pallas kernels for 0% -> 19%
where the time goes in v1:
time: 221 us; the launch traced here: 218 us
  waiting for transfers between devices  89.5 us (40%)
  Pallas kernels  55.1 us (25%)
  starting transfers between devices  40.9 us (19%)
  local copies, waits for them, and re-layouts  18.1 us (8%)
  other arithmetic  13 us (6%)
    ppermute x15, waiting for transfers between devices, exchange(): lax.ppermute(parts[e], 'space', [(i, i ^ stride * e) for i in range(count)])  78.5 us
    ppermute x15, starting transfers between devices, exchange(): lax.ppermute(parts[e], 'space', [(i, i ^ stride * e) for i in range(count)])  26.3 us
    pallas_call x2, Pallas kernels, late(): pl.pallas_call(late_kernel, grid_spec=pltpu.PrefetchScalarGridSpec(num_sc...  15.4 us
    pallas_call x2, Pallas kernels, first(): pl.pallas_call(functools.partial(first_kernel, k), grid_spec=pltpu.Prefet...  14.9 us
    all_to_all x2, starting transfers between devices, on_device(): lax.all_to_all(mixed.reshape(128, 2, PTS, 128), ('space', 'freq'), 0, 0,...  14.6 us
    all_to_all x2, waiting for transfers between devices, on_device(): lax.all_to_all(mixed.reshape(128, 2, PTS, 128), ('space', 'freq'), 0, 0,...  11 us
    pallas_call x2, Pallas kernels, early(): pl.pallas_call(early_kernel, grid_spec=pltpu.PrefetchScalarGridSpec(num_s...  10.8 us
    pallas_call x1, Pallas kernels, last(): pl.pallas_call(last_kernel, grid_spec=pltpu.PrefetchScalarGridSpec(num_sc...  7.06 us
  transfers between devices with their start and end apart: 17, of which 9 were waited for; matrix products, arithmetic and copies ran while one was open for 13% of the time, Pallas kernels for 19%

profile of v1, /device:TPU:0, one launch (start us, length us, event | category | flops | bytes accessed | tf_op | source)
XLA Modules:
  0.0 218.1 jit_solution(13629154943667476266)
XLA Ops:
  0.0 7.4 %first.2 = (f32[3,64,1024]{2,1,0:T(8,128)}, f32[3,64,1024]{2,1,0:T(8,128)}, f32[3,64,1024]{2,1,0:T(8,128)}, f32[3,64,1024]{2,1,0:T(8,128)}) custom-call(s32[1]{0:T(128)} %bitcast.1.zr, f32[2,128,4096]{2,1,0:T(8,128)} %bitcast.116, f32[2,128,4096]{2,1,0:T(8,128)} %bitcast.117, f32[2,128,4096]{2,1,0:T(8,128)} %bitcast.118, f32[2,128,4096]{2,1,0:T(8,128)} %bitcast.119, ...), custom_call_target="tpu_custom_call" | custom-call | flops 20000000 | bytes 11000000 | tf_op jit(solution)/shard_map/first/pallas_call | solution.py:62
  7.4 2.1 collective-permute-start
  9.5 3.6 %collective-permute-start.1 = (f32[3,64,1024]{2,1,0:T(8,128)}, f32[3,64,1024]{2,1,0:T(8,128)}, u32[]{:S(2)}, u32[]{:S(2)}) collective-permute-start(f32[3,64,1024]{2,1,0:T(8,128)} %get-tuple-element.52), channel_id=1, source_target_pairs={{0,16},{8,24},{16,0},{24,8},{32,48},{40,56},{48,32},{56,40},{64,80... | collective-permute-start | bytes 2359304 | tf_op jit(solution)/shard_map/ppermute | solution.py:278
  13.0 7.0 %share.1 = (f32[2,2,16,4096]{3,2,1,0:T(8,128)}, f32[2,2,16,4096]{3,2,1,0:T(8,128)}, f32[2,2,16,4096]{3,2,1,0:T(8,128)}, f32[2,2,16,4096]{3,2,1,0:T(8,128)}) custom-call(s32[1]{0:T(128)} %bitcast.yr, f32[4,128,4096]{2,1,0:T(8,128)} %bitcast.108, f32[4,128,4096]{2,1,0:T(8,128)} %bitcast.109, f32[4,128,4096]{2,1,0:T(8,128)} %bitcast.110, f32[4,128,4096]{2,1,0:T(8,128)} %bitcast.111), custom_call_target="tpu_custom_call" | custom-call | flops 1000000 | bytes 8400000 | tf_op jit(solution)/shard_map/share/pallas_call | solution.py:86
  20.0 1.7 collective-permute-start.3
  21.7 2.9 %collective-permute-start.4 = (f32[2,2,16,4096]{3,2,1,0:T(8,128)}, f32[2,2,16,4096]{3,2,1,0:T(8,128)}, u32[]{:S(2)}, u32[]{:S(2)}) collective-permute-start(f32[2,2,16,4096]{3,2,1,0:T(8,128)} %get-tuple-element.73), channel_id=1, source_target_pairs={{0,64},{8,72},{16,80},{24,88},{32,96},{40,104},{48,112},{56,120},{... | collective-permute-start | bytes 3145736 | tf_op jit(solution)/shard_map/ppermute | solution.py:278
  25.0 7.5 %first.3 = (f32[3,64,1024]{2,1,0:T(8,128)}, f32[3,64,1024]{2,1,0:T(8,128)}, f32[3,64,1024]{2,1,0:T(8,128)}, f32[3,64,1024]{2,1,0:T(8,128)}) custom-call(s32[1]{0:T(128)} %bitcast.1.zr, f32[2,128,4096]{2,1,0:T(8,128)} %bitcast.120, f32[2,128,4096]{2,1,0:T(8,128)} %bitcast.121, f32[2,128,4096]{2,1,0:T(8,128)} %bitcast.122, f32[2,128,4096]{2,1,0:T(8,128)} %bitcast.123, ...), custom_call_target="tpu_custom_call" | custom-call | flops 20000000 | bytes 11000000 | tf_op jit(solution)/shard_map/first/pallas_call | solution.py:62
  33.0 2.2 %select_reduce_fusion.2 = (f32[4,8,2,2,16,16]{5,4,3,2,1,0:T(8,128)S(1)}, f32[4,8,2,2,16,16]{5,4,3,2,1,0:T(8,128)}) fusion(f32[4,2,2,16,16]{4,3,2,1,0:T(8,128)S(1)} %get-tuple-element.113, pred[4,8,4]{2,1,0:T(8,128)(4,1)S(1)} %iota_compare_fusion.2, f32[4,2,2,16,16]{4,3,2,1,0:T(8,128)S(1)} %get-tuple-element.114, pred[4,8,4]{2,1,0:T(8,128)(4,1)S(1)} %iota_compare_fusion.3), kind=kLoop, calls=%fused_computation.2 | loop fusion | flops 458752 | bytes 295168 | tf_op jit(solution)/shard_map/reduce_sum | solution.py:214
  35.5 0.2 copy.40
  35.6 0.2 copy.41
  35.8 0.6 convolution_bitcast_fusion
  36.4 0.6 convolution_bitcast_fusion.1
  37.0 1.0 copy.29
  37.9 1.5 copy.30
  39.5 1.0 copy.32
  40.4 0.6 copy.33
  41.1 3.1 %add_bitcast_fusion = f32[2,4,2,2,2,16,2,2,16]{8,7,6,5,4,3,2,1,0:T(2,128)S(1)} fusion(f32[2,2,2,4,2,16,2,16]{7,6,5,4,0,1,3,2:T(2,128)S(1)} %copy.33, f32[2,2]{1,0:T(2,128)S(1)} %broadcast_subtract_fusion, f32[2,2,2,4,2,16,2,16]{7,6,5,4,0,1,3,2:T(2,128)} %copy.30, f32[2,2]{1,0:T(2,128)S(1)} %compare_convert_fusion), kind=kLoop, calls=%fused_computation.4 | loop fusion | flops 196608 | bytes 524320 | tf_op jit(solution)/shard_map/add | solution.py:257
  44.1 2.4 %reshape.211 = f32[2,4,2,64,64]{4,3,2,1,0:T(8,128)} reshape(f32[2,4,2,2,2,16,2,2,16]{8,7,6,5,4,3,2,1,0:T(2,128)S(1)} %add_bitcast_fusion) | data formatting | bytes 524288 | tf_op jit(solution)/shard_map/reshape | solution.py:258
  46.5 1.2 reduce-precision_convert_fusion
  47.7 1.3 fusion.13
  49.1 0.7 add_bitcast_fusion.1
  49.8 0.8 reshape.208
  51.0 0.3 pad_maximum_fusion
  51.2 0.7 slice_bitcast_fusion.2
  52.0 0.9 slice_bitcast_fusion
  52.8 5.4 %early.2 = f32[4,4,8,2,16,128]{5,4,3,2,1,0:T(8,128)} custom-call(s32[1]{0:T(128)} %bitcast.1.zr, f32[3,64,1024]{2,1,0:T(8,128)} %get-tuple-element.64.r0, f32[3,64,1024]{2,1,0:T(8,128)} %collective-permute-done.r1, f32[3,64,1024]{2,1,0:T(8,128)} %collective-permute-done.1.r2, f32[3,64,1024]{2,1,0:T(8,128)} %collective-permute-done.2.r3, ...), custom_call_target="tpu_custom_call" | custom-call | flops 400000000 | bytes 5000000 | tf_op jit(solution)/shard_map/early/pallas_call | solution.py:129
  58.2 7.7 %all-to-all-start = ((f32[128,2,16,128]{3,2,1,0:T(8,128)}), f32[128,2,16,128]{3,2,1,0:T(8,128)S(1)}, u32[]{:S(2)}, u32[]{:S(2)}) async-start(f32[128,2,16,128]{3,2,1,0:T(8,128)} %bitcast.126), calls=%async_computation | async-start | bytes 4194304 | tf_op jit(solution)/shard_map/all_to_all | solution.py:304
  66.2 1.1 collective-permute-start.9
  67.3 3.2 %collective-permute-start.10 = (f32[3,64,1024]{2,1,0:T(8,128)}, f32[3,64,1024]{2,1,0:T(8,128)S(1)}, u32[]{:S(2)}, u32[]{:S(2)}) collective-permute-start(f32[3,64,1024]{2,1,0:T(8,128)} %get-tuple-element.81), channel_id=1, source_target_pairs={{0,16},{8,24},{16,0},{24,8},{32,48},{40,56},{48,32},{56,40},{64,80... | collective-permute-start | bytes 2359304 | tf_op jit(solution)/shard_map/ppermute | solution.py:278
  70.5 0.4 collective-permute-start.11
  70.9 1.3 select_reduce_fusion
  72.2 1.0 fusion.11
  73.2 1.0 fusion.10
  74.2 33.7 %collective-permute-done.9.r1 = f32[3,64,1024]{2,1,0:T(8,128)S(1)} collective-permute-done((f32[3,64,1024]{2,1,0:T(8,128)}, f32[3,64,1024]{2,1,0:T(8,128)S(1)}, u32[]{:S(2)}, u32[]{:S(2)}) %collective-permute-start.9) | collective-permute-done | bytes 786464 | tf_op jit(solution)/shard_map/ppermute | solution.py:278
  107.9 1.8 collective-permute-start.5
  109.8 16.2 %collective-permute-done.10.r2 = f32[3,64,1024]{2,1,0:T(8,128)S(1)} collective-permute-done((f32[3,64,1024]{2,1,0:T(8,128)}, f32[3,64,1024]{2,1,0:T(8,128)S(1)}, u32[]{:S(2)}, u32[]{:S(2)}) %collective-permute-start.10) | collective-permute-done | bytes 786464 | tf_op jit(solution)/shard_map/ppermute | solution.py:278
  125.9 0.8 collective-permute-done.11.r3
  126.8 0.8 copy-done.4
  127.7 5.4 %early.3 = f32[4,4,8,2,16,128]{5,4,3,2,1,0:T(8,128)} custom-call(s32[1]{0:T(128)} %bitcast.1.zr, f32[3,64,1024]{2,1,0:T(8,128)} %get-tuple-element.79.r0, f32[3,64,1024]{2,1,0:T(8,128)} %copy-done.2, f32[3,64,1024]{2,1,0:T(8,128)} %copy-done.3, f32[3,64,1024]{2,1,0:T(8,128)} %copy-done.4, bf16[2,2,64,192]{3,2,1,0:T(8,128)(2,1)} %get-tuple-element.117.w0, ...), custom_call_target="tpu_custom_call" | custom-call | flops 400000000 | bytes 5000000 | tf_op jit(solution)/shard_map/early/pallas_call | solution.py:129
  133.1 7.0 %all-to-all-start.1 = ((f32[128,2,16,128]{3,2,1,0:T(8,128)}), f32[128,2,16,128]{3,2,1,0:T(8,128)}, u32[]{:S(2)}, u32[]{:S(2)}) async-start(f32[128,2,16,128]{3,2,1,0:T(8,128)} %bitcast.125), calls=%async_computation.1 | async-start | bytes 4194304 | tf_op jit(solution)/shard_map/all_to_all | solution.py:304
  140.0 1.7 select_reduce_fusion.5
  141.8 0.9 add_bitcast_fusion.2
  142.7 1.1 reshape.215
  143.8 0.2 reshape.214
  144.2 0.6 slice_bitcast_fusion.8
  144.9 0.6 slice_bitcast_fusion.9
  145.5 1.0 copy-done.1
  146.6 7.7 %late.2 = (f32[2,16,4096]{2,1,0:T(8,128)}, f32[2,16,4096]{2,1,0:T(8,128)}, f32[2,16,4096]{2,1,0:T(8,128)}, f32[2,16,4096]{2,1,0:T(8,128)}) custom-call(s32[1]{0:T(128)} %bitcast.yr, f32[4,4,8,2,16,128]{5,4,3,2,1,0:T(8,128)} %bitcast.124, f32[2,2,16,4096]{3,2,1,0:T(8,128)} %get-tuple-element.71.a0, f32[2,2,16,4096]{3,2,1,0:T(8,128)} %copy-done.1, ...), custom_call_target="tpu_custom_call" | custom-call | flops 400000000 | bytes 5000000 | tf_op jit(solution)/shard_map/late/pallas_call | solution.py:166
  154.3 1.0 collective-permute-start.6
  155.2 2.7 %collective-permute-start.7 = (f32[2,16,4096]{2,1,0:T(8,128)}, f32[2,16,4096]{2,1,0:T(8,128)S(1)}, u32[]{:S(2)}, u32[]{:S(2)}) collective-permute-start(f32[2,16,4096]{2,1,0:T(8,128)} %get-tuple-element.77), channel_id=1, source_target_pairs={{0,64},{8,72},{16,80},{24,88},{32,96},{40,104},{48,112},{56,120},{... | collective-permute-start | bytes 1572872 | tf_op jit(solution)/shard_map/ppermute | solution.py:278
  158.0 1.1 collective-permute-start.8
  159.0 11.0 %all-to-all-done.1 = f32[128,2,16,128]{3,2,1,0:T(8,128)} async-done(((f32[128,2,16,128]{3,2,1,0:T(8,128)}), f32[128,2,16,128]{3,2,1,0:T(8,128)}, u32[]{:S(2)}, u32[]{:S(2)}) %all-to-all-start.1) | async-done | bytes 2097184 | tf_op jit(solution)/shard_map/all_to_all | solution.py:304
  170.0 7.7 %late.3 = (f32[2,16,4096]{2,1,0:T(8,128)}, f32[2,16,4096]{2,1,0:T(8,128)}, f32[2,16,4096]{2,1,0:T(8,128)}, f32[2,16,4096]{2,1,0:T(8,128)}) custom-call(s32[1]{0:T(128)} %bitcast.yr, f32[4,4,8,2,16,128]{5,4,3,2,1,0:T(8,128)} %bitcast.58.x, f32[2,2,16,4096]{3,2,1,0:T(8,128)} %get-tuple-element.71.a0, f32[2,2,16,4096]{3,2,1,0:T(8,128)} %copy-done.1, ...), custom_call_target="tpu_custom_call" | custom-call | flops 400000000 | bytes 5000000 | tf_op jit(solution)/shard_map/late/pallas_call | solution.py:166
  177.7 0.2 collective-permute-start.12
  177.9 2.2 collective-permute-start.13
  180.1 2.4 %collective-permute-start.14 = (f32[2,16,4096]{2,1,0:T(8,128)}, f32[2,16,4096]{2,1,0:T(8,128)S(1)}, u32[]{:S(2)}, u32[]{:S(2)}) collective-permute-start(f32[2,16,4096]{2,1,0:T(8,128)} %get-tuple-element.86), channel_id=1, source_target_pairs={{0,96},{8,104},{16,112},{24,120},{32,64},{40,72},{48,80},{56,88},{... | collective-permute-start | bytes 1572872 | tf_op jit(solution)/shard_map/ppermute | solution.py:278
  182.5 4.9 %collective-permute-done.7.refs_2_ = f32[2,16,4096]{2,1,0:T(8,128)S(1)} collective-permute-done((f32[2,16,4096]{2,1,0:T(8,128)}, f32[2,16,4096]{2,1,0:T(8,128)S(1)}, u32[]{:S(2)}, u32[]{:S(2)}) %collective-permute-start.7) | collective-permute-done | bytes 524320 | tf_op jit(solution)/shard_map/ppermute | solution.py:278
  187.4 0.6 collective-permute-done.8.refs_3_
  188.0 9.5 %collective-permute-done.12.refs_5_ = f32[2,16,4096]{2,1,0:T(8,128)S(1)} collective-permute-done((f32[2,16,4096]{2,1,0:T(8,128)}, f32[2,16,4096]{2,1,0:T(8,128)S(1)}, u32[]{:S(2)}, u32[]{:S(2)}) %collective-permute-start.12) | collective-permute-done | bytes 524320 | tf_op jit(solution)/shard_map/ppermute | solution.py:278
  197.5 12.4 %collective-permute-done.13.refs_6_ = f32[2,16,4096]{2,1,0:T(8,128)S(1)} collective-permute-done((f32[2,16,4096]{2,1,0:T(8,128)}, f32[2,16,4096]{2,1,0:T(8,128)S(1)}, u32[]{:S(2)}, u32[]{:S(2)}) %collective-permute-start.13) | collective-permute-done | bytes 524320 | tf_op jit(solution)/shard_map/ppermute | solution.py:278
  209.9 0.4 collective-permute-done.14.refs_7_
  210.3 0.4 copy-done.9
  210.7 0.4 copy-done.10
  211.0 7.1 %last.1 = f32[2,128,4096]{2,1,0:T(8,128)} custom-call(s32[1]{0:T(128)} %bitcast.yr, f32[2,16,4096]{2,1,0:T(8,128)} %get-tuple-element.75.refs_0_, f32[2,16,4096]{2,1,0:T(8,128)} %copy-done.5, f32[2,16,4096]{2,1,0:T(8,128)} %copy-done.6, f32[2,16,4096]{2,1,0:T(8,128)} %copy-done.7, f32[2,16,4096]{2,1,0:T(8,128)} %get-tuple-element.83.refs_4_, ...), custom_call_target="tpu_custom_call" | custom-call | flops 1000000 | bytes 8400000 | tf_op jit(solution)/shard_map/last/pallas_call | solution.py:195
  (78 shorter events, 2.1 us)
Async XLA Ops:
  7.4 45.4 %collective-permute-start = (f32[3,64,1024]{2,1,0:T(8,128)}, f32[3,64,1024]{2,1,0:T(8,128)}, u32[]{:S(2)}, u32[]{:S(2)}) collective-permute-start(f32[3,64,1024]{2,1,0:T(8,128)} %get-tuple-element.51), channel_id=1, source_target_pairs={{0,8},{8,0},{16,24},{24,16},{32,40},{40,32},{48,56},{56,48},{64,72... | collective-permute-start | bytes 2359304 | tf_op jit(solution)/shard_map/ppermute | solution.py:278
  9.5 43.4 %collective-permute-start.1 = (f32[3,64,1024]{2,1,0:T(8,128)}, f32[3,64,1024]{2,1,0:T(8,128)}, u32[]{:S(2)}, u32[]{:S(2)}) collective-permute-start(f32[3,64,1024]{2,1,0:T(8,128)} %get-tuple-element.52), channel_id=1, source_target_pairs={{0,16},{8,24},{16,0},{24,8},{32,48},{40,56},{48,32},{56,40},{64,80... | collective-permute-start | bytes 2359304 | tf_op jit(solution)/shard_map/ppermute | solution.py:278
  13.0 39.8 %collective-permute-start.2 = (f32[3,64,1024]{2,1,0:T(8,128)}, f32[3,64,1024]{2,1,0:T(8,128)}, u32[]{:S(2)}, u32[]{:S(2)}) collective-permute-start(f32[3,64,1024]{2,1,0:T(8,128)} %get-tuple-element.53), channel_id=1, source_target_pairs={{0,24},{8,16},{16,8},{24,0},{32,56},{40,48},{48,40},{56,32},{64,88... | collective-permute-start | bytes 2359304 | tf_op jit(solution)/shard_map/ppermute | solution.py:278
  20.0 125.5 %collective-permute-start.3 = (f32[2,2,16,4096]{3,2,1,0:T(8,128)}, f32[2,2,16,4096]{3,2,1,0:T(8,128)S(1)}, u32[]{:S(2)}, u32[]{:S(2)}) collective-permute-start(f32[2,2,16,4096]{3,2,1,0:T(8,128)} %get-tuple-element.72), channel_id=1, source_target_pairs={{0,32},{8,40},{16,48},{24,56},{32,0},{40,8},{48,16},{56,24},{64,96... | collective-permute-start | bytes 3145736 | tf_op jit(solution)/shard_map/ppermute | solution.py:278
  21.7 123.8 %collective-permute-start.4 = (f32[2,2,16,4096]{3,2,1,0:T(8,128)}, f32[2,2,16,4096]{3,2,1,0:T(8,128)}, u32[]{:S(2)}, u32[]{:S(2)}) collective-permute-start(f32[2,2,16,4096]{3,2,1,0:T(8,128)} %get-tuple-element.73), channel_id=1, source_target_pairs={{0,64},{8,72},{16,80},{24,88},{32,96},{40,104},{48,112},{56,120},{... | collective-permute-start | bytes 3145736 | tf_op jit(solution)/shard_map/ppermute | solution.py:278
  25.0 7.5 %copy-start.12 = (f32[2,16,16]{2,1,0:T(8,128)S(1)}, f32[2,16,16]{2,1,0:T(8,128)}, u32[]{:S(2)}) copy-start(f32[2,16,16]{2,1,0:T(8,128)} %param.8) | copy-start | bytes 6148
  25.0 7.5 %copy-start.13 = (s32[4,128]{1,0:T(4,128)S(1)}, s32[4,128]{1,0:T(4,128)}, u32[]{:S(2)}) copy-start(s32[4,128]{1,0:T(4,128)} %param.9) | copy-start | bytes 6148
  25.0 8.0 %copy-start.11 = (f32[4,4,2,2,16,16]{5,4,3,2,1,0:T(8,128)S(1)}, f32[4,4,2,2,16,16]{5,4,3,2,1,0:T(8,128)}, u32[]{:S(2)}) copy-start(f32[4,4,2,2,16,16]{5,4,3,2,1,0:T(8,128)} %param.7) | copy-start | bytes 196612
  58.2 74.9 %all-to-all-start = ((f32[128,2,16,128]{3,2,1,0:T(8,128)}), f32[128,2,16,128]{3,2,1,0:T(8,128)S(1)}, u32[]{:S(2)}, u32[]{:S(2)}) async-start(f32[128,2,16,128]{3,2,1,0:T(8,128)} %bitcast.126), calls=%async_computation | async-start | bytes 4194304 | tf_op jit(solution)/shard_map/all_to_all | solution.py:304
  66.2 41.7 %collective-permute-start.9 = (f32[3,64,1024]{2,1,0:T(8,128)}, f32[3,64,1024]{2,1,0:T(8,128)S(1)}, u32[]{:S(2)}, u32[]{:S(2)}) collective-permute-start(f32[3,64,1024]{2,1,0:T(8,128)} %get-tuple-element.80), channel_id=1, source_target_pairs={{0,8},{8,0},{16,24},{24,16},{32,40},{40,32},{48,56},{56,48},{64,72... | collective-permute-start | bytes 2359304 | tf_op jit(solution)/shard_map/ppermute | solution.py:278
  67.3 58.6 %collective-permute-start.10 = (f32[3,64,1024]{2,1,0:T(8,128)}, f32[3,64,1024]{2,1,0:T(8,128)S(1)}, u32[]{:S(2)}, u32[]{:S(2)}) collective-permute-start(f32[3,64,1024]{2,1,0:T(8,128)} %get-tuple-element.81), channel_id=1, source_target_pairs={{0,16},{8,24},{16,0},{24,8},{32,48},{40,56},{48,32},{56,40},{64,80... | collective-permute-start | bytes 2359304 | tf_op jit(solution)/shard_map/ppermute | solution.py:278
  70.5 56.3 %collective-permute-start.11 = (f32[3,64,1024]{2,1,0:T(8,128)}, f32[3,64,1024]{2,1,0:T(8,128)S(1)}, u32[]{:S(2)}, u32[]{:S(2)}) collective-permute-start(f32[3,64,1024]{2,1,0:T(8,128)} %get-tuple-element.82), channel_id=1, source_target_pairs={{0,24},{8,16},{16,8},{24,0},{32,56},{40,48},{48,40},{56,32},{64,88... | collective-permute-start | bytes 2359304 | tf_op jit(solution)/shard_map/ppermute | solution.py:278
  107.9 18.9 %copy-start.2 = (f32[3,64,1024]{2,1,0:T(8,128)}, f32[3,64,1024]{2,1,0:T(8,128)S(1)}, u32[]{:S(2)}) copy-start(f32[3,64,1024]{2,1,0:T(8,128)S(1)} %collective-permute-done.9.r1) | copy-start | bytes 2359300
  107.9 37.6 %collective-permute-start.5 = (f32[2,2,16,4096]{3,2,1,0:T(8,128)}, f32[2,2,16,4096]{3,2,1,0:T(8,128)}, u32[]{:S(2)}, u32[]{:S(2)}) collective-permute-start(f32[2,2,16,4096]{3,2,1,0:T(8,128)} %get-tuple-element.74), channel_id=1, source_target_pairs={{0,96},{8,104},{16,112},{24,120},{32,64},{40,72},{48,80},{56,88},{... | collective-permute-start | bytes 3145736 | tf_op jit(solution)/shard_map/ppermute | solution.py:278
  125.9 0.9 copy-start.3
  126.8 0.9 copy-start.4
  133.1 11.1 %copy-start = (f32[128,2,16,128]{3,2,1,0:T(8,128)}, f32[128,2,16,128]{3,2,1,0:T(8,128)S(1)}, u32[]{:S(2)}) copy-start(f32[128,2,16,128]{3,2,1,0:T(8,128)S(1)} %all-to-all-done) | copy-start | bytes 6291460
  133.1 36.9 %all-to-all-start.1 = ((f32[128,2,16,128]{3,2,1,0:T(8,128)}), f32[128,2,16,128]{3,2,1,0:T(8,128)}, u32[]{:S(2)}, u32[]{:S(2)}) async-start(f32[128,2,16,128]{3,2,1,0:T(8,128)} %bitcast.125), calls=%async_computation.1 | async-start | bytes 4194304 | tf_op jit(solution)/shard_map/all_to_all | solution.py:304
  145.5 1.0 copy-start.1
  154.3 25.8 %collective-permute-start.6 = (f32[2,16,4096]{2,1,0:T(8,128)}, f32[2,16,4096]{2,1,0:T(8,128)S(1)}, u32[]{:S(2)}, u32[]{:S(2)}) collective-permute-start(f32[2,16,4096]{2,1,0:T(8,128)} %get-tuple-element.76), channel_id=1, source_target_pairs={{0,32},{8,40},{16,48},{24,56},{32,0},{40,8},{48,16},{56,24},{64,96... | collective-permute-start | bytes 1572872 | tf_op jit(solution)/shard_map/ppermute | solution.py:278
  155.2 32.2 %collective-permute-start.7 = (f32[2,16,4096]{2,1,0:T(8,128)}, f32[2,16,4096]{2,1,0:T(8,128)S(1)}, u32[]{:S(2)}, u32[]{:S(2)}) collective-permute-start(f32[2,16,4096]{2,1,0:T(8,128)} %get-tuple-element.77), channel_id=1, source_target_pairs={{0,64},{8,72},{16,80},{24,88},{32,96},{40,104},{48,112},{56,120},{... | collective-permute-start | bytes 1572872 | tf_op jit(solution)/shard_map/ppermute | solution.py:278
  158.0 30.0 %collective-permute-start.8 = (f32[2,16,4096]{2,1,0:T(8,128)}, f32[2,16,4096]{2,1,0:T(8,128)S(1)}, u32[]{:S(2)}, u32[]{:S(2)}) collective-permute-start(f32[2,16,4096]{2,1,0:T(8,128)} %get-tuple-element.78), channel_id=1, source_target_pairs={{0,96},{8,104},{16,112},{24,120},{32,64},{40,72},{48,80},{56,88},{... | collective-permute-start | bytes 1572872 | tf_op jit(solution)/shard_map/ppermute | solution.py:278
  177.7 19.8 %collective-permute-start.12 = (f32[2,16,4096]{2,1,0:T(8,128)}, f32[2,16,4096]{2,1,0:T(8,128)S(1)}, u32[]{:S(2)}, u32[]{:S(2)}) collective-permute-start(f32[2,16,4096]{2,1,0:T(8,128)} %get-tuple-element.84), channel_id=1, source_target_pairs={{0,32},{8,40},{16,48},{24,56},{32,0},{40,8},{48,16},{56,24},{64,96... | collective-permute-start | bytes 1572872 | tf_op jit(solution)/shard_map/ppermute | solution.py:278
  177.9 32.0 %collective-permute-start.13 = (f32[2,16,4096]{2,1,0:T(8,128)}, f32[2,16,4096]{2,1,0:T(8,128)S(1)}, u32[]{:S(2)}, u32[]{:S(2)}) collective-permute-start(f32[2,16,4096]{2,1,0:T(8,128)} %get-tuple-element.85), channel_id=1, source_target_pairs={{0,64},{8,72},{16,80},{24,88},{32,96},{40,104},{48,112},{56,120},{... | collective-permute-start | bytes 1572872 | tf_op jit(solution)/shard_map/ppermute | solution.py:278
  180.1 30.2 %copy-start.5 = (f32[2,16,4096]{2,1,0:T(8,128)}, f32[2,16,4096]{2,1,0:T(8,128)S(1)}, u32[]{:S(2)}) copy-start(f32[2,16,4096]{2,1,0:T(8,128)S(1)} %collective-permute-done.6.refs_1_) | copy-start | bytes 1572868
  180.1 30.2 %collective-permute-start.14 = (f32[2,16,4096]{2,1,0:T(8,128)}, f32[2,16,4096]{2,1,0:T(8,128)S(1)}, u32[]{:S(2)}, u32[]{:S(2)}) collective-permute-start(f32[2,16,4096]{2,1,0:T(8,128)} %get-tuple-element.86), channel_id=1, source_target_pairs={{0,96},{8,104},{16,112},{24,120},{32,64},{40,72},{48,80},{56,88},{... | collective-permute-start | bytes 1572872 | tf_op jit(solution)/shard_map/ppermute | solution.py:278
  187.4 22.9 %copy-start.6 = (f32[2,16,4096]{2,1,0:T(8,128)}, f32[2,16,4096]{2,1,0:T(8,128)S(1)}, u32[]{:S(2)}) copy-start(f32[2,16,4096]{2,1,0:T(8,128)S(1)} %collective-permute-done.7.refs_2_) | copy-start | bytes 1572868
  187.9 22.3 %copy-start.7 = (f32[2,16,4096]{2,1,0:T(8,128)}, f32[2,16,4096]{2,1,0:T(8,128)S(1)}, u32[]{:S(2)}) copy-start(f32[2,16,4096]{2,1,0:T(8,128)S(1)} %collective-permute-done.8.refs_3_) | copy-start | bytes 1572868
  197.5 12.8 %copy-start.8 = (f32[2,16,4096]{2,1,0:T(8,128)}, f32[2,16,4096]{2,1,0:T(8,128)S(1)}, u32[]{:S(2)}) copy-start(f32[2,16,4096]{2,1,0:T(8,128)S(1)} %collective-permute-done.12.refs_5_) | copy-start | bytes 1572868
  209.9 0.8 copy-start.9
  210.3 0.8 copy-start.10

commit v2 on v1

v2 whole, which is shorter than its diff:
```python
import functools

import jax
import jax.numpy as jnp
from jax import lax
from jax.experimental import pallas as pl
from jax.experimental.pallas import tpu as pltpu
from jax.sharding import PartitionSpec as P

NCLASS = 4
PTS = 16
BOX = 8
FL = 4096
CH = 2
Q = 4
HIGHEST = lax.Precision.HIGHEST
SIN = (1.0, -0.04166664555668831, 0.0005208156653679907, -3.095163492616848e-06, 1.0176427700514523e-08)
COS = (0.9999999403953552, -0.1249997615814209, 0.002603973727673292, -2.1646354070981033e-05, 9.044205739883182e-08)
VMEM = 56 * 1024 * 1024
COST = pl.CostEstimate(flops=1000, bytes_accessed=1000, transcendentals=0)


def poly(coefs, u):
    r = coefs[-1]
    for c in coefs[-2::-1]:
        r = r * u + c
    return r


def turn(re, im, a):
    u = a * a
    s2 = a * poly(SIN, u)
    sine = s2 * poly(COS, u)
    cosine = 1.0 - 0.5 * (s2 * s2)
    return cosine * re - sine * im, sine * re + cosine * im


def split3(x):
    hi = x.astype(jnp.bfloat16)
    lo = (x - hi.astype(jnp.float32)).astype(jnp.bfloat16)
    return jnp.concatenate([hi, lo, hi], axis=0)


def mm(w, x):
    return jnp.dot(w, split3(x), preferred_element_type=jnp.float32)


def by_box(v):
    return jnp.swapaxes(v.reshape(PTS, BOX, v.shape[-1]), 0, 1)


def first_kernel(n, zr, *refs):
    src, ang, outs, room = refs[:n], refs[n : 2 * n], refs[2 * n : 2 * n + Q], refs[-1]
    for d in range(n):
        re, im = turn(src[d][0], src[d][1], ang[d][0])
        for c, v in enumerate((re, im, ang[d][1])):
            room[c] = by_box(v)
        for e, o in enumerate(outs):
            for c in range(3):
                for i in range(2):
                    o[c, PTS * i : PTS * i + PTS, 256 * d : 256 * d + 256] = room[c, 2 * (zr[0] ^ e) + i]


def first(k, z, source, angles, n=2):
    def spec(d):
        return pl.BlockSpec((2, PTS * BOX, 256), lambda g, zr: (0, 0, 2 * (n * g + d) + k))

    return pl.pallas_call(
        functools.partial(first_kernel, n),
        grid_spec=pltpu.PrefetchScalarGridSpec(
            num_scalar_prefetch=1,
            grid=(8 // n,),
            in_specs=[spec(d) for d in range(n)] * 2,
            out_specs=[pl.BlockSpec((3, 2 * PTS, 256 * n), lambda g, zr: (0, 0, g))] * Q,
            scratch_shapes=[pltpu.VMEM((3, BOX, PTS, 256), jnp.float32)],
        ),
        out_shape=[jax.ShapeDtypeStruct((3, 2 * PTS, 2048), jnp.float32)] * Q,
        compiler_params=pltpu.CompilerParams(vmem_limit_bytes=VMEM),
        cost_estimate=COST,
        name="first",
    )(z, *[source] * n, *[angles] * n)


def share_kernel(yr, a, o0, o1, o2, o3, room):
    for l in range(2):
        for d in range(4):
            for t in range(Q):
                here = slice(512 * d + 128 * t, 512 * d + 128 * t + 128)
                v = by_box(a[l, :, here]).reshape(Q, 2, PTS, 128)
                for n in range(2):
                    room[t // 2, 2 * (t % 2) + n] = v[:, n].reshape(Q * PTS, 128)
            for e, o in enumerate((o0, o1, o2, o3)):
                for k in range(CH):
                    o[k, l, :, 128 * d : 128 * d + 128] = room[k, yr[0] ^ e]


def share(y, angles):
    return pl.pallas_call(
        share_kernel,
        grid_spec=pltpu.PrefetchScalarGridSpec(
            num_scalar_prefetch=1,
            grid=(2,),
            in_specs=[pl.BlockSpec((2, PTS * BOX, 2048), lambda d, yr: (1, 0, d))],
            out_specs=[pl.BlockSpec((CH, 2, Q * PTS, 512), lambda d, yr: (0, 0, 0, d))] * Q,
            scratch_shapes=[pltpu.VMEM((CH, Q, Q * PTS, 128), jnp.float32)],
        ),
        out_shape=[jax.ShapeDtypeStruct((CH, 2, Q * PTS, 1024), jnp.float32)] * Q,
        compiler_params=pltpu.CompilerParams(vmem_limit_bytes=VMEM),
        cost_estimate=COST,
        name="share",
    )(y, angles)


def early_kernel(zr, r0, r1, r2, r3, w0, w1, o):
    r = (r0, r1, r2, r3)
    x = []
    for q in range(2):
        part = []
        for c in range(2):
            rows = jnp.concatenate([r[2 * q + i][c] for i in range(2)], axis=0)
            part.append(mm(w0[0, q], rows))
        angle = jnp.concatenate([r[2 * q + i][2] for i in range(2)], axis=0)
        x.append(turn(*part, angle))
    for n in range(2):
        for m in range(2):
            here = slice(32 * m + PTS * n, 32 * m + PTS * n + PTS)
            rows = jnp.concatenate([x[i][c][here] for i in range(2) for c in range(2)], axis=0)
            out = mm(w1[0, n, m], rows)
            for i in range(2):
                for c in range(2):
                    piece = out[32 * i + PTS * c : 32 * i + PTS * c + PTS]
                    for t in range(piece.shape[1] // 128):
                        o[2 * (t % 2) + n, zr[0] ^ (m + 2 * i), t // 2, c] = piece[:, 128 * t : 128 * t + 128]


def early(k, z, parts, w0, w1, steps=4):
    lanes, n = 2048 // steps, 8 // steps
    return pl.pallas_call(
        early_kernel,
        grid_spec=pltpu.PrefetchScalarGridSpec(
            num_scalar_prefetch=1,
            grid=(steps,),
            in_specs=[pl.BlockSpec((3, 2 * PTS, lanes), lambda d, zr: (0, 0, d))] * Q
            + [
                pl.BlockSpec((1, 2, 64, 192), lambda d, zr: (0, 0, 0, 0)),
                pl.BlockSpec((1, 2, 2, 64, 192), lambda d, zr: (0, 0, 0, 0, 0)),
            ],
            out_specs=pl.BlockSpec((Q, Q, n, 2, PTS, 128), lambda d, zr: (0, 0, d, 0, 0, 0)),
        ),
        out_shape=jax.ShapeDtypeStruct((Q, Q, 8, 2, PTS, 128), jnp.float32),
        compiler_params=pltpu.CompilerParams(vmem_limit_bytes=VMEM),
        cost_estimate=COST,
        name="early",
    )(z, *parts, w0, w1)


def late_kernel(yr, x, a0, a1, a2, a3, w2, w3, o0, o1, o2, o3):
    y = yr[0]
    count = x.shape[2]
    for t in range(Q):
        here = slice(PTS * t, PTS * t + PTS)
        angles = [jnp.concatenate([a[0, l, here] for a in (a0, a1, a2, a3)], axis=0) for l in range(2)]
        pair = []
        for c in range(2):
            pair.append(
                jnp.concatenate(
                    [jnp.concatenate([x[y ^ e, t, d, c] for d in range(count)], axis=1) for e in range(Q)], axis=0
                )
            )
        for l, w in enumerate((w2, w3)):
            pair = [mm(w[t], v) for v in turn(*pair, angles[l])]
        for e, o in enumerate((o0, o1, o2, o3)):
            for c in range(2):
                o[c, here] = pair[c][PTS * e : PTS * e + PTS]


def late(k, y, x, angles, w2, w3, steps=4):
    n = 8 // steps
    return pl.pallas_call(
        late_kernel,
        grid_spec=pltpu.PrefetchScalarGridSpec(
            num_scalar_prefetch=1,
            grid=(steps,),
            in_specs=[pl.BlockSpec((Q, Q, n, 2, PTS, 128), lambda d, yr: (0, 0, d, 0, 0, 0))]
            + [pl.BlockSpec((1, 2, Q * PTS, 128 * n), lambda d, yr: (k, 0, 0, d))] * Q
            + [pl.BlockSpec((Q, 64, 192), lambda d, yr: (0, 0, 0))] * 2,
            out_specs=[pl.BlockSpec((2, Q * PTS, 128 * n), lambda d, yr: (0, 0, d))] * Q,
        ),
        out_shape=[jax.ShapeDtypeStruct((2, Q * PTS, 1024), jnp.float32)] * Q,
        compiler_params=pltpu.CompilerParams(vmem_limit_bytes=VMEM),
        cost_estimate=COST,
        name="late",
    )(y, x, *angles, w2, w3)


def last_kernel(k, yr, *refs):
    ins, (o, room, ready, sems) = refs[:Q], refs[-4:]
    copies = []
    for d in range(8):
        here = slice(128 * d, 128 * d + 128)
        for c in range(2):
            for e in range(Q):
                at = yr[0] ^ e
                for t in range(Q):
                    room[at // 2, c, 2 * t + at % 2] = ins[e][c, PTS * t : PTS * t + PTS, here]
        for c in range(2):
            for b in range(2):
                v = jnp.swapaxes(room[b, c], 0, 1).reshape(PTS * BOX, 128)
                ready[c, :, 256 * d + 128 * b : 256 * d + 128 * b + 128] = v
        copies.append(
            pltpu.make_async_copy(
                ready.at[:, :, pl.ds(256 * d, 256)], o.at[:, :, pl.ds(512 * d + 256 * k, 256)], sems.at[d]
            )
        )
        copies[-1].start()
    for copy in copies:
        copy.wait()


def last(k, y, parts, before):
    extra = [] if before is None else [before]
    return pl.pallas_call(
        functools.partial(last_kernel, k),
        grid_spec=pltpu.PrefetchScalarGridSpec(
            num_scalar_prefetch=1,
            grid=(1,),
            in_specs=[pl.BlockSpec((2, Q * PTS, 1024), lambda d, yr: (0, 0, 0))] * Q
            + [pl.BlockSpec(memory_space=pl.ANY)] * len(extra),
            out_specs=pl.BlockSpec(memory_space=pl.ANY),
            scratch_shapes=[
                pltpu.VMEM((2, 2, BOX, PTS, 128), jnp.float32),
                pltpu.VMEM((2, PTS * BOX, 2048), jnp.float32),
                pltpu.SemaphoreType.DMA((8,)),
            ],
        ),
        out_shape=jax.ShapeDtypeStruct((2, PTS * BOX, FL), jnp.float32),
        input_output_aliases={Q + 1: 0} if extra else {},
        compiler_params=pltpu.CompilerParams(vmem_limit_bytes=VMEM),
        cost_estimate=COST,
        name="last",
    )(y, *parts, *extra)


def pick(onehot, options):
    shape = onehot.shape + options.shape[1:]
    mask = onehot.reshape(onehot.shape + (1,) * (options.ndim - 1))
    return jnp.sum(jnp.where(mask, jnp.broadcast_to(options, shape), 0.0), axis=onehot.ndim - 1)


def halves(tables, classes, half):
    chosen = pick(classes[..., None] == jnp.arange(NCLASS), tables)
    upper = (half == 1)[:, None, None, None]
    own, other = chosen[:, :, 0, 0], chosen[:, :, 0, 1]
    own = jnp.where(upper, chosen[:, :, 1, 1], own)
    other = jnp.where(upper, chosen[:, :, 1, 0], other)
    return own, other


def two_parts(w):
    hi = lax.reduce_precision(w, 8, 7)
    lo = w - hi
    return jnp.concatenate([hi, hi, lo], axis=-1).astype(jnp.bfloat16)


def weights(cheb_tables, switch_kernel, box_class, y, z):
    near = jnp.arange(Q)
    byplace = box_class.reshape(4, Q, Q, BOX)
    mine_y = lax.dynamic_index_in_dim(byplace, y, 1, False)
    mine_z = lax.dynamic_index_in_dim(byplace, z, 2, False)
    mine_y = lax.dynamic_slice_in_dim(mine_y, 2 * z, 2, 2)
    mine_z = lax.dynamic_index_in_dim(mine_z.reshape(4, Q, Q, 2), y % 2, 3, False)
    by_z = pick((z ^ near)[:, None] == near, mine_y.transpose(1, 0, 2)).astype(jnp.int32)
    by_y = pick((y ^ near)[:, None] == near, mine_z.transpose(1, 0, 2)).astype(jnp.int32)
    eye = jnp.eye(2, dtype=jnp.float32)
    k0, k1 = switch_kernel[0], switch_kernel[1]
    kc = jnp.stack([jnp.stack([k0, -k1]), jnp.stack([k1, k0])])

    own, other = halves(cheb_tables[0], by_z[:, 0], (z ^ near) & 1)
    own, other = (v.reshape(2, 2, 2, PTS, PTS) for v in (own, other))
    w0 = jnp.einsum("qints,ij,nm->qintjms", own, eye, eye, precision=HIGHEST)
    w0 += jnp.einsum("qints,ij,nm->qintjms", other, 1 - eye, eye, precision=HIGHEST)
    w0 = w0.reshape(1, 2, 64, 64)

    own, other = halves(cheb_tables[1], by_z[:, 1], ((z ^ near) >> 1) & 1)
    own, other = (
        jnp.einsum("cdtu,pus->pctds", kc, v.reshape(8, PTS, PTS), precision=HIGHEST).reshape(2, 2, 2, 2, PTS, 2, PTS)
        for v in (own, other)
    )
    w1 = jnp.einsum("imnctds,ih->nmicthds", own, eye, precision=HIGHEST)
    w1 += jnp.einsum("imnctds,ih->nmicthds", other, 1 - eye, precision=HIGHEST)
    w1 = w1.reshape(1, 2, 2, 64, 64)

    late_w = []
    for l in (2, 3):
        own, other = halves(cheb_tables[l], by_y[:, l], ((y ^ near) >> (l - 2)) & 1)
        same = jnp.eye(Q, dtype=jnp.float32)
        swap = (near[:, None] ^ (l - 1) == near).astype(jnp.float32)
        w = jnp.einsum("ekts,eh->keths", own, same, precision=HIGHEST)
        w += jnp.einsum("ekts,eh->keths", other, swap, precision=HIGHEST)
        late_w.append(two_parts(w.reshape(Q, 64, 64)))
    return two_parts(w0), two_parts(w1), late_w[0], late_w[1]


def exchange(parts, stride):
    count = lax.axis_size("space")
    return [parts[0]] + [
        lax.ppermute(parts[e], "space", [(i, i ^ (stride * e)) for i in range(count)]) for e in range(1, Q)
    ]


def on_device(source, angles, cheb_tables, switch_kernel, box_class):
    place = lax.axis_index("space")
    y, z = place // Q, place % Q
    yr, zr = y.reshape(1).astype(jnp.int32), z.reshape(1).astype(jnp.int32)
    source = source.reshape(2, PTS * BOX, FL)
    angles = angles.reshape(4, PTS * BOX, FL)

    sent_a = first(0, zr, source, angles)
    sent_a, source, angles = lax.optimization_barrier((sent_a, source, angles))
    here_a = exchange(sent_a, 1)
    late_angles = exchange(share(yr, angles), Q)
    sent_b = first(1, zr, source, angles)
    sent_b, cheb_tables, switch_kernel, box_class = lax.optimization_barrier(
        (sent_b, cheb_tables, switch_kernel, box_class)
    )
    w0, w1, w2, w3 = weights(cheb_tables, switch_kernel, box_class, y, z)
    here_a, sent_b = lax.optimization_barrier((here_a, sent_b))
    here_b = exchange(sent_b, 1)

    result = None
    for k, here in enumerate((here_a, here_b)):
        if k == 1:
            here, done = lax.optimization_barrier((here, done))
        mixed = early(k, zr, here, w0, w1)
        moved = lax.all_to_all(mixed.reshape(128, 2, PTS, 128), ("space", "freq"), 0, 0, tiled=True)
        done = late(k, yr, moved.reshape(Q, Q, 8, 2, PTS, 128), late_angles, w2, w3)
        result = last(k, yr, exchange(done, Q), result)
    return result.reshape(2, PTS, BOX, FL)


def solution(mesh):
    in_specs = (P(None, None, "space", "freq"), P(None, None, "space", "freq"), P(), P(), P())
    out_specs = P(None, None, "space", "freq")
    return jax.shard_map(
        on_device, mesh=mesh, in_specs=in_specs, out_specs=out_specs, check_vma=False
    )
```

time: 221 us -> 210 us (0.950)
  waiting for transfers between devices: 89.5 us -> 104 us
  Pallas kernels: 55.1 us -> 45.2 us
  local copies, waits for them, and re-layouts: 18.1 us -> 9.71 us
  starting transfers between devices: 40.9 us -> 37.9 us
  other arithmetic: 13 us -> 10.4 us
    all_to_all x2, waiting for transfers between devices: 11 us -> 28.7 us  [on_device(): lax.all_to_all(mixed.reshape(128, 2, PTS, 128), ('space', 'freq'), 0, 0,...]
    pallas_call x3 -> x4, Pallas kernels: 21.9 us -> 16.9 us  [the longest x2 10.7 us: first(): pl.pallas_call(functools.partial(first_kernel, n), grid_spec=pltpu.Prefet...]
    ppermute x15, waiting for transfers between devices: 78.5 us -> 75.1 us  [exchange(): lax.ppermute(parts[e], 'space', [(i, i ^ stride * e) for i in range(count)])]
    slice x3 -> x2, local copies, waits for them, and re-layouts: 3.26 us -> 0.04 us  [halves(): own, other = (chosen[:, :, 0, 0], chosen[:, :, 0, 1])]
    add x2, other arithmetic: 3.74 us -> 0.57 us  [the longest x1 0.37 us: weights(): w1 += jnp.einsum('imnctds,ih->nmicthds', other, 1 - eye, precision=HIGHEST)]
    reshape x6, local copies, waits for them, and re-layouts: 6.58 us -> 3.56 us  [the longest x2 2.59 us: weights(): late_w.append(two_parts(w.reshape(Q, 64, 64)))]
    pallas_call x1, Pallas kernels: 6.99 us -> 4.15 us  [share(): pl.pallas_call(share_kernel, grid_spec=pltpu.PrefetchScalarGridSpec(num_s...]
    squeeze x4, local copies, waits for them, and re-layouts: 2.85 us -> 0.32 us  [the longest x2 0.16 us: halves(): own, other = (chosen[:, :, 0, 0], chosen[:, :, 0, 1])]
  transfers between devices with their start and end apart: 17 -> 17, of which waited for: 9 -> 10; matrix products, arithmetic and copies ran while one was open for 13% -> 8% of each run, Pallas kernels for 19% -> 15%
where the time goes in v2:
time: 210 us; the launch traced here: 209 us
  waiting for transfers between devices  104 us (50%)
  Pallas kernels  45.2 us (22%)
  starting transfers between devices  37.9 us (18%)
  other arithmetic  10.4 us (5%)
  local copies, waits for them, and re-layouts  9.71 us (5%)
    ppermute x15, waiting for transfers between devices, exchange(): lax.ppermute(parts[e], 'space', [(i, i ^ stride * e) for i in range(count)])  75.1 us
    all_to_all x2, waiting for transfers between devices, on_device(): lax.all_to_all(mixed.reshape(128, 2, PTS, 128), ('space', 'freq'), 0, 0,...  28.7 us
    ppermute x15, starting transfers between devices, exchange(): lax.ppermute(parts[e], 'space', [(i, i ^ stride * e) for i in range(count)])  24.5 us
    all_to_all x2, starting transfers between devices, on_device(): lax.all_to_all(mixed.reshape(128, 2, PTS, 128), ('space', 'freq'), 0, 0,...  13.4 us
    pallas_call x2, Pallas kernels, late(): pl.pallas_call(late_kernel, grid_spec=pltpu.PrefetchScalarGridSpec(num_sc...  13.2 us
    pallas_call x2, Pallas kernels, early(): pl.pallas_call(early_kernel, grid_spec=pltpu.PrefetchScalarGridSpec(num_s...  11.1 us
    pallas_call x2, Pallas kernels, first(): pl.pallas_call(functools.partial(first_kernel, n), grid_spec=pltpu.Prefet...  10.7 us
    pallas_call x2, Pallas kernels, last(): pl.pallas_call(functools.partial(last_kernel, k), grid_spec=pltpu.Prefetc...  6.17 us
  transfers between devices with their start and end apart: 17, of which 10 were waited for; matrix products, arithmetic and copies ran while one was open for 8% of the time, Pallas kernels for 15%

profile of v2, /device:TPU:0, one launch (start us, length us, event | category | flops | bytes accessed | tf_op | source)
XLA Modules:
  0.0 208.5 jit_solution(4834899651903241106)
XLA Ops:
  0.0 5.2 %first.2 = (f32[3,32,2048]{2,1,0:T(8,128)}, f32[3,32,2048]{2,1,0:T(8,128)}, f32[3,32,2048]{2,1,0:T(8,128)}, f32[3,32,2048]{2,1,0:T(8,128)}) custom-call(s32[1]{0:T(128)} %bitcast.1.zr, f32[2,128,4096]{2,1,0:T(8,128)} %bitcast.135, f32[2,128,4096]{2,1,0:T(8,128)} %bitcast.136, f32[4,128,4096]{2,1,0:T(8,128)} %bitcast.130, f32[4,128,4096]{2,1,0:T(8,128)} %bitcast.131), custom_call_target="tpu_custom_call" | custom-call | flops 1000 | bytes 1000 | tf_op jit(solution)/shard_map/first/pallas_call | solution.py:68
  5.2 2.0 collective-permute-start
  7.3 3.6 %collective-permute-start.1 = (f32[3,32,2048]{2,1,0:T(8,128)}, f32[3,32,2048]{2,1,0:T(8,128)}, u32[]{:S(2)}, u32[]{:S(2)}) collective-permute-start(f32[3,32,2048]{2,1,0:T(8,128)} %get-tuple-element.56), channel_id=1, source_target_pairs={{0,16},{8,24},{16,0},{24,8},{32,48},{40,56},{48,32},{56,40},{64,80... | collective-permute-start | bytes 2359304 | tf_op jit(solution)/shard_map/ppermute | solution.py:307
  10.9 4.1 %share.1 = (f32[2,2,64,1024]{3,2,1,0:T(8,128)}, f32[2,2,64,1024]{3,2,1,0:T(8,128)}, f32[2,2,64,1024]{3,2,1,0:T(8,128)}, f32[2,2,64,1024]{3,2,1,0:T(8,128)}) custom-call(s32[1]{0:T(128)} %bitcast.yr, f32[4,128,4096]{2,1,0:T(8,128)} %bitcast.132), custom_call_target="tpu_custom_call" | custom-call | flops 1000 | bytes 1000 | tf_op jit(solution)/shard_map/share/pallas_call | solution.py:98
  15.0 1.6 collective-permute-start.6
  16.6 2.9 %collective-permute-start.7 = (f32[2,2,64,1024]{3,2,1,0:T(8,128)}, f32[2,2,64,1024]{3,2,1,0:T(8,128)}, u32[]{:S(2)}, u32[]{:S(2)}) collective-permute-start(f32[2,2,64,1024]{3,2,1,0:T(8,128)} %get-tuple-element.81), channel_id=1, source_target_pairs={{0,64},{8,72},{16,80},{24,88},{32,96},{40,104},{48,112},{56,120},{... | collective-permute-start | bytes 3145736 | tf_op jit(solution)/shard_map/ppermute | solution.py:307
  19.9 5.4 %first.3 = (f32[3,32,2048]{2,1,0:T(8,128)}, f32[3,32,2048]{2,1,0:T(8,128)}, f32[3,32,2048]{2,1,0:T(8,128)}, f32[3,32,2048]{2,1,0:T(8,128)}) custom-call(s32[1]{0:T(128)} %bitcast.1.zr, f32[2,128,4096]{2,1,0:T(8,128)} %bitcast.137, f32[2,128,4096]{2,1,0:T(8,128)} %bitcast.138, f32[4,128,4096]{2,1,0:T(8,128)} %bitcast.133, f32[4,128,4096]{2,1,0:T(8,128)} %bitcast.134), custom_call_target="tpu_custom_call" | custom-call | flops 1000 | bytes 1000 | tf_op jit(solution)/shard_map/first/pallas_call | solution.py:68
  25.3 0.1 reshape.290
  25.6 0.1 copy.76
  25.7 0.1 copy.50
  26.0 0.1 copy.53
  26.6 0.1 copy.77
  26.9 0.3 select_reduce_fusion.2
  27.7 0.4 fusion.12
  28.1 0.2 copy.57
  28.3 0.4 fusion.10
  28.7 0.2 copy.60
  28.9 0.4 add_bitcast_fusion.2
  29.3 0.4 reshape.294
  29.9 0.2 add_bitcast_fusion.3
  30.1 0.2 reshape.291
  30.3 0.7 pad_maximum_fusion.3.w0
  31.1 0.8 pad_maximum_fusion.w1
  32.0 1.6 select_reduce_fusion
  33.6 0.2 collective-permute-start.8
  33.8 11.6 %collective-permute-done.1.r2 = f32[3,32,2048]{2,1,0:T(8,128)} collective-permute-done((f32[3,32,2048]{2,1,0:T(8,128)}, f32[3,32,2048]{2,1,0:T(8,128)}, u32[]{:S(2)}, u32[]{:S(2)}) %collective-permute-start.1) | collective-permute-done | bytes 786464 | tf_op jit(solution)/shard_map/ppermute | solution.py:307
  45.4 2.6 %collective-permute-done.2.r3 = f32[3,32,2048]{2,1,0:T(8,128)} collective-permute-done((f32[3,32,2048]{2,1,0:T(8,128)}, f32[3,32,2048]{2,1,0:T(8,128)}, u32[]{:S(2)}, u32[]{:S(2)}) %collective-permute-start.2) | collective-permute-done | bytes 786464 | tf_op jit(solution)/shard_map/ppermute | solution.py:307
  48.0 5.5 %early.2 = f32[4,4,8,2,16,128]{5,4,3,2,1,0:T(8,128)} custom-call(s32[1]{0:T(128)} %bitcast.1.zr, f32[3,32,2048]{2,1,0:T(8,128)} %get-tuple-element.72.r0, f32[3,32,2048]{2,1,0:T(8,128)} %copy-done.3, f32[3,32,2048]{2,1,0:T(8,128)} %collective-permute-done.1.r2, f32[3,32,2048]{2,1,0:T(8,128)} %collective-permute-done.2.r3, ...), custom_call_target="tpu_custom_call" | custom-call | flops 1000 | bytes 1000 | tf_op jit(solution)/shard_map/early/pallas_call | solution.py:138
  53.5 7.6 %all-to-all-start = ((f32[128,2,16,128]{3,2,1,0:T(8,128)}), f32[128,2,16,128]{3,2,1,0:T(8,128)S(1)}, u32[]{:S(2)}, u32[]{:S(2)}) async-start(f32[128,2,16,128]{3,2,1,0:T(8,128)} %bitcast.140), calls=%async_computation | async-start | bytes 4194304 | tf_op jit(solution)/shard_map/all_to_all | solution.py:335
  61.2 1.2 fusion.4
  62.4 1.2 fusion.6
  63.7 1.1 collective-permute-start.3
  64.8 3.2 %collective-permute-start.4 = (f32[3,32,2048]{2,1,0:T(8,128)}, f32[3,32,2048]{2,1,0:T(8,128)}, u32[]{:S(2)}, u32[]{:S(2)}) collective-permute-start(f32[3,32,2048]{2,1,0:T(8,128)} %get-tuple-element.70), channel_id=1, source_target_pairs={{0,16},{8,24},{16,0},{24,8},{32,48},{40,56},{48,32},{56,40},{64,80... | collective-permute-start | bytes 2359304 | tf_op jit(solution)/shard_map/ppermute | solution.py:307
  68.0 0.4 collective-permute-start.5
  68.4 1.4 add_bitcast_fusion
  69.8 1.3 reshape.299
  71.1 1.3 reshape.298
  72.4 0.8 pad_maximum_fusion.2.w3
  73.2 0.8 pad_maximum_fusion.1.w2
  74.0 28.4 %collective-permute-done.8.a3 = f32[2,2,64,1024]{3,2,1,0:T(8,128)} collective-permute-done((f32[2,2,64,1024]{3,2,1,0:T(8,128)}, f32[2,2,64,1024]{3,2,1,0:T(8,128)}, u32[]{:S(2)}, u32[]{:S(2)}) %collective-permute-start.8) | collective-permute-done | bytes 1048608 | tf_op jit(solution)/shard_map/ppermute | solution.py:307
  102.4 3.1 %all-to-all-done = f32[128,2,16,128]{3,2,1,0:T(8,128)S(1)} async-done(((f32[128,2,16,128]{3,2,1,0:T(8,128)}), f32[128,2,16,128]{3,2,1,0:T(8,128)S(1)}, u32[]{:S(2)}, u32[]{:S(2)}) %all-to-all-start) | async-done | bytes 2097184 | tf_op jit(solution)/shard_map/all_to_all | solution.py:335
  105.5 1.3 copy-done
  106.8 6.6 %late.2 = (f32[2,64,1024]{2,1,0:T(8,128)}, f32[2,64,1024]{2,1,0:T(8,128)}, f32[2,64,1024]{2,1,0:T(8,128)}, f32[2,64,1024]{2,1,0:T(8,128)}) custom-call(s32[1]{0:T(128)} %bitcast.yr, f32[4,4,8,2,16,128]{5,4,3,2,1,0:T(8,128)} %bitcast.139, f32[2,2,64,1024]{3,2,1,0:T(8,128)} %get-tuple-element.79.a0, f32[2,2,64,1024]{3,2,1,0:T(8,128)} %copy-done.2, ...), custom_call_target="tpu_custom_call" | custom-call | flops 1000 | bytes 1000 | tf_op jit(solution)/shard_map/late/pallas_call | solution.py:179
  113.4 9.1 %collective-permute-done.4.r2 = f32[3,32,2048]{2,1,0:T(8,128)} collective-permute-done((f32[3,32,2048]{2,1,0:T(8,128)}, f32[3,32,2048]{2,1,0:T(8,128)}, u32[]{:S(2)}, u32[]{:S(2)}) %collective-permute-start.4) | collective-permute-done | bytes 786464 | tf_op jit(solution)/shard_map/ppermute | solution.py:307
  122.4 0.2 collective-permute-done.5.r3
  122.6 5.5 %early.3 = f32[4,4,8,2,16,128]{5,4,3,2,1,0:T(8,128)} custom-call(s32[1]{0:T(128)} %bitcast.1.zr, f32[3,32,2048]{2,1,0:T(8,128)} %get-tuple-element.87.r0, f32[3,32,2048]{2,1,0:T(8,128)} %collective-permute-done.3.r1, f32[3,32,2048]{2,1,0:T(8,128)} %collective-permute-done.4.r2, f32[3,32,2048]{2,1,0:T(8,128)} %collective-permute-done.5.r3, ...), custom_call_target="tpu_custom_call" | custom-call | flops 1000 | bytes 1000 | tf_op jit(solution)/shard_map/early/pallas_call | solution.py:138
  128.1 5.8 %all-to-all-start.1 = ((f32[128,2,16,128]{3,2,1,0:T(8,128)}), f32[128,2,16,128]{3,2,1,0:T(8,128)S(1)}, u32[]{:S(2)}, u32[]{:S(2)}) async-start(f32[128,2,16,128]{3,2,1,0:T(8,128)} %bitcast.142), calls=%async_computation.1 | async-start | bytes 4194304 | tf_op jit(solution)/shard_map/all_to_all | solution.py:335
  134.0 1.0 collective-permute-start.12
  135.0 2.7 %collective-permute-start.13 = (f32[2,64,1024]{2,1,0:T(8,128)}, f32[2,64,1024]{2,1,0:T(8,128)S(1)}, u32[]{:S(2)}, u32[]{:S(2)}) collective-permute-start(f32[2,64,1024]{2,1,0:T(8,128)} %get-tuple-element.85), channel_id=1, source_target_pairs={{0,64},{8,72},{16,80},{24,88},{32,96},{40,104},{48,112},{56,120},{... | collective-permute-start | bytes 1572872 | tf_op jit(solution)/shard_map/ppermute | solution.py:307
  137.7 1.0 collective-permute-start.14
  138.7 25.6 %all-to-all-done.1 = f32[128,2,16,128]{3,2,1,0:T(8,128)S(1)} async-done(((f32[128,2,16,128]{3,2,1,0:T(8,128)}), f32[128,2,16,128]{3,2,1,0:T(8,128)S(1)}, u32[]{:S(2)}, u32[]{:S(2)}) %all-to-all-start.1) | async-done | bytes 2097184 | tf_op jit(solution)/shard_map/all_to_all | solution.py:335
  164.4 1.3 copy-done.1
  165.7 6.6 %late.3 = (f32[2,64,1024]{2,1,0:T(8,128)}, f32[2,64,1024]{2,1,0:T(8,128)}, f32[2,64,1024]{2,1,0:T(8,128)}, f32[2,64,1024]{2,1,0:T(8,128)}) custom-call(s32[1]{0:T(128)} %bitcast.yr, f32[4,4,8,2,16,128]{5,4,3,2,1,0:T(8,128)} %bitcast.141, f32[2,2,64,1024]{3,2,1,0:T(8,128)} %get-tuple-element.79.a0, f32[2,2,64,1024]{3,2,1,0:T(8,128)} %copy-done.2, ...), custom_call_target="tpu_custom_call" | custom-call | flops 1000 | bytes 1000 | tf_op jit(solution)/shard_map/late/pallas_call | solution.py:179
  172.3 0.2 collective-permute-start.9
  172.5 2.2 %collective-permute-start.10 = (f32[2,64,1024]{2,1,0:T(8,128)}, f32[2,64,1024]{2,1,0:T(8,128)S(1)}, u32[]{:S(2)}, u32[]{:S(2)}) collective-permute-start(f32[2,64,1024]{2,1,0:T(8,128)} %get-tuple-element.93), channel_id=1, source_target_pairs={{0,64},{8,72},{16,80},{24,88},{32,96},{40,104},{48,112},{56,120},{... | collective-permute-start | bytes 1572872 | tf_op jit(solution)/shard_map/ppermute | solution.py:307
  174.6 2.4 %collective-permute-start.11 = (f32[2,64,1024]{2,1,0:T(8,128)}, f32[2,64,1024]{2,1,0:T(8,128)S(1)}, u32[]{:S(2)}, u32[]{:S(2)}) collective-permute-start(f32[2,64,1024]{2,1,0:T(8,128)} %get-tuple-element.94), channel_id=1, source_target_pairs={{0,96},{8,104},{16,112},{24,120},{32,64},{40,72},{48,80},{56,88},{... | collective-permute-start | bytes 1572872 | tf_op jit(solution)/shard_map/ppermute | solution.py:307
  177.0 5.2 %collective-permute-done.13.refs_2_ = f32[2,64,1024]{2,1,0:T(8,128)S(1)} collective-permute-done((f32[2,64,1024]{2,1,0:T(8,128)}, f32[2,64,1024]{2,1,0:T(8,128)S(1)}, u32[]{:S(2)}, u32[]{:S(2)}) %collective-permute-start.13) | collective-permute-done | bytes 524320 | tf_op jit(solution)/shard_map/ppermute | solution.py:307
  182.2 0.8 copy-done.5
  183.0 3.1 %last.2.refs_4_ = f32[2,128,4096]{2,1,0:T(8,128)} custom-call(s32[1]{0:T(128)} %bitcast.yr, f32[2,64,1024]{2,1,0:T(8,128)} %get-tuple-element.83.refs_0_, f32[2,64,1024]{2,1,0:T(8,128)} %copy-done.4, f32[2,64,1024]{2,1,0:T(8,128)} %copy-done.5, f32[2,64,1024]{2,1,0:T(8,128)} %collective-permute-done.14.refs_3_), custom_call_target="tpu_custom_call" | custom-call | flops 1000 | bytes 1000 | tf_op jit(solution)/shard_map/last/pallas_call | solution.py:222
  186.1 5.8 %collective-permute-done.9.refs_1_ = f32[2,64,1024]{2,1,0:T(8,128)S(1)} collective-permute-done((f32[2,64,1024]{2,1,0:T(8,128)}, f32[2,64,1024]{2,1,0:T(8,128)S(1)}, u32[]{:S(2)}, u32[]{:S(2)}) %collective-permute-start.9) | collective-permute-done | bytes 524320 | tf_op jit(solution)/shard_map/ppermute | solution.py:307
  192.0 12.3 %collective-permute-done.10.refs_2_ = f32[2,64,1024]{2,1,0:T(8,128)S(1)} collective-permute-done((f32[2,64,1024]{2,1,0:T(8,128)}, f32[2,64,1024]{2,1,0:T(8,128)S(1)}, u32[]{:S(2)}, u32[]{:S(2)}) %collective-permute-start.10) | collective-permute-done | bytes 524320 | tf_op jit(solution)/shard_map/ppermute | solution.py:307
  204.2 0.8 copy-done.8
  205.0 0.2 copy-done.9
  205.3 3.1 %last.3 = f32[2,128,4096]{2,1,0:T(8,128)} custom-call(s32[1]{0:T(128)} %bitcast.yr, f32[2,64,1024]{2,1,0:T(8,128)} %get-tuple-element.91.refs_0_, f32[2,64,1024]{2,1,0:T(8,128)} %copy-done.7, f32[2,64,1024]{2,1,0:T(8,128)} %copy-done.8, f32[2,64,1024]{2,1,0:T(8,128)} %copy-done.9, f32[2,128,4096]{2,1,0:T(8,128)} %last.2.refs_4_), custom_call_target="tpu_custom_call", output_to_operand_aliasing={{}: (5, {})} | custom-call | flops 1000 | bytes 1000 | tf_op jit(solution)/shard_map/last/pallas_call | solution.py:222
  (77 shorter events, 2.3 us)
Async XLA Ops:
  5.2 28.3 %collective-permute-start = (f32[3,32,2048]{2,1,0:T(8,128)}, f32[3,32,2048]{2,1,0:T(8,128)S(1)}, u32[]{:S(2)}, u32[]{:S(2)}) collective-permute-start(f32[3,32,2048]{2,1,0:T(8,128)} %get-tuple-element.55), channel_id=1, source_target_pairs={{0,8},{8,0},{16,24},{24,16},{32,40},{40,32},{48,56},{56,48},{64,72... | collective-permute-start | bytes 2359304 | tf_op jit(solution)/shard_map/ppermute | solution.py:307
  7.3 38.1 %collective-permute-start.1 = (f32[3,32,2048]{2,1,0:T(8,128)}, f32[3,32,2048]{2,1,0:T(8,128)}, u32[]{:S(2)}, u32[]{:S(2)}) collective-permute-start(f32[3,32,2048]{2,1,0:T(8,128)} %get-tuple-element.56), channel_id=1, source_target_pairs={{0,16},{8,24},{16,0},{24,8},{32,48},{40,56},{48,32},{56,40},{64,80... | collective-permute-start | bytes 2359304 | tf_op jit(solution)/shard_map/ppermute | solution.py:307
  10.9 37.1 %collective-permute-start.2 = (f32[3,32,2048]{2,1,0:T(8,128)}, f32[3,32,2048]{2,1,0:T(8,128)}, u32[]{:S(2)}, u32[]{:S(2)}) collective-permute-start(f32[3,32,2048]{2,1,0:T(8,128)} %get-tuple-element.57), channel_id=1, source_target_pairs={{0,24},{8,16},{16,8},{24,0},{32,56},{40,48},{48,40},{56,32},{64,88... | collective-permute-start | bytes 2359304 | tf_op jit(solution)/shard_map/ppermute | solution.py:307
  15.0 53.0 %collective-permute-start.6 = (f32[2,2,64,1024]{3,2,1,0:T(8,128)}, f32[2,2,64,1024]{3,2,1,0:T(8,128)S(1)}, u32[]{:S(2)}, u32[]{:S(2)}) collective-permute-start(f32[2,2,64,1024]{3,2,1,0:T(8,128)} %get-tuple-element.80), channel_id=1, source_target_pairs={{0,32},{8,40},{16,48},{24,56},{32,0},{40,8},{48,16},{56,24},{64,96... | collective-permute-start | bytes 3145736 | tf_op jit(solution)/shard_map/ppermute | solution.py:307
  16.6 57.4 %collective-permute-start.7 = (f32[2,2,64,1024]{3,2,1,0:T(8,128)}, f32[2,2,64,1024]{3,2,1,0:T(8,128)}, u32[]{:S(2)}, u32[]{:S(2)}) collective-permute-start(f32[2,2,64,1024]{3,2,1,0:T(8,128)} %get-tuple-element.81), channel_id=1, source_target_pairs={{0,64},{8,72},{16,80},{24,88},{32,96},{40,104},{48,112},{56,120},{... | collective-permute-start | bytes 3145736 | tf_op jit(solution)/shard_map/ppermute | solution.py:307
  19.9 5.4 %copy-start.10 = (f32[2,16,16]{2,1,0:T(8,128)S(1)}, f32[2,16,16]{2,1,0:T(8,128)}, u32[]{:S(2)}) copy-start(f32[2,16,16]{2,1,0:T(8,128)} %param.8) | copy-start | bytes 6148
  19.9 5.5 %copy-start.11 = (s32[4,128]{1,0:T(4,128)S(1)}, s32[4,128]{1,0:T(4,128)}, u32[]{:S(2)}) copy-start(s32[4,128]{1,0:T(4,128)} %param.9) | copy-start | bytes 6148
  19.9 7.0 %copy-start.6 = (f32[4,4,2,2,16,16]{5,4,3,2,1,0:T(8,128)S(1)}, f32[4,4,2,2,16,16]{5,4,3,2,1,0:T(8,128)}, u32[]{:S(2)}) copy-start(f32[4,4,2,2,16,16]{5,4,3,2,1,0:T(8,128)} %param.7) | copy-start | bytes 196612
  33.6 14.4 %copy-start.3 = (f32[3,32,2048]{2,1,0:T(8,128)}, f32[3,32,2048]{2,1,0:T(8,128)S(1)}, u32[]{:S(2)}) copy-start(f32[3,32,2048]{2,1,0:T(8,128)S(1)} %collective-permute-done.r1) | copy-start | bytes 2359300
  33.6 68.8 %collective-permute-start.8 = (f32[2,2,64,1024]{3,2,1,0:T(8,128)}, f32[2,2,64,1024]{3,2,1,0:T(8,128)}, u32[]{:S(2)}, u32[]{:S(2)}) collective-permute-start(f32[2,2,64,1024]{3,2,1,0:T(8,128)} %get-tuple-element.82), channel_id=1, source_target_pairs={{0,96},{8,104},{16,112},{24,120},{32,64},{40,72},{48,80},{56,88},{... | collective-permute-start | bytes 3145736 | tf_op jit(solution)/shard_map/ppermute | solution.py:307
  53.5 52.0 %all-to-all-start = ((f32[128,2,16,128]{3,2,1,0:T(8,128)}), f32[128,2,16,128]{3,2,1,0:T(8,128)S(1)}, u32[]{:S(2)}, u32[]{:S(2)}) async-start(f32[128,2,16,128]{3,2,1,0:T(8,128)} %bitcast.140), calls=%async_computation | async-start | bytes 4194304 | tf_op jit(solution)/shard_map/all_to_all | solution.py:335
  63.7 49.7 %collective-permute-start.3 = (f32[3,32,2048]{2,1,0:T(8,128)}, f32[3,32,2048]{2,1,0:T(8,128)}, u32[]{:S(2)}, u32[]{:S(2)}) collective-permute-start(f32[3,32,2048]{2,1,0:T(8,128)} %get-tuple-element.69), channel_id=1, source_target_pairs={{0,8},{8,0},{16,24},{24,16},{32,40},{40,32},{48,56},{56,48},{64,72... | collective-permute-start | bytes 2359304 | tf_op jit(solution)/shard_map/ppermute | solution.py:307
  64.8 57.7 %collective-permute-start.4 = (f32[3,32,2048]{2,1,0:T(8,128)}, f32[3,32,2048]{2,1,0:T(8,128)}, u32[]{:S(2)}, u32[]{:S(2)}) collective-permute-start(f32[3,32,2048]{2,1,0:T(8,128)} %get-tuple-element.70), channel_id=1, source_target_pairs={{0,16},{8,24},{16,0},{24,8},{32,48},{40,56},{48,32},{56,40},{64,80... | collective-permute-start | bytes 2359304 | tf_op jit(solution)/shard_map/ppermute | solution.py:307
  68.0 37.5 %copy-start.2 = (f32[2,2,64,1024]{3,2,1,0:T(8,128)}, f32[2,2,64,1024]{3,2,1,0:T(8,128)S(1)}, u32[]{:S(2)}) copy-start(f32[2,2,64,1024]{3,2,1,0:T(8,128)S(1)} %collective-permute-done.6.a1) | copy-start | bytes 3145732
  68.0 54.6 %collective-permute-start.5 = (f32[3,32,2048]{2,1,0:T(8,128)}, f32[3,32,2048]{2,1,0:T(8,128)}, u32[]{:S(2)}, u32[]{:S(2)}) collective-permute-start(f32[3,32,2048]{2,1,0:T(8,128)} %get-tuple-element.71), channel_id=1, source_target_pairs={{0,24},{8,16},{16,8},{24,0},{32,56},{40,48},{48,40},{56,32},{64,88... | collective-permute-start | bytes 2359304 | tf_op jit(solution)/shard_map/ppermute | solution.py:307
  105.5 1.3 copy-start
  128.1 36.2 %all-to-all-start.1 = ((f32[128,2,16,128]{3,2,1,0:T(8,128)}), f32[128,2,16,128]{3,2,1,0:T(8,128)S(1)}, u32[]{:S(2)}, u32[]{:S(2)}) async-start(f32[128,2,16,128]{3,2,1,0:T(8,128)} %bitcast.142), calls=%async_computation.1 | async-start | bytes 4194304 | tf_op jit(solution)/shard_map/all_to_all | solution.py:335
  134.0 40.7 %collective-permute-start.12 = (f32[2,64,1024]{2,1,0:T(8,128)}, f32[2,64,1024]{2,1,0:T(8,128)S(1)}, u32[]{:S(2)}, u32[]{:S(2)}) collective-permute-start(f32[2,64,1024]{2,1,0:T(8,128)} %get-tuple-element.84), channel_id=1, source_target_pairs={{0,32},{8,40},{16,48},{24,56},{32,0},{40,8},{48,16},{56,24},{64,96... | collective-permute-start | bytes 1572872 | tf_op jit(solution)/shard_map/ppermute | solution.py:307
  135.0 47.2 %collective-permute-start.13 = (f32[2,64,1024]{2,1,0:T(8,128)}, f32[2,64,1024]{2,1,0:T(8,128)S(1)}, u32[]{:S(2)}, u32[]{:S(2)}) collective-permute-start(f32[2,64,1024]{2,1,0:T(8,128)} %get-tuple-element.85), channel_id=1, source_target_pairs={{0,64},{8,72},{16,80},{24,88},{32,96},{40,104},{48,112},{56,120},{... | collective-permute-start | bytes 1572872 | tf_op jit(solution)/shard_map/ppermute | solution.py:307
  137.7 44.5 %collective-permute-start.14 = (f32[2,64,1024]{2,1,0:T(8,128)}, f32[2,64,1024]{2,1,0:T(8,128)}, u32[]{:S(2)}, u32[]{:S(2)}) collective-permute-start(f32[2,64,1024]{2,1,0:T(8,128)} %get-tuple-element.86), channel_id=1, source_target_pairs={{0,96},{8,104},{16,112},{24,120},{32,64},{40,72},{48,80},{56,88},{... | collective-permute-start | bytes 1572872 | tf_op jit(solution)/shard_map/ppermute | solution.py:307
  164.4 1.3 copy-start.1
  172.3 19.7 %collective-permute-start.9 = (f32[2,64,1024]{2,1,0:T(8,128)}, f32[2,64,1024]{2,1,0:T(8,128)S(1)}, u32[]{:S(2)}, u32[]{:S(2)}) collective-permute-start(f32[2,64,1024]{2,1,0:T(8,128)} %get-tuple-element.92), channel_id=1, source_target_pairs={{0,32},{8,40},{16,48},{24,56},{32,0},{40,8},{48,16},{56,24},{64,96... | collective-permute-start | bytes 1572872 | tf_op jit(solution)/shard_map/ppermute | solution.py:307
  172.5 31.8 %collective-permute-start.10 = (f32[2,64,1024]{2,1,0:T(8,128)}, f32[2,64,1024]{2,1,0:T(8,128)S(1)}, u32[]{:S(2)}, u32[]{:S(2)}) collective-permute-start(f32[2,64,1024]{2,1,0:T(8,128)} %get-tuple-element.93), channel_id=1, source_target_pairs={{0,64},{8,72},{16,80},{24,88},{32,96},{40,104},{48,112},{56,120},{... | collective-permute-start | bytes 1572872 | tf_op jit(solution)/shard_map/ppermute | solution.py:307
  174.6 7.6 %copy-start.4 = (f32[2,64,1024]{2,1,0:T(8,128)}, f32[2,64,1024]{2,1,0:T(8,128)S(1)}, u32[]{:S(2)}) copy-start(f32[2,64,1024]{2,1,0:T(8,128)S(1)} %collective-permute-done.12.refs_1_) | copy-start | bytes 1572868
  174.6 29.6 %collective-permute-start.11 = (f32[2,64,1024]{2,1,0:T(8,128)}, f32[2,64,1024]{2,1,0:T(8,128)S(1)}, u32[]{:S(2)}, u32[]{:S(2)}) collective-permute-start(f32[2,64,1024]{2,1,0:T(8,128)} %get-tuple-element.94), channel_id=1, source_target_pairs={{0,96},{8,104},{16,112},{24,120},{32,64},{40,72},{48,80},{56,88},{... | collective-permute-start | bytes 1572872 | tf_op jit(solution)/shard_map/ppermute | solution.py:307
  182.2 0.8 copy-start.5
  192.0 12.3 %copy-start.7 = (f32[2,64,1024]{2,1,0:T(8,128)}, f32[2,64,1024]{2,1,0:T(8,128)S(1)}, u32[]{:S(2)}) copy-start(f32[2,64,1024]{2,1,0:T(8,128)S(1)} %collective-permute-done.9.refs_1_) | copy-start | bytes 1572868
  204.2 0.8 copy-start.8
  204.2 1.0 copy-start.9

commit v3 on v2

v3 whole, which is shorter than its diff:
```python
import functools

import jax
import jax.numpy as jnp
from jax import lax
from jax.experimental import pallas as pl
from jax.experimental.pallas import tpu as pltpu
from jax.sharding import PartitionSpec as P

NCLASS = 4
PTS = 16
BOX = 8
FL = 4096
Q = 4
HIGHEST = lax.Precision.HIGHEST
SIN = (1.0, -0.04166664555668831, 0.0005208156653679907, -3.095163492616848e-06, 1.0176427700514523e-08)
COS = (0.9999999403953552, -0.1249997615814209, 0.002603973727673292, -2.1646354070981033e-05, 9.044205739883182e-08)
VMEM = 56 * 1024 * 1024


def cost(flops=1000):
    return pl.CostEstimate(flops=flops, bytes_accessed=1000, transcendentals=0)


def poly(coefs, u):
    r = coefs[-1]
    for c in coefs[-2::-1]:
        r = r * u + c
    return r


def turn(re, im, a):
    u = a * a
    s2 = a * poly(SIN, u)
    sine = s2 * poly(COS, u)
    cosine = 1.0 - 0.5 * (s2 * s2)
    return cosine * re - sine * im, sine * re + cosine * im


def split3(x):
    hi = x.astype(jnp.bfloat16)
    lo = (x - hi.astype(jnp.float32)).astype(jnp.bfloat16)
    return jnp.concatenate([hi, lo, hi], axis=0)


def mm(w, x):
    return jnp.dot(w, split3(x), preferred_element_type=jnp.float32)


def by_box(v):
    return jnp.swapaxes(v.reshape(PTS, BOX, v.shape[-1]), 0, 1)


def swap_halves(a, b):
    low = lax.broadcasted_iota(jnp.int32, a.shape, a.ndim - 1) < 64
    return (
        jnp.where(low, a, pltpu.roll(b, 64, a.ndim - 1)),
        jnp.where(low, pltpu.roll(a, 64, a.ndim - 1), b),
    )


def first_kernel(n, zr, *refs):
    src, ang, outs, room = refs[:n], refs[n : 2 * n], refs[2 * n : 2 * n + Q], refs[-1]
    lanes = room.shape[-1]
    for d in range(n):
        re, im = turn(src[d][0], src[d][1], ang[d][0])
        for c, v in enumerate((re, im, ang[d][1])):
            room[c] = by_box(v)
        for e, o in enumerate(outs):
            for c in range(3):
                for i in range(2):
                    o[c, PTS * i : PTS * i + PTS, lanes * d : lanes * d + lanes] = room[c, 2 * ((zr[0] + e) % Q) + i]


def first(chunk, z, source, angles):
    tile, count = chunk
    lanes, n = 128 * count, 4

    def spec(d):
        return pl.BlockSpec((2, PTS * BOX, lanes), lambda g, zr: (0, 0, (n * g + d) * (4 // count) + tile // count))

    return pl.pallas_call(
        functools.partial(first_kernel, n),
        grid_spec=pltpu.PrefetchScalarGridSpec(
            num_scalar_prefetch=1,
            grid=(8 // n,),
            in_specs=[spec(d) for d in range(n)] * 2,
            out_specs=[pl.BlockSpec((3, 2 * PTS, lanes * n), lambda g, zr: (0, 0, g))] * Q,
            scratch_shapes=[pltpu.VMEM((3, BOX, PTS, lanes), jnp.float32)],
        ),
        out_shape=[jax.ShapeDtypeStruct((3, 2 * PTS, lanes * 8), jnp.float32)] * Q,
        compiler_params=pltpu.CompilerParams(vmem_limit_bytes=VMEM),
        cost_estimate=cost(),
        name="first",
    )(z, *[source] * n, *[angles] * n)


def share_kernel(yr, a, o0, o1, o2, o3, room):
    for l in range(2):
        for g in range(2):
            for t in range(Q):
                pair = [
                    by_box(a[l, :, 512 * d + 128 * t : 512 * d + 128 * t + 128]).reshape(Q, 2, PTS, 128)
                    for d in (2 * g, 2 * g + 1)
                ]
                for n in range(2):
                    for h, v in enumerate(swap_halves(pair[0][:, n], pair[1][:, n])):
                        room[2 * n + h] = v.reshape(Q * PTS, 128)
                for e, o in enumerate((o0, o1, o2, o3)):
                    o[t, l, :, 128 * g : 128 * g + 128] = room[(yr[0] + e) % Q]


def share(y, angles):
    return pl.pallas_call(
        share_kernel,
        grid_spec=pltpu.PrefetchScalarGridSpec(
            num_scalar_prefetch=1,
            grid=(2,),
            in_specs=[pl.BlockSpec((2, PTS * BOX, 2048), lambda d, yr: (1, 0, d))],
            out_specs=[pl.BlockSpec((4, 2, Q * PTS, 256), lambda d, yr: (0, 0, 0, d))] * Q,
            scratch_shapes=[pltpu.VMEM((Q, Q * PTS, 128), jnp.float32)],
        ),
        out_shape=[jax.ShapeDtypeStruct((4, 2, Q * PTS, 512), jnp.float32)] * Q,
        compiler_params=pltpu.CompilerParams(vmem_limit_bytes=VMEM),
        cost_estimate=cost(),
        name="share",
    )(y, angles)


def early_kernel(zr, r0, r1, r2, r3, w0, w1, o, r):
    for e, v in enumerate((r0, r1, r2, r3)):
        r[(zr[0] + Q - e) % Q] = v[...]
    count = o.shape[3]
    x = []
    for q in range(2):
        part = []
        for c in range(2):
            rows = jnp.concatenate([r[2 * q + i, c] for i in range(2)], axis=0)
            part.append(mm(w0[q], rows))
        angle = jnp.concatenate([r[2 * q + i, 2] for i in range(2)], axis=0)
        x.append(turn(*part, angle))
    for n in range(2):
        for m in range(2):
            here = slice(32 * m + PTS * n, 32 * m + PTS * n + PTS)
            rows = jnp.concatenate([x[i][c][here] for i in range(2) for c in range(2)], axis=0)
            out = mm(w1[n, m], rows)
            for i in range(2):
                both = [out[32 * i + PTS * c : 32 * i + PTS * c + PTS] for c in range(2)]
                for t in range(both[0].shape[1] // 128):
                    pieces = swap_halves(*[v[:, 128 * t : 128 * t + 128] for v in both])
                    for h in range(2):
                        o[2 * n + h, m + 2 * i, t // count, t % count] = pieces[h]


def early(chunk, z, parts, w0, w1, flops, steps=2):
    count = chunk[1]
    n = 8 // steps
    return pl.pallas_call(
        early_kernel,
        grid_spec=pltpu.PrefetchScalarGridSpec(
            num_scalar_prefetch=1,
            grid=(steps,),
            in_specs=[pl.BlockSpec((3, 2 * PTS, 128 * count * n), lambda d, zr: (0, 0, d))] * Q
            + [
                pl.BlockSpec((2, 64, 192), lambda d, zr: (0, 0, 0)),
                pl.BlockSpec((2, 2, 64, 192), lambda d, zr: (0, 0, 0, 0)),
            ],
            out_specs=pl.BlockSpec((Q, Q, n, count, PTS, 128), lambda d, zr: (0, 0, d, 0, 0, 0)),
            scratch_shapes=[pltpu.VMEM((Q, 3, 2 * PTS, 128 * count * n), jnp.float32)],
        ),
        out_shape=jax.ShapeDtypeStruct((Q, Q, 8, count, PTS, 128), jnp.float32),
        compiler_params=pltpu.CompilerParams(vmem_limit_bytes=VMEM),
        cost_estimate=cost(flops),
        name="early",
    )(z, *parts, w0, w1)


def late_kernel(yr, x, a0, a1, a2, a3, w2, w3, o0, o1, o2, o3, turns, done):
    y = yr[0]
    pairs, count = x.shape[2] // 2, x.shape[3]
    for e, a in enumerate((a0, a1, a2, a3)):
        turns[(y + Q - e) % Q] = a[...]
    for j in range(count):
        for t in range(Q):
            here = slice(PTS * t, PTS * t + PTS)
            angles = [jnp.concatenate([turns[e, j, l, here] for e in range(Q)], axis=0) for l in range(2)]
            split = [[swap_halves(x[e, t, 2 * g, j], x[e, t, 2 * g + 1, j]) for g in range(pairs)] for e in range(Q)]
            pair = [
                jnp.concatenate([jnp.concatenate([v[c] for v in row], axis=1) for row in split], axis=0)
                for c in range(2)
            ]
            for l, w in enumerate((w2, w3)):
                pair = [mm(w[t], v) for v in turn(*pair, angles[l])]
            for e in range(Q):
                for c in range(2):
                    done[e, j, c, here] = pair[c][PTS * e : PTS * e + PTS]
    for e, o in enumerate((o0, o1, o2, o3)):
        o[...] = done[(y + e) % Q]


def late(chunk, y, x, angles, w2, w3, flops, steps=2):
    tile, count = chunk
    n = 8 // steps
    return pl.pallas_call(
        late_kernel,
        grid_spec=pltpu.PrefetchScalarGridSpec(
            num_scalar_prefetch=1,
            grid=(steps,),
            in_specs=[pl.BlockSpec((Q, Q, n, count, PTS, 128), lambda d, yr: (0, 0, d, 0, 0, 0))]
            + [pl.BlockSpec((count, 2, Q * PTS, 64 * n), lambda d, yr: (tile // count, 0, 0, d))] * Q
            + [pl.BlockSpec((Q, 64, 192), lambda d, yr: (0, 0, 0))] * 2,
            out_specs=[pl.BlockSpec((count, 2, Q * PTS, 64 * n), lambda d, yr: (0, 0, 0, d))] * Q,
            scratch_shapes=[pltpu.VMEM((Q, count, 2, Q * PTS, 64 * n), jnp.float32)] * 2,
        ),
        out_shape=[jax.ShapeDtypeStruct((count, 2, Q * PTS, 512), jnp.float32)] * Q,
        compiler_params=pltpu.CompilerParams(vmem_limit_bytes=VMEM),
        cost_estimate=cost(flops),
        name="late",
    )(y, x, *angles, w2, w3)


def last_kernel(chunk, yr, *refs):
    tile, count = chunk
    ins, (o, room, ready, sems) = refs[:Q], refs[-4:]
    copies = []
    for g in range(4):
        here = slice(128 * g, 128 * g + 128)
        for j in range(count):
            for c in range(2):
                for e in range(Q):
                    at = (yr[0] + Q - e) % Q
                    for t in range(Q):
                        room[at % 2, 2 * t + at // 2] = ins[e][j, c, PTS * t : PTS * t + PTS, here]
                for i, v in enumerate(swap_halves(room[0], room[1])):
                    lanes = 128 * (count * (2 * g + i) + j)
                    ready[c, :, lanes : lanes + 128] = jnp.swapaxes(v, 0, 1).reshape(PTS * BOX, 128)
        for d in (2 * g, 2 * g + 1):
            copies.append(
                pltpu.make_async_copy(
                    ready.at[:, :, pl.ds(128 * count * d, 128 * count)],
                    o.at[:, :, pl.ds(512 * d + 128 * tile, 128 * count)],
                    sems.at[d],
                )
            )
            copies[-1].start()
    for copy in copies:
        copy.wait()


def last(chunk, y, parts, before):
    extra = [] if before is None else [before]
    count = chunk[1]
    return pl.pallas_call(
        functools.partial(last_kernel, chunk),
        grid_spec=pltpu.PrefetchScalarGridSpec(
            num_scalar_prefetch=1,
            grid=(1,),
            in_specs=[pl.BlockSpec((count, 2, Q * PTS, 512), lambda d, yr: (0, 0, 0, 0))] * Q
            + [pl.BlockSpec(memory_space=pl.ANY)] * len(extra),
            out_specs=pl.BlockSpec(memory_space=pl.ANY),
            scratch_shapes=[
                pltpu.VMEM((2, BOX, PTS, 128), jnp.float32),
                pltpu.VMEM((2, PTS * BOX, 1024 * count), jnp.float32),
                pltpu.SemaphoreType.DMA((8,)),
            ],
        ),
        out_shape=jax.ShapeDtypeStruct((2, PTS * BOX, FL), jnp.float32),
        input_output_aliases={Q + 1: 0} if extra else {},
        compiler_params=pltpu.CompilerParams(vmem_limit_bytes=VMEM),
        cost_estimate=cost(),
        name="last",
    )(y, *parts, *extra)


def pick(onehot, options):
    shape = onehot.shape + options.shape[1:]
    mask = onehot.reshape(onehot.shape + (1,) * (options.ndim - 1))
    return jnp.sum(jnp.where(mask, jnp.broadcast_to(options, shape), 0.0), axis=onehot.ndim - 1)


def halves(tables, classes, half):
    chosen = pick(classes[..., None] == jnp.arange(NCLASS), tables)
    upper = (half == 1)[:, None, None, None]
    own, other = chosen[:, :, 0, 0], chosen[:, :, 0, 1]
    own = jnp.where(upper, chosen[:, :, 1, 1], own)
    other = jnp.where(upper, chosen[:, :, 1, 0], other)
    return own, other


def two_parts(w):
    hi = lax.reduce_precision(w, 8, 7)
    lo = w - hi
    return jnp.concatenate([hi, hi, lo], axis=-1).astype(jnp.bfloat16)


def weights(cheb_tables, switch_kernel, box_class, y, z):
    near = jnp.arange(Q)
    byplace = box_class.reshape(4, Q, Q, BOX)
    mine_y = lax.dynamic_index_in_dim(byplace, y, 1, False)
    mine_z = lax.dynamic_index_in_dim(byplace, z, 2, False)
    mine_y = lax.dynamic_slice_in_dim(mine_y, 2 * z, 2, 2)
    mine_z = lax.dynamic_index_in_dim(mine_z.reshape(4, Q, Q, 2), y // 2, 3, False)
    by_z, by_y = mine_y.transpose(1, 0, 2), mine_z.transpose(1, 0, 2)
    eye = jnp.eye(2, dtype=jnp.float32)
    k0, k1 = switch_kernel[0], switch_kernel[1]
    kc = jnp.stack([jnp.stack([k0, -k1]), jnp.stack([k1, k0])])

    own, other = halves(cheb_tables[0], by_z[:, 0], near & 1)
    own, other = (v.reshape(2, 2, 2, PTS, PTS) for v in (own, other))
    w0 = jnp.einsum("qints,ij,nm->qintjms", own, eye, eye, precision=HIGHEST)
    w0 += jnp.einsum("qints,ij,nm->qintjms", other, 1 - eye, eye, precision=HIGHEST)
    w0 = w0.reshape(2, 64, 64)

    own, other = halves(cheb_tables[1], by_z[:, 1], (near >> 1) & 1)
    own, other = (
        jnp.einsum("cdtu,pus->pctds", kc, v.reshape(8, PTS, PTS), precision=HIGHEST).reshape(2, 2, 2, 2, PTS, 2, PTS)
        for v in (own, other)
    )
    w1 = jnp.einsum("imnctds,ih->nmicthds", own, eye, precision=HIGHEST)
    w1 += jnp.einsum("imnctds,ih->nmicthds", other, 1 - eye, precision=HIGHEST)
    w1 = w1.reshape(2, 2, 64, 64)

    late_w = []
    for l in (2, 3):
        own, other = halves(cheb_tables[l], by_y[:, l], (near >> (l - 2)) & 1)
        same = jnp.eye(Q, dtype=jnp.float32)
        swap = (near[:, None] ^ (l - 1) == near).astype(jnp.float32)
        w = jnp.einsum("ekts,eh->keths", own, same, precision=HIGHEST)
        w += jnp.einsum("ekts,eh->keths", other, swap, precision=HIGHEST)
        late_w.append(two_parts(w.reshape(Q, 64, 64)))
    return two_parts(w0), two_parts(w1), late_w[0], late_w[1]


def swapped(part, e, stride):
    count = lax.axis_size("space")

    def target(i):
        at = i // stride % Q
        return i + ((at + e) % Q - at) * stride

    return lax.ppermute(part, "space", [(i, target(i)) for i in range(count)])


def exchange(parts, stride):
    return [parts[0]] + [swapped(parts[e], e, stride) for e in range(1, Q)]


CHUNKS = ((0, 2), (2, 1), (3, 1))
LONG = 40_000_000_000


def on_device(source, angles, cheb_tables, switch_kernel, box_class):
    place = lax.axis_index("space")
    y, z = place // Q, place % Q
    yr, zr = y.reshape(1).astype(jnp.int32), z.reshape(1).astype(jnp.int32)
    source = source.reshape(2, PTS * BOX, FL)
    angles = angles.reshape(4, PTS * BOX, FL)
    tie = lax.optimization_barrier
    count = len(CHUNKS)

    sent, here, mixed, moved, back = [None] * count, [None] * count, [None] * count, [None] * count, [None] * count
    ready = first(CHUNKS[0], zr, source, angles)
    ready, source, angles = tie((ready, source, angles))
    here[0] = exchange(ready, 1)
    turns = share(yr, angles)
    turns, source, angles = tie((turns, source, angles))
    turns = list(turns)
    turns[1], turns[3] = swapped(turns[1], 1, Q), swapped(turns[3], 3, Q)
    for k in range(1, count):
        sent[k] = first(CHUNKS[k], zr, source, angles)
    sent[1:], cheb_tables, switch_kernel, box_class = tie((sent[1:], cheb_tables, switch_kernel, box_class))
    w0, w1, w2, w3 = weights(cheb_tables, switch_kernel, box_class, y, z)
    here[0], sent[1:], w0, w1, w2, w3 = tie((here[0], sent[1:], w0, w1, w2, w3))

    def do_late(k):
        if k:
            if k + 1 < len(CHUNKS):
                back[k - 1], moved[k] = tie((back[k - 1], moved[k]))
            else:
                back[k - 1][1], moved[k] = tie((back[k - 1][1], moved[k]))
        done = late(CHUNKS[k], yr, moved[k], turns, w2, w3, (8_000_000_000, 7_000_000_000, 1000)[k])
        back[k] = exchange(done, Q)

    for k, chunk in enumerate(CHUNKS):
        if k + 1 < count:
            here[k], sent[k + 1] = tie((here[k], sent[k + 1]))
            here[k + 1] = exchange(sent[k + 1], 1)
        if k == 1:
            here[k], turns[2] = tie((here[k], turns[2]))
        mixed[k] = early(chunk, zr, here[k], w0, w1, (1000, LONG, 3_000_000_000)[k])
        if k:
            moved[k - 1], mixed[k] = tie((moved[k - 1], mixed[k]))
        if k == 0:
            turns[1], turns[2], turns[3] = tie((turns[1], turns[2], turns[3]))
            turns[2] = swapped(turns[2], 2, Q)
        all_parts = lax.all_to_all(mixed[k].reshape(128, chunk[1], PTS, 128), ("space", "freq"), 0, 0, tiled=True)
        moved[k] = all_parts.reshape(Q, Q, 8, chunk[1], PTS, 128)
        if k:
            do_late(k - 1)
            if k + 1 < count:
                back[k - 1][0], here[k + 1] = tie((back[k - 1][0], here[k + 1]))
    do_late(count - 1)
    result = None
    for k, chunk in enumerate(CHUNKS):
        if k + 1 < count:
            back[k], back[k + 1][0] = tie((back[k], back[k + 1][0]))
        result = last(chunk, yr, back[k], result)
    return result.reshape(2, PTS, BOX, FL)


def solution(mesh):
    in_specs = (P(None, None, "space", "freq"), P(None, None, "space", "freq"), P(), P(), P())
    out_specs = P(None, None, "space", "freq")
    return jax.shard_map(
        on_device, mesh=mesh, in_specs=in_specs, out_specs=out_specs, check_vma=False
    )
```

time: 210 us -> 197 us (0.938)
  waiting for transfers between devices: 104 us -> 66 us
  starting transfers between devices: 37.9 us -> 58.5 us
  Pallas kernels: 45.2 us -> 53.3 us
    all_to_all x2 -> x3, waiting for transfers between devices: 28.7 us -> 8.66 us  [on_device(): lax.all_to_all(mixed[k].reshape(128, chunk[1], PTS, 128), ('space', 'freq...]
    ppermute x15 -> x21, waiting for transfers between devices: 75.1 us -> 57.3 us  [swapped(): return lax.ppermute(part, 'space', [(i, target(i)) for i in range(count)])]
    ppermute x15 -> x21, starting transfers between devices: 24.5 us -> 35 us  [swapped(): return lax.ppermute(part, 'space', [(i, target(i)) for i in range(count)])]
    all_to_all x2 -> x3, starting transfers between devices: 13.4 us -> 23.5 us  [on_device(): lax.all_to_all(mixed[k].reshape(128, chunk[1], PTS, 128), ('space', 'freq...]
    pallas_call x2 -> x3, Pallas kernels: 13.2 us -> 16 us  [late(): pl.pallas_call(late_kernel, grid_spec=pltpu.PrefetchScalarGridSpec(num_sc...]
    pallas_call x2 -> x3, Pallas kernels: 11.1 us -> 13.4 us  [early(): pl.pallas_call(early_kernel, grid_spec=pltpu.PrefetchScalarGridSpec(num_s...]
    select_n x3, other arithmetic: 2.47 us -> 0.27 us  [halves(): own = jnp.where(upper, chosen[:, :, 1, 1], own)]
    pallas_call x2 -> x3, Pallas kernels: 6.17 us -> 8.11 us  [last(): pl.pallas_call(functools.partial(last_kernel, chunk), grid_spec=pltpu.Pre...]
  transfers between devices with their start and end apart: 17 -> 24, of which waited for: 10 -> 10; matrix products, arithmetic and copies ran while one was open for 8% -> 8% of each run, Pallas kernels for 15% -> 21%
where the time goes in v3:
time: 197 us; the launch traced here: 196 us
  waiting for transfers between devices  66 us (34%)
  starting transfers between devices  58.5 us (30%)
  Pallas kernels  53.3 us (27%)
  other arithmetic  9.4 us (5%)
  local copies, waits for them, and re-layouts  7.68 us (4%)
    ppermute x21, waiting for transfers between devices, swapped(): return lax.ppermute(part, 'space', [(i, target(i)) for i in range(count)])  57.3 us
    ppermute x21, starting transfers between devices, swapped(): return lax.ppermute(part, 'space', [(i, target(i)) for i in range(count)])  35 us
    all_to_all x3, starting transfers between devices, on_device(): lax.all_to_all(mixed[k].reshape(128, chunk[1], PTS, 128), ('space', 'freq...  23.5 us
    pallas_call x3, Pallas kernels, late(): pl.pallas_call(late_kernel, grid_spec=pltpu.PrefetchScalarGridSpec(num_sc...  16 us
    pallas_call x3, Pallas kernels, early(): pl.pallas_call(early_kernel, grid_spec=pltpu.PrefetchScalarGridSpec(num_s...  13.4 us
    pallas_call x3, Pallas kernels, first(): pl.pallas_call(functools.partial(first_kernel, n), grid_spec=pltpu.Prefet...  11.5 us
    all_to_all x3, waiting for transfers between devices, on_device(): lax.all_to_all(mixed[k].reshape(128, chunk[1], PTS, 128), ('space', 'freq...  8.66 us
    pallas_call x3, Pallas kernels, last(): pl.pallas_call(functools.partial(last_kernel, chunk), grid_spec=pltpu.Pre...  8.11 us
  transfers between devices with their start and end apart: 24, of which 10 were waited for; matrix products, arithmetic and copies ran while one was open for 8% of the time, Pallas kernels for 21%

profile of v3, /device:TPU:0, one launch (start us, length us, event | category | flops | bytes accessed | tf_op | source)
XLA Modules:
  0.0 196.4 jit_solution(15847746805217833910)
XLA Ops:
  0.0 5.0 %first.3 = (f32[3,32,2048]{2,1,0:T(8,128)}, f32[3,32,2048]{2,1,0:T(8,128)}, f32[3,32,2048]{2,1,0:T(8,128)}, f32[3,32,2048]{2,1,0:T(8,128)}) custom-call(s32[1]{0:T(128)} %bitcast.1.zr, f32[2,128,4096]{2,1,0:T(8,128)} %bitcast.141, f32[2,128,4096]{2,1,0:T(8,128)} %bitcast.142, f32[2,128,4096]{2,1,0:T(8,128)} %bitcast.143, f32[2,128,4096]{2,1,0:T(8,128)} %bitcast.144, ...), custom_call_target="tpu_custom_call" | custom-call | flops 1000 | bytes 1000 | tf_op jit(solution)/shard_map/first/pallas_call | solution.py:82
  5.0 4.3 %share.1 = (f32[4,2,64,512]{3,2,1,0:T(8,128)}, f32[4,2,64,512]{3,2,1,0:T(8,128)}, f32[4,2,64,512]{3,2,1,0:T(8,128)}, f32[4,2,64,512]{3,2,1,0:T(8,128)}) custom-call(s32[1]{0:T(128)} %bitcast.yr, f32[4,128,4096]{2,1,0:T(8,128)} %bitcast.132), custom_call_target="tpu_custom_call" | custom-call | flops 1000 | bytes 1000 | tf_op jit(solution)/shard_map/share/pallas_call | solution.py:114
  9.3 1.7 collective-permute-start.6
  11.0 1.6 collective-permute-start.7
  12.5 2.0 %collective-permute-start = (f32[3,32,2048]{2,1,0:T(8,128)}, f32[3,32,2048]{2,1,0:T(8,128)}, u32[]{:S(2)}, u32[]{:S(2)}) collective-permute-start(f32[3,32,2048]{2,1,0:T(8,128)} %get-tuple-element.127), channel_id=1, source_target_pairs={{0,8},{8,16},{16,24},{24,0},{32,40},{40,48},{48,56},{56,32},{64,72... | collective-permute-start | bytes 2359304 | tf_op jit(solution)/shard_map/ppermute | solution.py:341
  14.5 3.6 %collective-permute-start.1 = (f32[3,32,2048]{2,1,0:T(8,128)}, f32[3,32,2048]{2,1,0:T(8,128)}, u32[]{:S(2)}, u32[]{:S(2)}) collective-permute-start(f32[3,32,2048]{2,1,0:T(8,128)} %get-tuple-element.128), channel_id=1, source_target_pairs={{0,16},{8,24},{16,0},{24,8},{32,48},{40,56},{48,32},{56,40},{64,80... | collective-permute-start | bytes 2359304 | tf_op jit(solution)/shard_map/ppermute | solution.py:341
  18.1 1.0 collective-permute-start.2
  19.1 3.3 %first.5 = (f32[3,32,1024]{2,1,0:T(8,128)}, f32[3,32,1024]{2,1,0:T(8,128)}, f32[3,32,1024]{2,1,0:T(8,128)}, f32[3,32,1024]{2,1,0:T(8,128)}) custom-call(s32[1]{0:T(128)} %bitcast.1.zr, f32[2,128,4096]{2,1,0:T(8,128)} %bitcast.145, f32[2,128,4096]{2,1,0:T(8,128)} %bitcast.146, f32[2,128,4096]{2,1,0:T(8,128)} %bitcast.147, f32[2,128,4096]{2,1,0:T(8,128)} %bitcast.148, ...), custom_call_target="tpu_custom_call" | custom-call | flops 1000 | bytes 1000 | tf_op jit(solution)/shard_map/first/pallas_call | solution.py:82
  22.4 3.3 %first.4 = (f32[3,32,1024]{2,1,0:T(8,128)}, f32[3,32,1024]{2,1,0:T(8,128)}, f32[3,32,1024]{2,1,0:T(8,128)}, f32[3,32,1024]{2,1,0:T(8,128)}) custom-call(s32[1]{0:T(128)} %bitcast.1.zr, f32[2,128,4096]{2,1,0:T(8,128)} %bitcast.149, f32[2,128,4096]{2,1,0:T(8,128)} %bitcast.150, f32[2,128,4096]{2,1,0:T(8,128)} %bitcast.151, f32[2,128,4096]{2,1,0:T(8,128)} %bitcast.152, ...), custom_call_target="tpu_custom_call" | custom-call | flops 1000 | bytes 1000 | tf_op jit(solution)/shard_map/first/pallas_call | solution.py:82
  25.8 0.5 broadcast_subtract_fusion
  26.4 0.6 compare_convert_fusion
  27.0 0.6 and_compare_fusion
  28.3 0.7 slice_bitcast_fusion.8
  29.2 0.6 select_reduce_fusion
  30.4 0.9 reshape.135
  31.7 0.8 constant_dynamic-slice_fusion.2
  32.9 1.4 select_reduce_fusion.2
  34.6 0.4 fusion.10
  35.4 0.4 fusion.8
  36.4 0.4 reshape.132
  37.5 0.9 reduce-precision_convert_fusion
  38.4 0.8 pad_maximum_fusion.2.w3
  39.2 0.7 pad_maximum_fusion.3.w0
  39.9 2.1 %collective-permute-start.8 = (f32[4,2,64,512]{3,2,1,0:T(8,128)}, f32[4,2,64,512]{3,2,1,0:T(8,128)S(1)}, u32[]{:S(2)}, u32[]{:S(2)}) collective-permute-start(f32[4,2,64,512]{3,2,1,0:T(8,128)} %get-tuple-element.186), channel_id=1, source_target_pairs={{0,64},{8,72},{16,80},{24,88},{32,96},{40,104},{48,112},{56,120},{... | collective-permute-start | bytes 3145736 | tf_op jit(solution)/shard_map/ppermute | solution.py:341
  42.0 0.8 pad_maximum_fusion.1.w2
  42.8 0.8 pad_maximum_fusion.w1
  43.6 8.5 %collective-permute-done.1.r2 = f32[3,32,2048]{2,1,0:T(8,128)} collective-permute-done((f32[3,32,2048]{2,1,0:T(8,128)}, f32[3,32,2048]{2,1,0:T(8,128)}, u32[]{:S(2)}, u32[]{:S(2)}) %collective-permute-start.1) | collective-permute-done | bytes 786464 | tf_op jit(solution)/shard_map/ppermute | solution.py:341
  52.1 1.1 collective-permute-start.3
  53.2 2.4 %collective-permute-start.4 = (f32[3,32,1024]{2,1,0:T(8,128)}, f32[3,32,1024]{2,1,0:T(8,128)}, u32[]{:S(2)}, u32[]{:S(2)}) collective-permute-start(f32[3,32,1024]{2,1,0:T(8,128)} %get-tuple-element.173), channel_id=1, source_target_pairs={{0,16},{8,24},{16,0},{24,8},{32,48},{40,56},{48,32},{56,40},{64,80... | collective-permute-start | bytes 1179656 | tf_op jit(solution)/shard_map/ppermute | solution.py:341
  55.6 1.3 collective-permute-start.5
  56.9 5.4 %early.3 = f32[4,4,8,2,16,128]{5,4,3,2,1,0:T(8,128)} custom-call(s32[1]{0:T(128)} %bitcast.1.zr, f32[3,32,2048]{2,1,0:T(8,128)} %get-tuple-element.165.r0, f32[3,32,2048]{2,1,0:T(8,128)} %collective-permute-done.r1, f32[3,32,2048]{2,1,0:T(8,128)} %collective-permute-done.1.r2, f32[3,32,2048]{2,1,0:T(8,128)} %collective-permute-done.2.r3, ...), custom_call_target="tpu_custom_call" | custom-call | flops 1000 | bytes 1000 | tf_op jit(solution)/shard_map/early/pallas_call | solution.py:158
  62.3 7.0 %all-to-all-start = ((f32[128,2,16,128]{3,2,1,0:T(8,128)}), f32[128,2,16,128]{3,2,1,0:T(8,128)S(1)}, u32[]{:S(2)}, u32[]{:S(2)}) async-start(f32[128,2,16,128]{3,2,1,0:T(8,128)} %bitcast.153), calls=%async_computation | async-start | bytes 4194304 | tf_op jit(solution)/shard_map/all_to_all | solution.py:396
  69.4 4.5 %collective-permute-done.4.r2 = f32[3,32,1024]{2,1,0:T(8,128)} collective-permute-done((f32[3,32,1024]{2,1,0:T(8,128)}, f32[3,32,1024]{2,1,0:T(8,128)}, u32[]{:S(2)}, u32[]{:S(2)}) %collective-permute-start.4) | collective-permute-done | bytes 393248 | tf_op jit(solution)/shard_map/ppermute | solution.py:341
  73.9 10.9 %collective-permute-done.5.r3 = f32[3,32,1024]{2,1,0:T(8,128)} collective-permute-done((f32[3,32,1024]{2,1,0:T(8,128)}, f32[3,32,1024]{2,1,0:T(8,128)}, u32[]{:S(2)}, u32[]{:S(2)}) %collective-permute-start.5) | collective-permute-done | bytes 393248 | tf_op jit(solution)/shard_map/ppermute | solution.py:341
  84.9 4.8 %collective-permute-start.11 = (f32[3,32,1024]{2,1,0:T(8,128)}, f32[3,32,1024]{2,1,0:T(8,128)}, u32[]{:S(2)}, u32[]{:S(2)}) collective-permute-start(f32[3,32,1024]{2,1,0:T(8,128)} %get-tuple-element.202), channel_id=1, source_target_pairs={{0,24},{8,0},{16,8},{24,16},{32,56},{40,32},{48,40},{56,48},{64,88... | collective-permute-start | bytes 1179656 | tf_op jit(solution)/shard_map/ppermute | solution.py:341
  89.7 0.9 collective-permute-start.9
  90.6 4.2 %early.4 = f32[4,4,8,1,16,128]{5,4,3,2,1,0:T(8,128)} custom-call(s32[1]{0:T(128)} %bitcast.1.zr, f32[3,32,1024]{2,1,0:T(8,128)} %get-tuple-element.187.r0, f32[3,32,1024]{2,1,0:T(8,128)} %collective-permute-done.3.r1, f32[3,32,1024]{2,1,0:T(8,128)} %collective-permute-done.4.r2, f32[3,32,1024]{2,1,0:T(8,128)} %collective-permute-done.5.r3, ...), custom_call_target="tpu_custom_call" | custom-call | flops 40000000000 | bytes 1000 | tf_op jit(solution)/shard_map/early/pallas_call | solution.py:158
  94.8 5.4 %all-to-all-done = f32[128,2,16,128]{3,2,1,0:T(8,128)S(1)} async-done(((f32[128,2,16,128]{3,2,1,0:T(8,128)}), f32[128,2,16,128]{3,2,1,0:T(8,128)S(1)}, u32[]{:S(2)}, u32[]{:S(2)}) %all-to-all-start) | async-done | bytes 2097184 | tf_op jit(solution)/shard_map/all_to_all | solution.py:396
  100.1 10.5 %all-to-all-start.1 = ((f32[128,1,16,128]{3,2,1,0:T(8,128)}), f32[128,1,16,128]{3,2,1,0:T(8,128)S(1)}, u32[]{:S(2)}, u32[]{:S(2)}) async-start(f32[128,1,16,128]{3,2,1,0:T(8,128)} %bitcast.157), calls=%async_computation.1 | async-start | bytes 2097152 | tf_op jit(solution)/shard_map/all_to_all | solution.py:396
  110.7 6.9 %late.3 = (f32[2,2,64,512]{3,2,1,0:T(8,128)}, f32[2,2,64,512]{3,2,1,0:T(8,128)}, f32[2,2,64,512]{3,2,1,0:T(8,128)}, f32[2,2,64,512]{3,2,1,0:T(8,128)}) custom-call(s32[1]{0:T(128)} %bitcast.yr, f32[4,4,8,2,16,128]{5,4,3,2,1,0:T(8,128)} %bitcast.155, f32[4,2,64,512]{3,2,1,0:T(8,128)} %get-tuple-element.192.a0, f32[4,2,64,512]{3,2,1,0:T(8,128)} %copy-done.3, ...), custom_call_target="tpu_custom_call" | custom-call | flops 8000000000 | bytes 1000 | tf_op jit(solution)/shard_map/late/pallas_call | solution.py:204
  117.6 1.0 collective-permute-start.12
  118.5 2.7 %collective-permute-start.13 = (f32[2,2,64,512]{3,2,1,0:T(8,128)}, f32[2,2,64,512]{3,2,1,0:T(8,128)S(1)}, u32[]{:S(2)}, u32[]{:S(2)}) collective-permute-start(f32[2,2,64,512]{3,2,1,0:T(8,128)} %get-tuple-element.205), channel_id=1, source_target_pairs={{0,64},{8,72},{16,80},{24,88},{32,96},{40,104},{48,112},{56,120},{... | collective-permute-start | bytes 1572872 | tf_op jit(solution)/shard_map/ppermute | solution.py:341
  121.3 1.4 collective-permute-start.14
  122.7 3.8 %early.5 = f32[4,4,8,1,16,128]{5,4,3,2,1,0:T(8,128)} custom-call(s32[1]{0:T(128)} %bitcast.1.zr, f32[3,32,1024]{2,1,0:T(8,128)} %get-tuple-element.208.r0, f32[3,32,1024]{2,1,0:T(8,128)} %collective-permute-done.9.r1, f32[3,32,1024]{2,1,0:T(8,128)} %collective-permute-done.10.r2, f32[3,32,1024]{2,1,0:T(8,128)} %collective-permute-done.11.r3, ...), custom_call_target="tpu_custom_call" | custom-call | flops 3000000000 | bytes 1000 | tf_op jit(solution)/shard_map/early/pallas_call | solution.py:158
  126.5 3.3 %all-to-all-done.1 = f32[128,1,16,128]{3,2,1,0:T(8,128)S(1)} async-done(((f32[128,1,16,128]{3,2,1,0:T(8,128)}), f32[128,1,16,128]{3,2,1,0:T(8,128)S(1)}, u32[]{:S(2)}, u32[]{:S(2)}) %all-to-all-start.1) | async-done | bytes 1048608 | tf_op jit(solution)/shard_map/all_to_all | solution.py:396
  129.8 5.9 %all-to-all-start.2 = ((f32[128,1,16,128]{3,2,1,0:T(8,128)}), f32[128,1,16,128]{3,2,1,0:T(8,128)S(1)}, u32[]{:S(2)}, u32[]{:S(2)}) async-start(f32[128,1,16,128]{3,2,1,0:T(8,128)} %bitcast.158), calls=%async_computation.2 | async-start | bytes 2097152 | tf_op jit(solution)/shard_map/all_to_all | solution.py:396
  135.7 0.4 collective-permute-done.12.refs_1_
  136.2 20.4 %collective-permute-done.13.refs_2_ = f32[2,2,64,512]{3,2,1,0:T(8,128)S(1)} collective-permute-done((f32[2,2,64,512]{3,2,1,0:T(8,128)}, f32[2,2,64,512]{3,2,1,0:T(8,128)S(1)}, u32[]{:S(2)}, u32[]{:S(2)}) %collective-permute-start.13) | collective-permute-done | bytes 524320 | tf_op jit(solution)/shard_map/ppermute | solution.py:341
  156.5 4.6 %late.4 = (f32[1,2,64,512]{3,2,1,0:T(8,128)}, f32[1,2,64,512]{3,2,1,0:T(8,128)}, f32[1,2,64,512]{3,2,1,0:T(8,128)}, f32[1,2,64,512]{3,2,1,0:T(8,128)}) custom-call(s32[1]{0:T(128)} %bitcast.yr, f32[4,4,8,1,16,128]{5,4,3,2,1,0:T(8,128)} %bitcast.156, f32[4,2,64,512]{3,2,1,0:T(8,128)} %get-tuple-element.192.a0, f32[4,2,64,512]{3,2,1,0:T(8,128)} %copy-done.3, ...), custom_call_target="tpu_custom_call" | custom-call | flops 7000000000 | bytes 1000 | tf_op jit(solution)/shard_map/late/pallas_call | solution.py:204
  161.2 0.4 collective-permute-start.15
  161.6 2.0 %collective-permute-start.16 = (f32[1,2,64,512]{3,2,1,0:T(8,128)}, f32[1,2,64,512]{3,2,1,0:T(8,128)S(1)}, u32[]{:S(2)}, u32[]{:S(2)}) collective-permute-start(f32[1,2,64,512]{3,2,1,0:T(8,128)} %get-tuple-element.223), channel_id=1, source_target_pairs={{0,64},{8,72},{16,80},{24,88},{32,96},{40,104},{48,112},{56,120},{... | collective-permute-start | bytes 786440 | tf_op jit(solution)/shard_map/ppermute | solution.py:341
  163.6 1.8 collective-permute-start.17
  165.3 10.8 %collective-permute-done.15.refs_1_ = f32[1,2,64,512]{3,2,1,0:T(8,128)S(1)} collective-permute-done((f32[1,2,64,512]{3,2,1,0:T(8,128)}, f32[1,2,64,512]{3,2,1,0:T(8,128)S(1)}, u32[]{:S(2)}, u32[]{:S(2)}) %collective-permute-start.15) | collective-permute-done | bytes 262176 | tf_op jit(solution)/shard_map/ppermute | solution.py:341
  176.2 1.0 copy-done
  177.2 4.4 %late.5 = (f32[1,2,64,512]{3,2,1,0:T(8,128)}, f32[1,2,64,512]{3,2,1,0:T(8,128)}, f32[1,2,64,512]{3,2,1,0:T(8,128)}, f32[1,2,64,512]{3,2,1,0:T(8,128)}) custom-call(s32[1]{0:T(128)} %bitcast.yr, f32[4,4,8,1,16,128]{5,4,3,2,1,0:T(8,128)} %bitcast.154, f32[4,2,64,512]{3,2,1,0:T(8,128)} %get-tuple-element.192.a0, f32[4,2,64,512]{3,2,1,0:T(8,128)} %copy-done.3, ...), custom_call_target="tpu_custom_call" | custom-call | flops 1000 | bytes 1000 | tf_op jit(solution)/shard_map/late/pallas_call | solution.py:204
  181.6 1.1 collective-permute-start.19
  182.8 2.1 %collective-permute-start.20 = (f32[1,2,64,512]{3,2,1,0:T(8,128)}, f32[1,2,64,512]{3,2,1,0:T(8,128)S(1)}, u32[]{:S(2)}, u32[]{:S(2)}) collective-permute-start(f32[1,2,64,512]{3,2,1,0:T(8,128)} %get-tuple-element.230), channel_id=1, source_target_pairs={{0,96},{8,104},{16,112},{24,120},{32,0},{40,8},{48,16},{56,24},{64... | collective-permute-start | bytes 786440 | tf_op jit(solution)/shard_map/ppermute | solution.py:341
  184.8 3.2 %last.3.refs_4_ = f32[2,128,4096]{2,1,0:T(8,128)} custom-call(s32[1]{0:T(128)} %bitcast.yr, f32[2,2,64,512]{3,2,1,0:T(8,128)} %get-tuple-element.235.refs_0_, f32[2,2,64,512]{3,2,1,0:T(8,128)} %copy-done.6, f32[2,2,64,512]{3,2,1,0:T(8,128)} %copy-done.7, f32[2,2,64,512]{3,2,1,0:T(8,128)} %collective-permute-done.14.refs_3_), custom_call_target="tpu_custom_call" | custom-call | flops 1000 | bytes 1000 | tf_op jit(solution)/shard_map/last/pallas_call | solution.py:253
  188.2 0.7 copy-done.10
  188.9 2.4 %last.4.refs_4_ = f32[2,128,4096]{2,1,0:T(8,128)} custom-call(s32[1]{0:T(128)} %bitcast.yr, f32[1,2,64,512]{3,2,1,0:T(8,128)} %get-tuple-element.231.refs_0_, f32[1,2,64,512]{3,2,1,0:T(8,128)} %copy-done.9, f32[1,2,64,512]{3,2,1,0:T(8,128)} %copy-done.10, f32[1,2,64,512]{3,2,1,0:T(8,128)} %copy-done.11, ...), custom_call_target="tpu_custom_call", output_to_operand_aliasing={{}: (5, {})} | custom-call | flops 1000 | bytes 1000 | tf_op jit(solution)/shard_map/last/pallas_call | solution.py:253
  191.4 0.8 collective-permute-done.18.refs_1_
  192.2 0.9 collective-permute-done.20.refs_3_
  193.1 0.7 copy-done.14
  193.8 2.4 %last.5 = f32[2,128,4096]{2,1,0:T(8,128)} custom-call(s32[1]{0:T(128)} %bitcast.yr, f32[1,2,64,512]{3,2,1,0:T(8,128)} %get-tuple-element.227.refs_0_, f32[1,2,64,512]{3,2,1,0:T(8,128)} %copy-done.12, f32[1,2,64,512]{3,2,1,0:T(8,128)} %copy-done.13, f32[1,2,64,512]{3,2,1,0:T(8,128)} %copy-done.14, ...), custom_call_target="tpu_custom_call", output_to_operand_aliasing={{}: (5, {})} | custom-call | flops 1000 | bytes 1000 | tf_op jit(solution)/shard_map/last/pallas_call | solution.py:253
  (105 shorter events, 4.3 us)
Async XLA Ops:
  9.3 30.6 %collective-permute-start.6 = (f32[4,2,64,512]{3,2,1,0:T(8,128)}, f32[4,2,64,512]{3,2,1,0:T(8,128)S(1)}, u32[]{:S(2)}, u32[]{:S(2)}) collective-permute-start(f32[4,2,64,512]{3,2,1,0:T(8,128)} %get-tuple-element.183), channel_id=1, source_target_pairs={{0,32},{8,40},{16,48},{24,56},{32,64},{40,72},{48,80},{56,88},{64,... | collective-permute-start | bytes 3145736 | tf_op jit(solution)/shard_map/ppermute | solution.py:341
  11.0 29.0 %collective-permute-start.7 = (f32[4,2,64,512]{3,2,1,0:T(8,128)}, f32[4,2,64,512]{3,2,1,0:T(8,128)S(1)}, u32[]{:S(2)}, u32[]{:S(2)}) collective-permute-start(f32[4,2,64,512]{3,2,1,0:T(8,128)} %get-tuple-element.185), channel_id=1, source_target_pairs={{0,96},{8,104},{16,112},{24,120},{32,0},{40,8},{48,16},{56,24},{64... | collective-permute-start | bytes 3145736 | tf_op jit(solution)/shard_map/ppermute | solution.py:341
  12.5 31.0 %collective-permute-start = (f32[3,32,2048]{2,1,0:T(8,128)}, f32[3,32,2048]{2,1,0:T(8,128)}, u32[]{:S(2)}, u32[]{:S(2)}) collective-permute-start(f32[3,32,2048]{2,1,0:T(8,128)} %get-tuple-element.127), channel_id=1, source_target_pairs={{0,8},{8,16},{16,24},{24,0},{32,40},{40,48},{48,56},{56,32},{64,72... | collective-permute-start | bytes 2359304 | tf_op jit(solution)/shard_map/ppermute | solution.py:341
  14.5 37.5 %collective-permute-start.1 = (f32[3,32,2048]{2,1,0:T(8,128)}, f32[3,32,2048]{2,1,0:T(8,128)}, u32[]{:S(2)}, u32[]{:S(2)}) collective-permute-start(f32[3,32,2048]{2,1,0:T(8,128)} %get-tuple-element.128), channel_id=1, source_target_pairs={{0,16},{8,24},{16,0},{24,8},{32,48},{40,56},{48,32},{56,40},{64,80... | collective-permute-start | bytes 2359304 | tf_op jit(solution)/shard_map/ppermute | solution.py:341
  18.1 33.9 %collective-permute-start.2 = (f32[3,32,2048]{2,1,0:T(8,128)}, f32[3,32,2048]{2,1,0:T(8,128)}, u32[]{:S(2)}, u32[]{:S(2)}) collective-permute-start(f32[3,32,2048]{2,1,0:T(8,128)} %get-tuple-element.129), channel_id=1, source_target_pairs={{0,24},{8,0},{16,8},{24,16},{32,56},{40,32},{48,40},{56,48},{64,88... | collective-permute-start | bytes 2359304 | tf_op jit(solution)/shard_map/ppermute | solution.py:341
  22.4 5.1 %copy-start.19 = (s32[4,128]{1,0:T(4,128)S(1)}, s32[4,128]{1,0:T(4,128)}, u32[]{:S(2)}) copy-start(s32[4,128]{1,0:T(4,128)} %param.9) | copy-start | bytes 6148
  22.4 5.9 %copy-start.8 = (f32[4,4,2,2,16,16]{5,4,3,2,1,0:T(8,128)S(1)}, f32[4,4,2,2,16,16]{5,4,3,2,1,0:T(8,128)}, u32[]{:S(2)}) copy-start(f32[4,4,2,2,16,16]{5,4,3,2,1,0:T(8,128)} %param.7) | copy-start | bytes 196612
  25.8 4.6 %copy-start.21 = (pred[4]{0:T(512)(128)(4,1)}, pred[4]{0:T(512)(128)(4,1)S(1)}, u32[]{:S(2)}) copy-start(pred[4]{0:T(512)(128)(4,1)S(1)} %and_compare_fusion.2) | copy-start | bytes 16
  27.6 0.6 copy-start.15
  29.8 1.8 copy-start.16
  30.4 4.0 %copy-start.22 = (pred[4]{0:T(512)(128)(4,1)S(1)}, pred[4]{0:T(512)(128)(4,1)}, u32[]{:S(2)}) copy-start(pred[4]{0:T(512)(128)(4,1)} %copy-done.21) | copy-start | bytes 16
  31.6 4.4 %copy-start.17 = (f32[2,2]{1,0:T(2,128)S(1)}, f32[2,2]{1,0:T(2,128)}, u32[]{:S(2)}) copy-start(f32[2,2]{1,0:T(2,128)} %compare_convert_fusion) | copy-start | bytes 52
  31.6 4.4 %copy-start.18 = (f32[2,2]{1,0:T(2,128)S(1)}, f32[2,2]{1,0:T(2,128)}, u32[]{:S(2)}) copy-start(f32[2,2]{1,0:T(2,128)} %broadcast_subtract_fusion) | copy-start | bytes 52
  35.1 1.8 copy-start.20
  39.9 22.4 %copy-start.3 = (f32[4,2,64,512]{3,2,1,0:T(8,128)}, f32[4,2,64,512]{3,2,1,0:T(8,128)S(1)}, u32[]{:S(2)}) copy-start(f32[4,2,64,512]{3,2,1,0:T(8,128)S(1)} %collective-permute-done.6.a1) | copy-start | bytes 3145732
  39.9 22.4 %copy-start.4 = (f32[4,2,64,512]{3,2,1,0:T(8,128)}, f32[4,2,64,512]{3,2,1,0:T(8,128)S(1)}, u32[]{:S(2)}) copy-start(f32[4,2,64,512]{3,2,1,0:T(8,128)S(1)} %collective-permute-done.7.a3) | copy-start | bytes 3145732
  39.9 50.6 %collective-permute-start.8 = (f32[4,2,64,512]{3,2,1,0:T(8,128)}, f32[4,2,64,512]{3,2,1,0:T(8,128)S(1)}, u32[]{:S(2)}, u32[]{:S(2)}) collective-permute-start(f32[4,2,64,512]{3,2,1,0:T(8,128)} %get-tuple-element.186), channel_id=1, source_target_pairs={{0,64},{8,72},{16,80},{24,88},{32,96},{40,104},{48,112},{56,120},{... | collective-permute-start | bytes 3145736 | tf_op jit(solution)/shard_map/ppermute | solution.py:341
  52.1 17.3 %collective-permute-start.3 = (f32[3,32,1024]{2,1,0:T(8,128)}, f32[3,32,1024]{2,1,0:T(8,128)}, u32[]{:S(2)}, u32[]{:S(2)}) collective-permute-start(f32[3,32,1024]{2,1,0:T(8,128)} %get-tuple-element.172), channel_id=1, source_target_pairs={{0,8},{8,16},{16,24},{24,0},{32,40},{40,48},{48,56},{56,32},{64,72... | collective-permute-start | bytes 1179656 | tf_op jit(solution)/shard_map/ppermute | solution.py:341
  53.2 20.7 %collective-permute-start.4 = (f32[3,32,1024]{2,1,0:T(8,128)}, f32[3,32,1024]{2,1,0:T(8,128)}, u32[]{:S(2)}, u32[]{:S(2)}) collective-permute-start(f32[3,32,1024]{2,1,0:T(8,128)} %get-tuple-element.173), channel_id=1, source_target_pairs={{0,16},{8,24},{16,0},{24,8},{32,48},{40,56},{48,32},{56,40},{64,80... | collective-permute-start | bytes 1179656 | tf_op jit(solution)/shard_map/ppermute | solution.py:341
  55.6 29.3 %collective-permute-start.5 = (f32[3,32,1024]{2,1,0:T(8,128)}, f32[3,32,1024]{2,1,0:T(8,128)}, u32[]{:S(2)}, u32[]{:S(2)}) collective-permute-start(f32[3,32,1024]{2,1,0:T(8,128)} %get-tuple-element.174), channel_id=1, source_target_pairs={{0,24},{8,0},{16,8},{24,16},{32,56},{40,32},{48,40},{56,48},{64,88... | collective-permute-start | bytes 1179656 | tf_op jit(solution)/shard_map/ppermute | solution.py:341
  62.3 27.4 %copy-start.23 = (f32[3,32,1024]{2,1,0:T(8,128)S(1)}, f32[3,32,1024]{2,1,0:T(8,128)}, u32[]{:S(2)}) copy-start(f32[3,32,1024]{2,1,0:T(8,128)} %get-tuple-element.200) | copy-start | bytes 1179652
  62.3 37.8 %all-to-all-start = ((f32[128,2,16,128]{3,2,1,0:T(8,128)}), f32[128,2,16,128]{3,2,1,0:T(8,128)S(1)}, u32[]{:S(2)}, u32[]{:S(2)}) async-start(f32[128,2,16,128]{3,2,1,0:T(8,128)} %bitcast.153), calls=%async_computation | async-start | bytes 4194304 | tf_op jit(solution)/shard_map/all_to_all | solution.py:396
  84.9 36.4 %collective-permute-start.10 = (f32[3,32,1024]{2,1,0:T(8,128)}, f32[3,32,1024]{2,1,0:T(8,128)}, u32[]{:S(2)}, u32[]{:S(2)}) collective-permute-start(f32[3,32,1024]{2,1,0:T(8,128)} %get-tuple-element.201), channel_id=1, source_target_pairs={{0,16},{8,24},{16,0},{24,8},{32,48},{40,56},{48,32},{56,40},{64,80... | collective-permute-start | bytes 1179656 | tf_op jit(solution)/shard_map/ppermute | solution.py:341
  84.9 37.8 %collective-permute-start.11 = (f32[3,32,1024]{2,1,0:T(8,128)}, f32[3,32,1024]{2,1,0:T(8,128)}, u32[]{:S(2)}, u32[]{:S(2)}) collective-permute-start(f32[3,32,1024]{2,1,0:T(8,128)} %get-tuple-element.202), channel_id=1, source_target_pairs={{0,24},{8,0},{16,8},{24,16},{32,56},{40,32},{48,40},{56,48},{64,88... | collective-permute-start | bytes 1179656 | tf_op jit(solution)/shard_map/ppermute | solution.py:341
  89.7 33.0 %collective-permute-start.9 = (f32[3,32,1024]{2,1,0:T(8,128)S(1)}, f32[3,32,1024]{2,1,0:T(8,128)}, u32[]{:S(2)}, u32[]{:S(2)}) collective-permute-start(f32[3,32,1024]{2,1,0:T(8,128)S(1)} %copy-done.23), channel_id=1, source_target_pairs={{0,8},{8,16},{16,24},{24,0},{32,40},{40,48},{48,56},{56,32},{64,72... | collective-permute-start | bytes 1179656 | tf_op jit(solution)/shard_map/ppermute | solution.py:341
  90.6 4.2 %copy-start.5 = (f32[4,2,64,512]{3,2,1,0:T(8,128)}, f32[4,2,64,512]{3,2,1,0:T(8,128)S(1)}, u32[]{:S(2)}) copy-start(f32[4,2,64,512]{3,2,1,0:T(8,128)S(1)} %collective-permute-done.8.a2) | copy-start | bytes 3145732
  100.1 10.5 %copy-start.1 = (f32[128,2,16,128]{3,2,1,0:T(8,128)}, f32[128,2,16,128]{3,2,1,0:T(8,128)S(1)}, u32[]{:S(2)}) copy-start(f32[128,2,16,128]{3,2,1,0:T(8,128)S(1)} %all-to-all-done) | copy-start | bytes 6291460
  100.1 29.7 %all-to-all-start.1 = ((f32[128,1,16,128]{3,2,1,0:T(8,128)}), f32[128,1,16,128]{3,2,1,0:T(8,128)S(1)}, u32[]{:S(2)}, u32[]{:S(2)}) async-start(f32[128,1,16,128]{3,2,1,0:T(8,128)} %bitcast.157), calls=%async_computation.1 | async-start | bytes 2097152 | tf_op jit(solution)/shard_map/all_to_all | solution.py:396
  117.6 18.6 %collective-permute-start.12 = (f32[2,2,64,512]{3,2,1,0:T(8,128)}, f32[2,2,64,512]{3,2,1,0:T(8,128)S(1)}, u32[]{:S(2)}, u32[]{:S(2)}) collective-permute-start(f32[2,2,64,512]{3,2,1,0:T(8,128)} %get-tuple-element.204), channel_id=1, source_target_pairs={{0,32},{8,40},{16,48},{24,56},{32,64},{40,72},{48,80},{56,88},{64,... | collective-permute-start | bytes 1572872 | tf_op jit(solution)/shard_map/ppermute | solution.py:341
  118.5 38.0 %collective-permute-start.13 = (f32[2,2,64,512]{3,2,1,0:T(8,128)}, f32[2,2,64,512]{3,2,1,0:T(8,128)S(1)}, u32[]{:S(2)}, u32[]{:S(2)}) collective-permute-start(f32[2,2,64,512]{3,2,1,0:T(8,128)} %get-tuple-element.205), channel_id=1, source_target_pairs={{0,64},{8,72},{16,80},{24,88},{32,96},{40,104},{48,112},{56,120},{... | collective-permute-start | bytes 1572872 | tf_op jit(solution)/shard_map/ppermute | solution.py:341
  121.3 35.3 %collective-permute-start.14 = (f32[2,2,64,512]{3,2,1,0:T(8,128)}, f32[2,2,64,512]{3,2,1,0:T(8,128)}, u32[]{:S(2)}, u32[]{:S(2)}) collective-permute-start(f32[2,2,64,512]{3,2,1,0:T(8,128)} %get-tuple-element.206), channel_id=1, source_target_pairs={{0,96},{8,104},{16,112},{24,120},{32,0},{40,8},{48,16},{56,24},{64... | collective-permute-start | bytes 1572872 | tf_op jit(solution)/shard_map/ppermute | solution.py:341
  129.8 26.7 %copy-start.2 = (f32[128,1,16,128]{3,2,1,0:T(8,128)}, f32[128,1,16,128]{3,2,1,0:T(8,128)S(1)}, u32[]{:S(2)}) copy-start(f32[128,1,16,128]{3,2,1,0:T(8,128)S(1)} %all-to-all-done.1) | copy-start | bytes 3145732
  129.8 46.3 %all-to-all-start.2 = ((f32[128,1,16,128]{3,2,1,0:T(8,128)}), f32[128,1,16,128]{3,2,1,0:T(8,128)S(1)}, u32[]{:S(2)}, u32[]{:S(2)}) async-start(f32[128,1,16,128]{3,2,1,0:T(8,128)} %bitcast.158), calls=%async_computation.2 | async-start | bytes 2097152 | tf_op jit(solution)/shard_map/all_to_all | solution.py:396
  136.2 25.0 %copy-start.6 = (f32[2,2,64,512]{3,2,1,0:T(8,128)}, f32[2,2,64,512]{3,2,1,0:T(8,128)S(1)}, u32[]{:S(2)}) copy-start(f32[2,2,64,512]{3,2,1,0:T(8,128)S(1)} %collective-permute-done.12.refs_1_) | copy-start | bytes 1572868
  156.5 4.6 %copy-start.7 = (f32[2,2,64,512]{3,2,1,0:T(8,128)}, f32[2,2,64,512]{3,2,1,0:T(8,128)S(1)}, u32[]{:S(2)}) copy-start(f32[2,2,64,512]{3,2,1,0:T(8,128)S(1)} %collective-permute-done.13.refs_2_) | copy-start | bytes 1572868
  161.2 15.0 %collective-permute-start.15 = (f32[1,2,64,512]{3,2,1,0:T(8,128)}, f32[1,2,64,512]{3,2,1,0:T(8,128)S(1)}, u32[]{:S(2)}, u32[]{:S(2)}) collective-permute-start(f32[1,2,64,512]{3,2,1,0:T(8,128)} %get-tuple-element.220), channel_id=1, source_target_pairs={{0,32},{8,40},{16,48},{24,56},{32,64},{40,72},{48,80},{56,88},{64,... | collective-permute-start | bytes 786440 | tf_op jit(solution)/shard_map/ppermute | solution.py:341
  161.6 26.5 %collective-permute-start.16 = (f32[1,2,64,512]{3,2,1,0:T(8,128)}, f32[1,2,64,512]{3,2,1,0:T(8,128)S(1)}, u32[]{:S(2)}, u32[]{:S(2)}) collective-permute-start(f32[1,2,64,512]{3,2,1,0:T(8,128)} %get-tuple-element.223), channel_id=1, source_target_pairs={{0,64},{8,72},{16,80},{24,88},{32,96},{40,104},{48,112},{56,120},{... | collective-permute-start | bytes 786440 | tf_op jit(solution)/shard_map/ppermute | solution.py:341
  163.6 24.6 %collective-permute-start.17 = (f32[1,2,64,512]{3,2,1,0:T(8,128)}, f32[1,2,64,512]{3,2,1,0:T(8,128)S(1)}, u32[]{:S(2)}, u32[]{:S(2)}) collective-permute-start(f32[1,2,64,512]{3,2,1,0:T(8,128)} %get-tuple-element.224), channel_id=1, source_target_pairs={{0,96},{8,104},{16,112},{24,120},{32,0},{40,8},{48,16},{56,24},{64... | collective-permute-start | bytes 786440 | tf_op jit(solution)/shard_map/ppermute | solution.py:341
  176.1 12.0 %copy-start.9 = (f32[1,2,64,512]{3,2,1,0:T(8,128)}, f32[1,2,64,512]{3,2,1,0:T(8,128)S(1)}, u32[]{:S(2)}) copy-start(f32[1,2,64,512]{3,2,1,0:T(8,128)S(1)} %collective-permute-done.15.refs_1_) | copy-start | bytes 786436
  176.2 1.0 copy-start
  181.6 10.6 %collective-permute-start.18 = (f32[1,2,64,512]{3,2,1,0:T(8,128)}, f32[1,2,64,512]{3,2,1,0:T(8,128)S(1)}, u32[]{:S(2)}, u32[]{:S(2)}) collective-permute-start(f32[1,2,64,512]{3,2,1,0:T(8,128)} %get-tuple-element.228), channel_id=1, source_target_pairs={{0,32},{8,40},{16,48},{24,56},{32,64},{40,72},{48,80},{56,88},{64,... | collective-permute-start | bytes 786440 | tf_op jit(solution)/shard_map/ppermute | solution.py:341
  181.6 10.6 %collective-permute-start.19 = (f32[1,2,64,512]{3,2,1,0:T(8,128)}, f32[1,2,64,512]{3,2,1,0:T(8,128)S(1)}, u32[]{:S(2)}, u32[]{:S(2)}) collective-permute-start(f32[1,2,64,512]{3,2,1,0:T(8,128)} %get-tuple-element.229), channel_id=1, source_target_pairs={{0,64},{8,72},{16,80},{24,88},{32,96},{40,104},{48,112},{56,120},{... | collective-permute-start | bytes 786440 | tf_op jit(solution)/shard_map/ppermute | solution.py:341
  182.8 10.4 %collective-permute-start.20 = (f32[1,2,64,512]{3,2,1,0:T(8,128)}, f32[1,2,64,512]{3,2,1,0:T(8,128)S(1)}, u32[]{:S(2)}, u32[]{:S(2)}) collective-permute-start(f32[1,2,64,512]{3,2,1,0:T(8,128)} %get-tuple-element.230), channel_id=1, source_target_pairs={{0,96},{8,104},{16,112},{24,120},{32,0},{40,8},{48,16},{56,24},{64... | collective-permute-start | bytes 786440 | tf_op jit(solution)/shard_map/ppermute | solution.py:341
  188.1 0.7 copy-start.10
  188.1 0.8 copy-start.11
  192.2 0.9 copy-start.12
  192.2 0.9 copy-start.13
  193.1 0.7 copy-start.14

commit v4 on v3

--- a/solution.py
+++ b/solution.py
@@ -247,7 +247,7 @@
         copy.wait()
 
 
-def last(chunk, y, parts, before):
+def last(chunk, y, parts, before, flops=1000):
     extra = [] if before is None else [before]
     count = chunk[1]
     return pl.pallas_call(
@@ -267,7 +267,7 @@
         out_shape=jax.ShapeDtypeStruct((2, PTS * BOX, FL), jnp.float32),
         input_output_aliases={Q + 1: 0} if extra else {},
         compiler_params=pltpu.CompilerParams(vmem_limit_bytes=VMEM),
-        cost_estimate=cost(),
+        cost_estimate=cost(flops),
         name="last",
     )(y, *parts, *extra)
 
@@ -372,13 +372,14 @@
     w0, w1, w2, w3 = weights(cheb_tables, switch_kernel, box_class, y, z)
     here[0], sent[1:], w0, w1, w2, w3 = tie((here[0], sent[1:], w0, w1, w2, w3))
 
+    result = [None]
+
     def do_late(k):
         if k:
-            if k + 1 < len(CHUNKS):
-                back[k - 1], moved[k] = tie((back[k - 1], moved[k]))
-            else:
-                back[k - 1][1], moved[k] = tie((back[k - 1][1], moved[k]))
-        done = late(CHUNKS[k], yr, moved[k], turns, w2, w3, (8_000_000_000, 7_000_000_000, 1000)[k])
+            if k + 1 == len(CHUNKS):
+                result[0] = last(CHUNKS[0], yr, back[0], None, 10_000_000_000)
+                result[0], back[k - 1][1], moved[k] = tie((result[0], back[k - 1][1], moved[k]))
+        done = late(CHUNKS[k], yr, moved[k], turns, w2, w3, (8_000_000_000, 1000, 1000)[k])
         back[k] = exchange(done, Q)
 
     for k, chunk in enumerate(CHUNKS):
@@ -400,12 +401,11 @@
             if k + 1 < count:
                 back[k - 1][0], here[k + 1] = tie((back[k - 1][0], here[k + 1]))
     do_late(count - 1)
-    result = None
-    for k, chunk in enumerate(CHUNKS):
+    for k in range(1, count):
         if k + 1 < count:
             back[k], back[k + 1][0] = tie((back[k], back[k + 1][0]))
-        result = last(chunk, yr, back[k], result)
-    return result.reshape(2, PTS, BOX, FL)
+        result[0] = last(CHUNKS[k], yr, back[k], result[0])
+    return result[0].reshape(2, PTS, BOX, FL)
 
 
 def solution(mesh):

time: 197 us -> 182 us (0.924)
  waiting for transfers between devices: 66 us -> 51.4 us
    ppermute x21, waiting for transfers between devices: 57.3 us -> 32.2 us  [swapped(): return lax.ppermute(part, 'space', [(i, target(i)) for i in range(count)])]
    all_to_all x3, waiting for transfers between devices: 8.66 us -> 19.2 us  [on_device(): lax.all_to_all(mixed[k].reshape(128, chunk[1], PTS, 128), ('space', 'freq...]
    all_to_all x3, starting transfers between devices: 23.5 us -> 25.5 us  [on_device(): lax.all_to_all(mixed[k].reshape(128, chunk[1], PTS, 128), ('space', 'freq...]
  transfers between devices with their start and end apart: 24 -> 24, of which waited for: 10 -> 9; matrix products, arithmetic and copies ran while one was open for 8% -> 7% of each run, Pallas kernels for 21% -> 25%
where the time goes in v4:
time: 182 us
  starting transfers between devices  60.3 us (33%)
  Pallas kernels  53.1 us (29%)
  waiting for transfers between devices  51.4 us (28%)
  other arithmetic  8.32 us (5%)
  local copies, waits for them, and re-layouts  7.05 us (4%)
    ppermute x21, starting transfers between devices, swapped(): return lax.ppermute(part, 'space', [(i, target(i)) for i in range(count)])  34.9 us
    ppermute x21, waiting for transfers between devices, swapped(): return lax.ppermute(part, 'space', [(i, target(i)) for i in range(count)])  32.2 us
    all_to_all x3, starting transfers between devices, on_device(): lax.all_to_all(mixed[k].reshape(128, chunk[1], PTS, 128), ('space', 'freq...  25.5 us
    all_to_all x3, waiting for transfers between devices, on_device(): lax.all_to_all(mixed[k].reshape(128, chunk[1], PTS, 128), ('space', 'freq...  19.2 us
    pallas_call x3, Pallas kernels, late(): pl.pallas_call(late_kernel, grid_spec=pltpu.PrefetchScalarGridSpec(num_sc...  15.6 us
    pallas_call x3, Pallas kernels, early(): pl.pallas_call(early_kernel, grid_spec=pltpu.PrefetchScalarGridSpec(num_s...  13.4 us
    pallas_call x3, Pallas kernels, first(): pl.pallas_call(functools.partial(first_kernel, n), grid_spec=pltpu.Prefet...  11.6 us
    pallas_call x3, Pallas kernels, last(): pl.pallas_call(functools.partial(last_kernel, chunk), grid_spec=pltpu.Pre...  8.11 us
  transfers between devices with their start and end apart: 24, of which 9 were waited for; matrix products, arithmetic and copies ran while one was open for 7% of the time, Pallas kernels for 25%

profile of v4, /device:TPU:0, one launch (start us, length us, event | category | flops | bytes accessed | tf_op | source)
XLA Modules:
  0.0 181.6 jit_solution(8512554682817340234)
XLA Ops:
  0.0 5.0 %first.3 = (f32[3,32,2048]{2,1,0:T(8,128)}, f32[3,32,2048]{2,1,0:T(8,128)}, f32[3,32,2048]{2,1,0:T(8,128)}, f32[3,32,2048]{2,1,0:T(8,128)}) custom-call(s32[1]{0:T(128)} %bitcast.1.zr, f32[2,128,4096]{2,1,0:T(8,128)} %bitcast.141, f32[2,128,4096]{2,1,0:T(8,128)} %bitcast.142, f32[2,128,4096]{2,1,0:T(8,128)} %bitcast.143, f32[2,128,4096]{2,1,0:T(8,128)} %bitcast.144, ...), custom_call_target="tpu_custom_call" | custom-call | flops 1000 | bytes 1000 | tf_op jit(solution)/shard_map/first/pallas_call | solution.py:82
  5.0 2.1 %collective-permute-start = (f32[3,32,2048]{2,1,0:T(8,128)}, f32[3,32,2048]{2,1,0:T(8,128)}, u32[]{:S(2)}, u32[]{:S(2)}) collective-permute-start(f32[3,32,2048]{2,1,0:T(8,128)} %get-tuple-element.118), channel_id=1, source_target_pairs={{0,8},{8,16},{16,24},{24,0},{32,40},{40,48},{48,56},{56,32},{64,72... | collective-permute-start | bytes 2359304 | tf_op jit(solution)/shard_map/ppermute | solution.py:341
  7.1 3.6 %collective-permute-start.1 = (f32[3,32,2048]{2,1,0:T(8,128)}, f32[3,32,2048]{2,1,0:T(8,128)}, u32[]{:S(2)}, u32[]{:S(2)}) collective-permute-start(f32[3,32,2048]{2,1,0:T(8,128)} %get-tuple-element.119), channel_id=1, source_target_pairs={{0,16},{8,24},{16,0},{24,8},{32,48},{40,56},{48,32},{56,40},{64,80... | collective-permute-start | bytes 2359304 | tf_op jit(solution)/shard_map/ppermute | solution.py:341
  10.6 1.0 collective-permute-start.2
  11.6 4.3 %share.1 = (f32[4,2,64,512]{3,2,1,0:T(8,128)}, f32[4,2,64,512]{3,2,1,0:T(8,128)}, f32[4,2,64,512]{3,2,1,0:T(8,128)}, f32[4,2,64,512]{3,2,1,0:T(8,128)}) custom-call(s32[1]{0:T(128)} %bitcast.yr, f32[4,128,4096]{2,1,0:T(8,128)} %bitcast.132), custom_call_target="tpu_custom_call" | custom-call | flops 1000 | bytes 1000 | tf_op jit(solution)/shard_map/share/pallas_call | solution.py:114
  16.0 1.6 collective-permute-start.6
  17.6 1.7 collective-permute-start.7
  19.3 3.3 %first.5 = (f32[3,32,1024]{2,1,0:T(8,128)}, f32[3,32,1024]{2,1,0:T(8,128)}, f32[3,32,1024]{2,1,0:T(8,128)}, f32[3,32,1024]{2,1,0:T(8,128)}) custom-call(s32[1]{0:T(128)} %bitcast.1.zr, f32[2,128,4096]{2,1,0:T(8,128)} %bitcast.145, f32[2,128,4096]{2,1,0:T(8,128)} %bitcast.146, f32[2,128,4096]{2,1,0:T(8,128)} %bitcast.147, f32[2,128,4096]{2,1,0:T(8,128)} %bitcast.148, ...), custom_call_target="tpu_custom_call" | custom-call | flops 1000 | bytes 1000 | tf_op jit(solution)/shard_map/first/pallas_call | solution.py:82
  22.6 3.3 %first.4 = (f32[3,32,1024]{2,1,0:T(8,128)}, f32[3,32,1024]{2,1,0:T(8,128)}, f32[3,32,1024]{2,1,0:T(8,128)}, f32[3,32,1024]{2,1,0:T(8,128)}) custom-call(s32[1]{0:T(128)} %bitcast.1.zr, f32[2,128,4096]{2,1,0:T(8,128)} %bitcast.149, f32[2,128,4096]{2,1,0:T(8,128)} %bitcast.150, f32[2,128,4096]{2,1,0:T(8,128)} %bitcast.151, f32[2,128,4096]{2,1,0:T(8,128)} %bitcast.152, ...), custom_call_target="tpu_custom_call" | custom-call | flops 1000 | bytes 1000 | tf_op jit(solution)/shard_map/first/pallas_call | solution.py:82
  27.3 0.3 select_reduce_fusion.2
  28.0 0.4 fusion.10
  28.6 0.4 fusion.8
  29.2 0.6 select_reduce_fusion
  30.0 0.4 add_bitcast_fusion.2
  30.4 0.8 fusion.6
  31.6 0.4 reshape.132
  32.0 0.9 reshape.129
  32.9 1.3 add_bitcast_fusion
  34.2 0.3 reshape.135
  34.4 0.3 reshape.134
  34.7 0.8 pad_maximum_fusion.w1
  35.5 0.9 reduce-precision_convert_fusion.3
  36.4 0.7 pad_maximum_fusion.3.w0
  37.1 4.4 %collective-permute-done.6.a1 = f32[4,2,64,512]{3,2,1,0:T(8,128)S(1)} collective-permute-done((f32[4,2,64,512]{3,2,1,0:T(8,128)}, f32[4,2,64,512]{3,2,1,0:T(8,128)S(1)}, u32[]{:S(2)}, u32[]{:S(2)}) %collective-permute-start.6) | collective-permute-done | bytes 1048608 | tf_op jit(solution)/shard_map/ppermute | solution.py:341
  41.5 2.9 %collective-permute-start.8 = (f32[4,2,64,512]{3,2,1,0:T(8,128)}, f32[4,2,64,512]{3,2,1,0:T(8,128)S(1)}, u32[]{:S(2)}, u32[]{:S(2)}) collective-permute-start(f32[4,2,64,512]{3,2,1,0:T(8,128)} %get-tuple-element.177), channel_id=1, source_target_pairs={{0,64},{8,72},{16,80},{24,88},{32,96},{40,104},{48,112},{56,120},{... | collective-permute-start | bytes 3145736 | tf_op jit(solution)/shard_map/ppermute | solution.py:341
  44.5 0.7 pad_maximum_fusion.2.w3
  45.3 0.8 pad_maximum_fusion.1.w2
  46.0 1.1 collective-permute-start.3
  47.1 1.6 collective-permute-start.4
  48.7 1.2 collective-permute-start.5
  49.9 5.4 %early.3 = f32[4,4,8,2,16,128]{5,4,3,2,1,0:T(8,128)} custom-call(s32[1]{0:T(128)} %bitcast.1.zr, f32[3,32,2048]{2,1,0:T(8,128)} %get-tuple-element.156.r0, f32[3,32,2048]{2,1,0:T(8,128)} %collective-permute-done.r1, f32[3,32,2048]{2,1,0:T(8,128)} %collective-permute-done.1.r2, f32[3,32,2048]{2,1,0:T(8,128)} %collective-permute-done.2.r3, ...), custom_call_target="tpu_custom_call" | custom-call | flops 1000 | bytes 1000 | tf_op jit(solution)/shard_map/early/pallas_call | solution.py:158
  55.4 8.9 %all-to-all-start = ((f32[128,2,16,128]{3,2,1,0:T(8,128)}), f32[128,2,16,128]{3,2,1,0:T(8,128)}, u32[]{:S(2)}, u32[]{:S(2)}) async-start(f32[128,2,16,128]{3,2,1,0:T(8,128)} %bitcast.153), calls=%async_computation | async-start | bytes 4194304 | tf_op jit(solution)/shard_map/all_to_all | solution.py:397
  64.2 2.2 %collective-permute-done.4.r2 = f32[3,32,1024]{2,1,0:T(8,128)} collective-permute-done((f32[3,32,1024]{2,1,0:T(8,128)}, f32[3,32,1024]{2,1,0:T(8,128)}, u32[]{:S(2)}, u32[]{:S(2)}) %collective-permute-start.4) | collective-permute-done | bytes 393248 | tf_op jit(solution)/shard_map/ppermute | solution.py:341
  66.4 0.8 collective-permute-start.9
  67.3 3.2 %collective-permute-start.10 = (f32[3,32,1024]{2,1,0:T(8,128)S(1)}, f32[3,32,1024]{2,1,0:T(8,128)}, u32[]{:S(2)}, u32[]{:S(2)}) collective-permute-start(f32[3,32,1024]{2,1,0:T(8,128)S(1)} %copy-done.17), channel_id=1, source_target_pairs={{0,16},{8,24},{16,0},{24,8},{32,48},{40,56},{48,32},{56,40},{64,80... | collective-permute-start | bytes 1179656 | tf_op jit(solution)/shard_map/ppermute | solution.py:341
  70.5 3.1 %collective-permute-done.8.a2 = f32[4,2,64,512]{3,2,1,0:T(8,128)S(1)} collective-permute-done((f32[4,2,64,512]{3,2,1,0:T(8,128)}, f32[4,2,64,512]{3,2,1,0:T(8,128)S(1)}, u32[]{:S(2)}, u32[]{:S(2)}) %collective-permute-start.8) | collective-permute-done | bytes 1048608 | tf_op jit(solution)/shard_map/ppermute | solution.py:341
  73.6 4.2 %early.4 = f32[4,4,8,1,16,128]{5,4,3,2,1,0:T(8,128)} custom-call(s32[1]{0:T(128)} %bitcast.1.zr, f32[3,32,1024]{2,1,0:T(8,128)} %get-tuple-element.178.r0, f32[3,32,1024]{2,1,0:T(8,128)} %collective-permute-done.3.r1, f32[3,32,1024]{2,1,0:T(8,128)} %collective-permute-done.4.r2, f32[3,32,1024]{2,1,0:T(8,128)} %collective-permute-done.5.r3, ...), custom_call_target="tpu_custom_call" | custom-call | flops 40000000000 | bytes 1000 | tf_op jit(solution)/shard_map/early/pallas_call | solution.py:158
  77.8 16.4 %all-to-all-done = f32[128,2,16,128]{3,2,1,0:T(8,128)} async-done(((f32[128,2,16,128]{3,2,1,0:T(8,128)}), f32[128,2,16,128]{3,2,1,0:T(8,128)}, u32[]{:S(2)}, u32[]{:S(2)}) %all-to-all-start) | async-done | bytes 2097184 | tf_op jit(solution)/shard_map/all_to_all | solution.py:397
  94.2 8.3 %all-to-all-start.1 = ((f32[128,1,16,128]{3,2,1,0:T(8,128)}), f32[128,1,16,128]{3,2,1,0:T(8,128)S(1)}, u32[]{:S(2)}, u32[]{:S(2)}) async-start(f32[128,1,16,128]{3,2,1,0:T(8,128)} %bitcast.157), calls=%async_computation.1 | async-start | bytes 2097152 | tf_op jit(solution)/shard_map/all_to_all | solution.py:397
  102.5 6.8 %late.3 = (f32[2,2,64,512]{3,2,1,0:T(8,128)}, f32[2,2,64,512]{3,2,1,0:T(8,128)}, f32[2,2,64,512]{3,2,1,0:T(8,128)}, f32[2,2,64,512]{3,2,1,0:T(8,128)}) custom-call(s32[1]{0:T(128)} %bitcast.yr, f32[4,4,8,2,16,128]{5,4,3,2,1,0:T(8,128)} %bitcast.55.x, f32[4,2,64,512]{3,2,1,0:T(8,128)} %get-tuple-element.184.a0, f32[4,2,64,512]{3,2,1,0:T(8,128)} %copy-done.2, ...), custom_call_target="tpu_custom_call" | custom-call | flops 8000000000 | bytes 1000 | tf_op jit(solution)/shard_map/late/pallas_call | solution.py:204
  109.3 1.0 collective-permute-start.12
  110.3 2.7 %collective-permute-start.13 = (f32[2,2,64,512]{3,2,1,0:T(8,128)}, f32[2,2,64,512]{3,2,1,0:T(8,128)S(1)}, u32[]{:S(2)}, u32[]{:S(2)}) collective-permute-start(f32[2,2,64,512]{3,2,1,0:T(8,128)} %get-tuple-element.203), channel_id=1, source_target_pairs={{0,64},{8,72},{16,80},{24,88},{32,96},{40,104},{48,112},{56,120},{... | collective-permute-start | bytes 1572872 | tf_op jit(solution)/shard_map/ppermute | solution.py:341
  113.0 2.0 %collective-permute-start.14 = (f32[2,2,64,512]{3,2,1,0:T(8,128)}, f32[2,2,64,512]{3,2,1,0:T(8,128)}, u32[]{:S(2)}, u32[]{:S(2)}) collective-permute-start(f32[2,2,64,512]{3,2,1,0:T(8,128)} %get-tuple-element.204), channel_id=1, source_target_pairs={{0,96},{8,104},{16,112},{24,120},{32,0},{40,8},{48,16},{56,24},{64... | collective-permute-start | bytes 1572872 | tf_op jit(solution)/shard_map/ppermute | solution.py:341
  115.0 3.8 %early.5 = f32[4,4,8,1,16,128]{5,4,3,2,1,0:T(8,128)} custom-call(s32[1]{0:T(128)} %bitcast.1.zr, f32[3,32,1024]{2,1,0:T(8,128)} %get-tuple-element.195.r0, f32[3,32,1024]{2,1,0:T(8,128)} %collective-permute-done.9.r1, f32[3,32,1024]{2,1,0:T(8,128)} %collective-permute-done.10.r2, f32[3,32,1024]{2,1,0:T(8,128)} %collective-permute-done.11.r3, ...), custom_call_target="tpu_custom_call" | custom-call | flops 3000000000 | bytes 1000 | tf_op jit(solution)/shard_map/early/pallas_call | solution.py:158
  118.9 2.8 %all-to-all-done.1 = f32[128,1,16,128]{3,2,1,0:T(8,128)S(1)} async-done(((f32[128,1,16,128]{3,2,1,0:T(8,128)}), f32[128,1,16,128]{3,2,1,0:T(8,128)S(1)}, u32[]{:S(2)}, u32[]{:S(2)}) %all-to-all-start.1) | async-done | bytes 1048608 | tf_op jit(solution)/shard_map/all_to_all | solution.py:397
  121.7 8.3 %all-to-all-start.2 = ((f32[128,1,16,128]{3,2,1,0:T(8,128)}), f32[128,1,16,128]{3,2,1,0:T(8,128)S(1)}, u32[]{:S(2)}, u32[]{:S(2)}) async-start(f32[128,1,16,128]{3,2,1,0:T(8,128)} %bitcast.156), calls=%async_computation.2 | async-start | bytes 2097152 | tf_op jit(solution)/shard_map/all_to_all | solution.py:397
  130.0 4.4 %late.4 = (f32[1,2,64,512]{3,2,1,0:T(8,128)}, f32[1,2,64,512]{3,2,1,0:T(8,128)}, f32[1,2,64,512]{3,2,1,0:T(8,128)}, f32[1,2,64,512]{3,2,1,0:T(8,128)}) custom-call(s32[1]{0:T(128)} %bitcast.yr, f32[4,4,8,1,16,128]{5,4,3,2,1,0:T(8,128)} %bitcast.155, f32[4,2,64,512]{3,2,1,0:T(8,128)} %get-tuple-element.184.a0, f32[4,2,64,512]{3,2,1,0:T(8,128)} %copy-done.2, ...), custom_call_target="tpu_custom_call" | custom-call | flops 1000 | bytes 1000 | tf_op jit(solution)/shard_map/late/pallas_call | solution.py:204
  134.4 1.0 collective-permute-start.15
  135.4 2.7 %collective-permute-start.16 = (f32[1,2,64,512]{3,2,1,0:T(8,128)}, f32[1,2,64,512]{3,2,1,0:T(8,128)S(1)}, u32[]{:S(2)}, u32[]{:S(2)}) collective-permute-start(f32[1,2,64,512]{3,2,1,0:T(8,128)} %get-tuple-element.208), channel_id=1, source_target_pairs={{0,64},{8,72},{16,80},{24,88},{32,96},{40,104},{48,112},{56,120},{... | collective-permute-start | bytes 786440 | tf_op jit(solution)/shard_map/ppermute | solution.py:341
  138.2 1.4 collective-permute-start.17
  139.6 8.8 %collective-permute-done.13.refs_2_ = f32[2,2,64,512]{3,2,1,0:T(8,128)S(1)} collective-permute-done((f32[2,2,64,512]{3,2,1,0:T(8,128)}, f32[2,2,64,512]{3,2,1,0:T(8,128)S(1)}, u32[]{:S(2)}, u32[]{:S(2)}) %collective-permute-start.13) | collective-permute-done | bytes 524320 | tf_op jit(solution)/shard_map/ppermute | solution.py:341
  148.4 0.8 copy-done.15
  149.2 3.2 %last.3.refs_4_ = f32[2,128,4096]{2,1,0:T(8,128)} custom-call(s32[1]{0:T(128)} %bitcast.yr, f32[2,2,64,512]{3,2,1,0:T(8,128)} %get-tuple-element.201.refs_0_, f32[2,2,64,512]{3,2,1,0:T(8,128)} %copy-done.14, f32[2,2,64,512]{3,2,1,0:T(8,128)} %copy-done.15, f32[2,2,64,512]{3,2,1,0:T(8,128)} %collective-permute-done.14.refs_3_), custom_call_target="tpu_custom_call" | custom-call | flops 10000000000 | bytes 1000 | tf_op jit(solution)/shard_map/last/pallas_call | solution.py:253
  152.5 4.2 %collective-permute-done.15.refs_1_ = f32[1,2,64,512]{3,2,1,0:T(8,128)S(1)} collective-permute-done((f32[1,2,64,512]{3,2,1,0:T(8,128)}, f32[1,2,64,512]{3,2,1,0:T(8,128)S(1)}, u32[]{:S(2)}, u32[]{:S(2)}) %collective-permute-start.15) | collective-permute-done | bytes 262176 | tf_op jit(solution)/shard_map/ppermute | solution.py:341
  156.7 1.1 copy-done
  157.8 4.4 %late.5 = (f32[1,2,64,512]{3,2,1,0:T(8,128)}, f32[1,2,64,512]{3,2,1,0:T(8,128)}, f32[1,2,64,512]{3,2,1,0:T(8,128)}, f32[1,2,64,512]{3,2,1,0:T(8,128)}) custom-call(s32[1]{0:T(128)} %bitcast.yr, f32[4,4,8,1,16,128]{5,4,3,2,1,0:T(8,128)} %bitcast.154, f32[4,2,64,512]{3,2,1,0:T(8,128)} %get-tuple-element.184.a0, f32[4,2,64,512]{3,2,1,0:T(8,128)} %copy-done.2, ...), custom_call_target="tpu_custom_call" | custom-call | flops 1000 | bytes 1000 | tf_op jit(solution)/shard_map/late/pallas_call | solution.py:204
  162.3 2.1 %collective-permute-start.19 = (f32[1,2,64,512]{3,2,1,0:T(8,128)}, f32[1,2,64,512]{3,2,1,0:T(8,128)S(1)}, u32[]{:S(2)}, u32[]{:S(2)}) collective-permute-start(f32[1,2,64,512]{3,2,1,0:T(8,128)} %get-tuple-element.214), channel_id=1, source_target_pairs={{0,64},{8,72},{16,80},{24,88},{32,96},{40,104},{48,112},{56,120},{... | collective-permute-start | bytes 786440 | tf_op jit(solution)/shard_map/ppermute | solution.py:341
  164.4 1.1 collective-permute-start.20
  165.5 0.7 copy-done.7
  166.3 2.4 %last.4.refs_4_ = f32[2,128,4096]{2,1,0:T(8,128)} custom-call(s32[1]{0:T(128)} %bitcast.yr, f32[1,2,64,512]{3,2,1,0:T(8,128)} %get-tuple-element.216.refs_0_, f32[1,2,64,512]{3,2,1,0:T(8,128)} %copy-done.6, f32[1,2,64,512]{3,2,1,0:T(8,128)} %copy-done.7, f32[1,2,64,512]{3,2,1,0:T(8,128)} %copy-done.8, ...), custom_call_target="tpu_custom_call", output_to_operand_aliasing={{}: (5, {})} | custom-call | flops 1000 | bytes 1000 | tf_op jit(solution)/shard_map/last/pallas_call | solution.py:253
  168.7 8.8 %collective-permute-done.18.refs_1_ = f32[1,2,64,512]{3,2,1,0:T(8,128)S(1)} collective-permute-done((f32[1,2,64,512]{3,2,1,0:T(8,128)}, f32[1,2,64,512]{3,2,1,0:T(8,128)S(1)}, u32[]{:S(2)}, u32[]{:S(2)}) %collective-permute-start.18) | collective-permute-done | bytes 262176 | tf_op jit(solution)/shard_map/ppermute | solution.py:341
  177.5 0.6 collective-permute-done.20.refs_3_
  178.3 0.7 copy-done.11
  179.0 2.4 %last.5 = f32[2,128,4096]{2,1,0:T(8,128)} custom-call(s32[1]{0:T(128)} %bitcast.yr, f32[1,2,64,512]{3,2,1,0:T(8,128)} %get-tuple-element.212.refs_0_, f32[1,2,64,512]{3,2,1,0:T(8,128)} %copy-done.9, f32[1,2,64,512]{3,2,1,0:T(8,128)} %copy-done.10, f32[1,2,64,512]{3,2,1,0:T(8,128)} %copy-done.11, ...), custom_call_target="tpu_custom_call", output_to_operand_aliasing={{}: (5, {})} | custom-call | flops 1000 | bytes 1000 | tf_op jit(solution)/shard_map/last/pallas_call | solution.py:253
  (95 shorter events, 3.1 us)
Async XLA Ops:
  5.0 41.0 %collective-permute-start = (f32[3,32,2048]{2,1,0:T(8,128)}, f32[3,32,2048]{2,1,0:T(8,128)}, u32[]{:S(2)}, u32[]{:S(2)}) collective-permute-start(f32[3,32,2048]{2,1,0:T(8,128)} %get-tuple-element.118), channel_id=1, source_target_pairs={{0,8},{8,16},{16,24},{24,0},{32,40},{40,48},{48,56},{56,32},{64,72... | collective-permute-start | bytes 2359304 | tf_op jit(solution)/shard_map/ppermute | solution.py:341
  7.1 39.0 %collective-permute-start.1 = (f32[3,32,2048]{2,1,0:T(8,128)}, f32[3,32,2048]{2,1,0:T(8,128)}, u32[]{:S(2)}, u32[]{:S(2)}) collective-permute-start(f32[3,32,2048]{2,1,0:T(8,128)} %get-tuple-element.119), channel_id=1, source_target_pairs={{0,16},{8,24},{16,0},{24,8},{32,48},{40,56},{48,32},{56,40},{64,80... | collective-permute-start | bytes 2359304 | tf_op jit(solution)/shard_map/ppermute | solution.py:341
  10.6 35.4 %collective-permute-start.2 = (f32[3,32,2048]{2,1,0:T(8,128)}, f32[3,32,2048]{2,1,0:T(8,128)}, u32[]{:S(2)}, u32[]{:S(2)}) collective-permute-start(f32[3,32,2048]{2,1,0:T(8,128)} %get-tuple-element.120), channel_id=1, source_target_pairs={{0,24},{8,0},{16,8},{24,16},{32,56},{40,32},{48,40},{56,48},{64,88... | collective-permute-start | bytes 2359304 | tf_op jit(solution)/shard_map/ppermute | solution.py:341
  16.0 25.6 %collective-permute-start.6 = (f32[4,2,64,512]{3,2,1,0:T(8,128)}, f32[4,2,64,512]{3,2,1,0:T(8,128)S(1)}, u32[]{:S(2)}, u32[]{:S(2)}) collective-permute-start(f32[4,2,64,512]{3,2,1,0:T(8,128)} %get-tuple-element.174), channel_id=1, source_target_pairs={{0,32},{8,40},{16,48},{24,56},{32,64},{40,72},{48,80},{56,88},{64,... | collective-permute-start | bytes 3145736 | tf_op jit(solution)/shard_map/ppermute | solution.py:341
  17.6 24.0 %collective-permute-start.7 = (f32[4,2,64,512]{3,2,1,0:T(8,128)}, f32[4,2,64,512]{3,2,1,0:T(8,128)S(1)}, u32[]{:S(2)}, u32[]{:S(2)}) collective-permute-start(f32[4,2,64,512]{3,2,1,0:T(8,128)} %get-tuple-element.176), channel_id=1, source_target_pairs={{0,96},{8,104},{16,112},{24,120},{32,0},{40,8},{48,16},{56,24},{64... | collective-permute-start | bytes 3145736 | tf_op jit(solution)/shard_map/ppermute | solution.py:341
  22.5 3.6 %copy-start.12 = (f32[2,16,16]{2,1,0:T(8,128)S(1)}, f32[2,16,16]{2,1,0:T(8,128)}, u32[]{:S(2)}) copy-start(f32[2,16,16]{2,1,0:T(8,128)} %param.8) | copy-start | bytes 6148
  22.6 3.6 %copy-start.13 = (s32[4,128]{1,0:T(4,128)S(1)}, s32[4,128]{1,0:T(4,128)}, u32[]{:S(2)}) copy-start(s32[4,128]{1,0:T(4,128)} %param.9) | copy-start | bytes 6148
  22.6 4.6 %copy-start.5 = (f32[4,4,2,2,16,16]{5,4,3,2,1,0:T(8,128)S(1)}, f32[4,4,2,2,16,16]{5,4,3,2,1,0:T(8,128)}, u32[]{:S(2)}) copy-start(f32[4,4,2,2,16,16]{5,4,3,2,1,0:T(8,128)} %param.7) | copy-start | bytes 196612
  41.5 13.8 %copy-start.2 = (f32[4,2,64,512]{3,2,1,0:T(8,128)}, f32[4,2,64,512]{3,2,1,0:T(8,128)S(1)}, u32[]{:S(2)}) copy-start(f32[4,2,64,512]{3,2,1,0:T(8,128)S(1)} %collective-permute-done.6.a1) | copy-start | bytes 3145732
  41.5 13.8 %copy-start.3 = (f32[4,2,64,512]{3,2,1,0:T(8,128)}, f32[4,2,64,512]{3,2,1,0:T(8,128)S(1)}, u32[]{:S(2)}) copy-start(f32[4,2,64,512]{3,2,1,0:T(8,128)S(1)} %collective-permute-done.7.a3) | copy-start | bytes 3145732
  41.5 32.1 %collective-permute-start.8 = (f32[4,2,64,512]{3,2,1,0:T(8,128)}, f32[4,2,64,512]{3,2,1,0:T(8,128)S(1)}, u32[]{:S(2)}, u32[]{:S(2)}) collective-permute-start(f32[4,2,64,512]{3,2,1,0:T(8,128)} %get-tuple-element.177), channel_id=1, source_target_pairs={{0,64},{8,72},{16,80},{24,88},{32,96},{40,104},{48,112},{56,120},{... | collective-permute-start | bytes 3145736 | tf_op jit(solution)/shard_map/ppermute | solution.py:341
  46.0 18.2 %collective-permute-start.3 = (f32[3,32,1024]{2,1,0:T(8,128)}, f32[3,32,1024]{2,1,0:T(8,128)}, u32[]{:S(2)}, u32[]{:S(2)}) collective-permute-start(f32[3,32,1024]{2,1,0:T(8,128)} %get-tuple-element.163), channel_id=1, source_target_pairs={{0,8},{8,16},{16,24},{24,0},{32,40},{40,48},{48,56},{56,32},{64,72... | collective-permute-start | bytes 1179656 | tf_op jit(solution)/shard_map/ppermute | solution.py:341
  47.1 19.3 %collective-permute-start.4 = (f32[3,32,1024]{2,1,0:T(8,128)}, f32[3,32,1024]{2,1,0:T(8,128)}, u32[]{:S(2)}, u32[]{:S(2)}) collective-permute-start(f32[3,32,1024]{2,1,0:T(8,128)} %get-tuple-element.164), channel_id=1, source_target_pairs={{0,16},{8,24},{16,0},{24,8},{32,48},{40,56},{48,32},{56,40},{64,80... | collective-permute-start | bytes 1179656 | tf_op jit(solution)/shard_map/ppermute | solution.py:341
  48.7 17.8 %collective-permute-start.5 = (f32[3,32,1024]{2,1,0:T(8,128)}, f32[3,32,1024]{2,1,0:T(8,128)}, u32[]{:S(2)}, u32[]{:S(2)}) collective-permute-start(f32[3,32,1024]{2,1,0:T(8,128)} %get-tuple-element.165), channel_id=1, source_target_pairs={{0,24},{8,0},{16,8},{24,16},{32,56},{40,32},{48,40},{56,48},{64,88... | collective-permute-start | bytes 1179656 | tf_op jit(solution)/shard_map/ppermute | solution.py:341
  55.3 11.1 %copy-start.18 = (f32[3,32,1024]{2,1,0:T(8,128)S(1)}, f32[3,32,1024]{2,1,0:T(8,128)}, u32[]{:S(2)}) copy-start(f32[3,32,1024]{2,1,0:T(8,128)} %get-tuple-element.192) | copy-start | bytes 1179652
  55.3 11.9 %copy-start.17 = (f32[3,32,1024]{2,1,0:T(8,128)S(1)}, f32[3,32,1024]{2,1,0:T(8,128)}, u32[]{:S(2)}) copy-start(f32[3,32,1024]{2,1,0:T(8,128)} %get-tuple-element.193) | copy-start | bytes 1179652
  55.4 15.1 %copy-start.16 = (f32[3,32,1024]{2,1,0:T(8,128)S(1)}, f32[3,32,1024]{2,1,0:T(8,128)}, u32[]{:S(2)}) copy-start(f32[3,32,1024]{2,1,0:T(8,128)} %get-tuple-element.194) | copy-start | bytes 1179652
  55.4 38.8 %all-to-all-start = ((f32[128,2,16,128]{3,2,1,0:T(8,128)}), f32[128,2,16,128]{3,2,1,0:T(8,128)}, u32[]{:S(2)}, u32[]{:S(2)}) async-start(f32[128,2,16,128]{3,2,1,0:T(8,128)} %bitcast.153), calls=%async_computation | async-start | bytes 4194304 | tf_op jit(solution)/shard_map/all_to_all | solution.py:397
  66.4 46.6 %collective-permute-start.9 = (f32[3,32,1024]{2,1,0:T(8,128)S(1)}, f32[3,32,1024]{2,1,0:T(8,128)}, u32[]{:S(2)}, u32[]{:S(2)}) collective-permute-start(f32[3,32,1024]{2,1,0:T(8,128)S(1)} %copy-done.18), channel_id=1, source_target_pairs={{0,8},{8,16},{16,24},{24,0},{32,40},{40,48},{48,56},{56,32},{64,72... | collective-permute-start | bytes 1179656 | tf_op jit(solution)/shard_map/ppermute | solution.py:341
  67.3 47.7 %collective-permute-start.10 = (f32[3,32,1024]{2,1,0:T(8,128)S(1)}, f32[3,32,1024]{2,1,0:T(8,128)}, u32[]{:S(2)}, u32[]{:S(2)}) collective-permute-start(f32[3,32,1024]{2,1,0:T(8,128)S(1)} %copy-done.17), channel_id=1, source_target_pairs={{0,16},{8,24},{16,0},{24,8},{32,48},{40,56},{48,32},{56,40},{64,80... | collective-permute-start | bytes 1179656 | tf_op jit(solution)/shard_map/ppermute | solution.py:341
  70.4 44.6 %collective-permute-start.11 = (f32[3,32,1024]{2,1,0:T(8,128)S(1)}, f32[3,32,1024]{2,1,0:T(8,128)}, u32[]{:S(2)}, u32[]{:S(2)}) collective-permute-start(f32[3,32,1024]{2,1,0:T(8,128)S(1)} %copy-done.16), channel_id=1, source_target_pairs={{0,24},{8,0},{16,8},{24,16},{32,56},{40,32},{48,40},{56,48},{64,88... | collective-permute-start | bytes 1179656 | tf_op jit(solution)/shard_map/ppermute | solution.py:341
  73.6 4.2 %copy-start.4 = (f32[4,2,64,512]{3,2,1,0:T(8,128)}, f32[4,2,64,512]{3,2,1,0:T(8,128)S(1)}, u32[]{:S(2)}) copy-start(f32[4,2,64,512]{3,2,1,0:T(8,128)S(1)} %collective-permute-done.8.a2) | copy-start | bytes 3145732
  94.2 27.5 %all-to-all-start.1 = ((f32[128,1,16,128]{3,2,1,0:T(8,128)}), f32[128,1,16,128]{3,2,1,0:T(8,128)S(1)}, u32[]{:S(2)}, u32[]{:S(2)}) async-start(f32[128,1,16,128]{3,2,1,0:T(8,128)} %bitcast.157), calls=%async_computation.1 | async-start | bytes 2097152 | tf_op jit(solution)/shard_map/all_to_all | solution.py:397
  109.3 28.9 %collective-permute-start.12 = (f32[2,2,64,512]{3,2,1,0:T(8,128)}, f32[2,2,64,512]{3,2,1,0:T(8,128)S(1)}, u32[]{:S(2)}, u32[]{:S(2)}) collective-permute-start(f32[2,2,64,512]{3,2,1,0:T(8,128)} %get-tuple-element.202), channel_id=1, source_target_pairs={{0,32},{8,40},{16,48},{24,56},{32,64},{40,72},{48,80},{56,88},{64,... | collective-permute-start | bytes 1572872 | tf_op jit(solution)/shard_map/ppermute | solution.py:341
  110.3 38.1 %collective-permute-start.13 = (f32[2,2,64,512]{3,2,1,0:T(8,128)}, f32[2,2,64,512]{3,2,1,0:T(8,128)S(1)}, u32[]{:S(2)}, u32[]{:S(2)}) collective-permute-start(f32[2,2,64,512]{3,2,1,0:T(8,128)} %get-tuple-element.203), channel_id=1, source_target_pairs={{0,64},{8,72},{16,80},{24,88},{32,96},{40,104},{48,112},{56,120},{... | collective-permute-start | bytes 1572872 | tf_op jit(solution)/shard_map/ppermute | solution.py:341
  113.0 35.4 %collective-permute-start.14 = (f32[2,2,64,512]{3,2,1,0:T(8,128)}, f32[2,2,64,512]{3,2,1,0:T(8,128)}, u32[]{:S(2)}, u32[]{:S(2)}) collective-permute-start(f32[2,2,64,512]{3,2,1,0:T(8,128)} %get-tuple-element.204), channel_id=1, source_target_pairs={{0,96},{8,104},{16,112},{24,120},{32,0},{40,8},{48,16},{56,24},{64... | collective-permute-start | bytes 1572872 | tf_op jit(solution)/shard_map/ppermute | solution.py:341
  121.7 8.3 %copy-start.1 = (f32[128,1,16,128]{3,2,1,0:T(8,128)}, f32[128,1,16,128]{3,2,1,0:T(8,128)S(1)}, u32[]{:S(2)}) copy-start(f32[128,1,16,128]{3,2,1,0:T(8,128)S(1)} %all-to-all-done.1) | copy-start | bytes 3145732
  121.7 35.1 %all-to-all-start.2 = ((f32[128,1,16,128]{3,2,1,0:T(8,128)}), f32[128,1,16,128]{3,2,1,0:T(8,128)S(1)}, u32[]{:S(2)}, u32[]{:S(2)}) async-start(f32[128,1,16,128]{3,2,1,0:T(8,128)} %bitcast.156), calls=%async_computation.2 | async-start | bytes 2097152 | tf_op jit(solution)/shard_map/all_to_all | solution.py:397
  134.4 22.3 %collective-permute-start.15 = (f32[1,2,64,512]{3,2,1,0:T(8,128)}, f32[1,2,64,512]{3,2,1,0:T(8,128)S(1)}, u32[]{:S(2)}, u32[]{:S(2)}) collective-permute-start(f32[1,2,64,512]{3,2,1,0:T(8,128)} %get-tuple-element.205), channel_id=1, source_target_pairs={{0,32},{8,40},{16,48},{24,56},{32,64},{40,72},{48,80},{56,88},{64,... | collective-permute-start | bytes 786440 | tf_op jit(solution)/shard_map/ppermute | solution.py:341
  135.4 30.0 %collective-permute-start.16 = (f32[1,2,64,512]{3,2,1,0:T(8,128)}, f32[1,2,64,512]{3,2,1,0:T(8,128)S(1)}, u32[]{:S(2)}, u32[]{:S(2)}) collective-permute-start(f32[1,2,64,512]{3,2,1,0:T(8,128)} %get-tuple-element.208), channel_id=1, source_target_pairs={{0,64},{8,72},{16,80},{24,88},{32,96},{40,104},{48,112},{56,120},{... | collective-permute-start | bytes 786440 | tf_op jit(solution)/shard_map/ppermute | solution.py:341
  138.2 10.2 %copy-start.14 = (f32[2,2,64,512]{3,2,1,0:T(8,128)}, f32[2,2,64,512]{3,2,1,0:T(8,128)S(1)}, u32[]{:S(2)}) copy-start(f32[2,2,64,512]{3,2,1,0:T(8,128)S(1)} %collective-permute-done.12.refs_1_) | copy-start | bytes 1572868
  138.2 27.3 %collective-permute-start.17 = (f32[1,2,64,512]{3,2,1,0:T(8,128)}, f32[1,2,64,512]{3,2,1,0:T(8,128)S(1)}, u32[]{:S(2)}, u32[]{:S(2)}) collective-permute-start(f32[1,2,64,512]{3,2,1,0:T(8,128)} %get-tuple-element.209), channel_id=1, source_target_pairs={{0,96},{8,104},{16,112},{24,120},{32,0},{40,8},{48,16},{56,24},{64... | collective-permute-start | bytes 786440 | tf_op jit(solution)/shard_map/ppermute | solution.py:341
  148.4 0.9 copy-start.15
  156.7 8.8 %copy-start.6 = (f32[1,2,64,512]{3,2,1,0:T(8,128)}, f32[1,2,64,512]{3,2,1,0:T(8,128)S(1)}, u32[]{:S(2)}) copy-start(f32[1,2,64,512]{3,2,1,0:T(8,128)S(1)} %collective-permute-done.15.refs_1_) | copy-start | bytes 786436
  156.7 1.1 copy-start
  162.2 15.3 %collective-permute-start.18 = (f32[1,2,64,512]{3,2,1,0:T(8,128)}, f32[1,2,64,512]{3,2,1,0:T(8,128)S(1)}, u32[]{:S(2)}, u32[]{:S(2)}) collective-permute-start(f32[1,2,64,512]{3,2,1,0:T(8,128)} %get-tuple-element.213), channel_id=1, source_target_pairs={{0,32},{8,40},{16,48},{24,56},{32,64},{40,72},{48,80},{56,88},{64,... | collective-permute-start | bytes 786440 | tf_op jit(solution)/shard_map/ppermute | solution.py:341
  162.3 15.3 %collective-permute-start.19 = (f32[1,2,64,512]{3,2,1,0:T(8,128)}, f32[1,2,64,512]{3,2,1,0:T(8,128)S(1)}, u32[]{:S(2)}, u32[]{:S(2)}) collective-permute-start(f32[1,2,64,512]{3,2,1,0:T(8,128)} %get-tuple-element.214), channel_id=1, source_target_pairs={{0,64},{8,72},{16,80},{24,88},{32,96},{40,104},{48,112},{56,120},{... | collective-permute-start | bytes 786440 | tf_op jit(solution)/shard_map/ppermute | solution.py:341
  164.4 13.8 %collective-permute-start.20 = (f32[1,2,64,512]{3,2,1,0:T(8,128)}, f32[1,2,64,512]{3,2,1,0:T(8,128)S(1)}, u32[]{:S(2)}, u32[]{:S(2)}) collective-permute-start(f32[1,2,64,512]{3,2,1,0:T(8,128)} %get-tuple-element.215), channel_id=1, source_target_pairs={{0,96},{8,104},{16,112},{24,120},{32,0},{40,8},{48,16},{56,24},{64... | collective-permute-start | bytes 786440 | tf_op jit(solution)/shard_map/ppermute | solution.py:341
  165.5 0.7 copy-start.7
  165.5 0.8 copy-start.8
  177.5 0.7 copy-start.9
  177.5 0.8 copy-start.10
  178.3 0.7 copy-start.11

commit v5 on v4

--- a/solution.py
+++ b/solution.py
@@ -378,7 +378,7 @@
         if k:
             if k + 1 == len(CHUNKS):
                 result[0] = last(CHUNKS[0], yr, back[0], None, 10_000_000_000)
-                result[0], back[k - 1][1], moved[k] = tie((result[0], back[k - 1][1], moved[k]))
+                result[0], moved[k] = tie((result[0], moved[k]))
         done = late(CHUNKS[k], yr, moved[k], turns, w2, w3, (8_000_000_000, 1000, 1000)[k])
         back[k] = exchange(done, Q)
 
@@ -404,7 +404,7 @@
     for k in range(1, count):
         if k + 1 < count:
             back[k], back[k + 1][0] = tie((back[k], back[k + 1][0]))
-        result[0] = last(CHUNKS[k], yr, back[k], result[0])
+        result[0] = last(CHUNKS[k], yr, back[k], result[0], 5_000_000_000 if k == 1 else 1000)
     return result[0].reshape(2, PTS, BOX, FL)
 
 

time: 182 us -> 182 us (level)
  other arithmetic: 8.32 us -> 14.7 us
  starting transfers between devices: 60.3 us -> 56.2 us
  waiting for transfers between devices: 51.4 us -> 47.9 us
    all_to_all x3, waiting for transfers between devices: 19.2 us -> 11.1 us  [on_device(): lax.all_to_all(mixed[k].reshape(128, chunk[1], PTS, 128), ('space', 'freq...]
    all_to_all x3, starting transfers between devices: 25.5 us -> 20.5 us  [on_device(): lax.all_to_all(mixed[k].reshape(128, chunk[1], PTS, 128), ('space', 'freq...]
    ppermute x21, waiting for transfers between devices: 32.2 us -> 36.8 us  [swapped(): return lax.ppermute(part, 'space', [(i, target(i)) for i in range(count)])]
    unnamed x38 -> x50, local copies, waits for them, and re-layouts: 3.64 us -> 2.76 us
  transfers between devices with their start and end apart: 24 -> 24, of which waited for: 9 -> 10; matrix products, arithmetic and copies ran while one was open for 7% -> 11% of each run, Pallas kernels for 25% -> 25%
where the time goes in v5:
time: 182 us; the launch traced here: 181 us
  starting transfers between devices  56.2 us (31%)
  Pallas kernels  53.3 us (29%)
  waiting for transfers between devices  47.9 us (26%)
  other arithmetic  14.7 us (8%)
  local copies, waits for them, and re-layouts  7.51 us (4%)
    ppermute x21, waiting for transfers between devices, swapped(): return lax.ppermute(part, 'space', [(i, target(i)) for i in range(count)])  36.8 us
    ppermute x21, starting transfers between devices, swapped(): return lax.ppermute(part, 'space', [(i, target(i)) for i in range(count)])  35.7 us
    all_to_all x3, starting transfers between devices, on_device(): lax.all_to_all(mixed[k].reshape(128, chunk[1], PTS, 128), ('space', 'freq...  20.5 us
    pallas_call x3, Pallas kernels, late(): pl.pallas_call(late_kernel, grid_spec=pltpu.PrefetchScalarGridSpec(num_sc...  15.8 us
    pallas_call x3, Pallas kernels, early(): pl.pallas_call(early_kernel, grid_spec=pltpu.PrefetchScalarGridSpec(num_s...  13.4 us
    pallas_call x3, Pallas kernels, first(): pl.pallas_call(functools.partial(first_kernel, n), grid_spec=pltpu.Prefet...  11.6 us
    all_to_all x3, waiting for transfers between devices, on_device(): lax.all_to_all(mixed[k].reshape(128, chunk[1], PTS, 128), ('space', 'freq...  11.1 us
    pallas_call x3, Pallas kernels, last(): pl.pallas_call(functools.partial(last_kernel, chunk), grid_spec=pltpu.Pre...  8.11 us
  transfers between devices with their start and end apart: 24, of which 10 were waited for; matrix products, arithmetic and copies ran while one was open for 11% of the time, Pallas kernels for 25%

profile of v5, /device:TPU:0, one launch (start us, length us, event | category | flops | bytes accessed | tf_op | source)
XLA Modules:
  0.0 181.0 jit_solution(13337518325898270901)
XLA Ops:
  0.0 5.0 %first.3 = (f32[3,32,2048]{2,1,0:T(8,128)}, f32[3,32,2048]{2,1,0:T(8,128)}, f32[3,32,2048]{2,1,0:T(8,128)}, f32[3,32,2048]{2,1,0:T(8,128)}) custom-call(s32[1]{0:T(128)} %bitcast.1.zr, f32[2,128,4096]{2,1,0:T(8,128)} %bitcast.141, f32[2,128,4096]{2,1,0:T(8,128)} %bitcast.142, f32[2,128,4096]{2,1,0:T(8,128)} %bitcast.143, f32[2,128,4096]{2,1,0:T(8,128)} %bitcast.144, ...), custom_call_target="tpu_custom_call" | custom-call | flops 1000 | bytes 1000 | tf_op jit(solution)/shard_map/first/pallas_call | solution.py:82
  5.0 2.1 %collective-permute-start = (f32[3,32,2048]{2,1,0:T(8,128)}, f32[3,32,2048]{2,1,0:T(8,128)}, u32[]{:S(2)}, u32[]{:S(2)}) collective-permute-start(f32[3,32,2048]{2,1,0:T(8,128)} %get-tuple-element.117), channel_id=1, source_target_pairs={{0,8},{8,16},{16,24},{24,0},{32,40},{40,48},{48,56},{56,32},{64,72... | collective-permute-start | bytes 2359304 | tf_op jit(solution)/shard_map/ppermute | solution.py:341
  7.0 3.6 %collective-permute-start.1 = (f32[3,32,2048]{2,1,0:T(8,128)}, f32[3,32,2048]{2,1,0:T(8,128)}, u32[]{:S(2)}, u32[]{:S(2)}) collective-permute-start(f32[3,32,2048]{2,1,0:T(8,128)} %get-tuple-element.118), channel_id=1, source_target_pairs={{0,16},{8,24},{16,0},{24,8},{32,48},{40,56},{48,32},{56,40},{64,80... | collective-permute-start | bytes 2359304 | tf_op jit(solution)/shard_map/ppermute | solution.py:341
  10.6 1.0 collective-permute-start.2
  11.6 4.3 %share.1 = (f32[4,2,64,512]{3,2,1,0:T(8,128)}, f32[4,2,64,512]{3,2,1,0:T(8,128)}, f32[4,2,64,512]{3,2,1,0:T(8,128)}, f32[4,2,64,512]{3,2,1,0:T(8,128)}) custom-call(s32[1]{0:T(128)} %bitcast.yr, f32[4,128,4096]{2,1,0:T(8,128)} %bitcast.132), custom_call_target="tpu_custom_call" | custom-call | flops 1000 | bytes 1000 | tf_op jit(solution)/shard_map/share/pallas_call | solution.py:114
  15.9 1.6 collective-permute-start.6
  17.5 1.7 collective-permute-start.7
  19.2 0.6 and_compare_fusion.1
  19.8 0.6 iota_xor_fusion
  20.9 0.6 broadcast_subtract_fusion
  21.5 3.3 %first.5 = (f32[3,32,1024]{2,1,0:T(8,128)}, f32[3,32,1024]{2,1,0:T(8,128)}, f32[3,32,1024]{2,1,0:T(8,128)}, f32[3,32,1024]{2,1,0:T(8,128)}) custom-call(s32[1]{0:T(128)} %bitcast.1.zr, f32[2,128,4096]{2,1,0:T(8,128)} %bitcast.145, f32[2,128,4096]{2,1,0:T(8,128)} %bitcast.146, f32[2,128,4096]{2,1,0:T(8,128)} %bitcast.147, f32[2,128,4096]{2,1,0:T(8,128)} %bitcast.148, ...), custom_call_target="tpu_custom_call" | custom-call | flops 1000 | bytes 1000 | tf_op jit(solution)/shard_map/first/pallas_call | solution.py:82
  24.8 3.4 %first.4 = (f32[3,32,1024]{2,1,0:T(8,128)}, f32[3,32,1024]{2,1,0:T(8,128)}, f32[3,32,1024]{2,1,0:T(8,128)}, f32[3,32,1024]{2,1,0:T(8,128)}) custom-call(s32[1]{0:T(128)} %bitcast.1.zr, f32[2,128,4096]{2,1,0:T(8,128)} %bitcast.149, f32[2,128,4096]{2,1,0:T(8,128)} %bitcast.150, f32[2,128,4096]{2,1,0:T(8,128)} %bitcast.151, f32[2,128,4096]{2,1,0:T(8,128)} %bitcast.152, ...), custom_call_target="tpu_custom_call" | custom-call | flops 1000 | bytes 1000 | tf_op jit(solution)/shard_map/first/pallas_call | solution.py:82
  29.4 0.6 iota_compare_fusion.1
  30.0 0.7 slice_bitcast_fusion.8
  32.5 0.9 copy.38
  33.4 1.6 select_reduce_fusion
  35.0 1.4 fusion.4
  36.4 0.7 multiply_bitcast_fusion.1
  37.2 1.0 add_bitcast_fusion.2
  38.2 0.8 fusion.6
  39.8 0.8 reshape.129
  40.7 1.3 add_bitcast_fusion
  42.6 0.8 pad_maximum_fusion.w1
  43.4 0.9 reduce-precision_convert_fusion.3
  44.2 0.7 pad_maximum_fusion.3.w0
  44.9 2.1 %collective-permute-start.8 = (f32[4,2,64,512]{3,2,1,0:T(8,128)}, f32[4,2,64,512]{3,2,1,0:T(8,128)S(1)}, u32[]{:S(2)}, u32[]{:S(2)}) collective-permute-start(f32[4,2,64,512]{3,2,1,0:T(8,128)} %get-tuple-element.176), channel_id=1, source_target_pairs={{0,64},{8,72},{16,80},{24,88},{32,96},{40,104},{48,112},{56,120},{... | collective-permute-start | bytes 3145736 | tf_op jit(solution)/shard_map/ppermute | solution.py:341
  47.0 0.8 pad_maximum_fusion.2.w3
  47.8 0.7 pad_maximum_fusion.1.w2
  48.6 1.1 collective-permute-start.3
  50.1 2.3 %collective-permute-start.5 = (f32[3,32,1024]{2,1,0:T(8,128)}, f32[3,32,1024]{2,1,0:T(8,128)}, u32[]{:S(2)}, u32[]{:S(2)}) collective-permute-start(f32[3,32,1024]{2,1,0:T(8,128)} %get-tuple-element.164), channel_id=1, source_target_pairs={{0,24},{8,0},{16,8},{24,16},{32,56},{40,32},{48,40},{56,48},{64,88... | collective-permute-start | bytes 1179656 | tf_op jit(solution)/shard_map/ppermute | solution.py:341
  52.5 5.4 %early.3 = f32[4,4,8,2,16,128]{5,4,3,2,1,0:T(8,128)} custom-call(s32[1]{0:T(128)} %bitcast.1.zr, f32[3,32,2048]{2,1,0:T(8,128)} %get-tuple-element.155.r0, f32[3,32,2048]{2,1,0:T(8,128)} %collective-permute-done.r1, f32[3,32,2048]{2,1,0:T(8,128)} %collective-permute-done.1.r2, f32[3,32,2048]{2,1,0:T(8,128)} %collective-permute-done.2.r3, ...), custom_call_target="tpu_custom_call" | custom-call | flops 1000 | bytes 1000 | tf_op jit(solution)/shard_map/early/pallas_call | solution.py:158
  57.9 7.7 %all-to-all-start = ((f32[128,2,16,128]{3,2,1,0:T(8,128)}), f32[128,2,16,128]{3,2,1,0:T(8,128)S(1)}, u32[]{:S(2)}, u32[]{:S(2)}) async-start(f32[128,2,16,128]{3,2,1,0:T(8,128)} %bitcast.153), calls=%async_computation | async-start | bytes 4194304 | tf_op jit(solution)/shard_map/all_to_all | solution.py:397
  65.6 2.2 %collective-permute-done.3.r1 = f32[3,32,1024]{2,1,0:T(8,128)} collective-permute-done((f32[3,32,1024]{2,1,0:T(8,128)}, f32[3,32,1024]{2,1,0:T(8,128)}, u32[]{:S(2)}, u32[]{:S(2)}) %collective-permute-start.3) | collective-permute-done | bytes 393248 | tf_op jit(solution)/shard_map/ppermute | solution.py:341
  67.8 2.3 %collective-permute-done.5.r3 = f32[3,32,1024]{2,1,0:T(8,128)} collective-permute-done((f32[3,32,1024]{2,1,0:T(8,128)}, f32[3,32,1024]{2,1,0:T(8,128)}, u32[]{:S(2)}, u32[]{:S(2)}) %collective-permute-start.5) | collective-permute-done | bytes 393248 | tf_op jit(solution)/shard_map/ppermute | solution.py:341
  70.1 5.5 %collective-permute-start.10 = (f32[3,32,1024]{2,1,0:T(8,128)}, f32[3,32,1024]{2,1,0:T(8,128)}, u32[]{:S(2)}, u32[]{:S(2)}) collective-permute-start(f32[3,32,1024]{2,1,0:T(8,128)} %get-tuple-element.192), channel_id=1, source_target_pairs={{0,16},{8,24},{16,0},{24,8},{32,48},{40,56},{48,32},{56,40},{64,80... | collective-permute-start | bytes 1179656 | tf_op jit(solution)/shard_map/ppermute | solution.py:341
  75.7 6.5 %collective-permute-done.8.a2 = f32[4,2,64,512]{3,2,1,0:T(8,128)S(1)} collective-permute-done((f32[4,2,64,512]{3,2,1,0:T(8,128)}, f32[4,2,64,512]{3,2,1,0:T(8,128)S(1)}, u32[]{:S(2)}, u32[]{:S(2)}) %collective-permute-start.8) | collective-permute-done | bytes 1048608 | tf_op jit(solution)/shard_map/ppermute | solution.py:341
  82.2 4.2 %early.4 = f32[4,4,8,1,16,128]{5,4,3,2,1,0:T(8,128)} custom-call(s32[1]{0:T(128)} %bitcast.1.zr, f32[3,32,1024]{2,1,0:T(8,128)} %get-tuple-element.177.r0, f32[3,32,1024]{2,1,0:T(8,128)} %collective-permute-done.3.r1, f32[3,32,1024]{2,1,0:T(8,128)} %collective-permute-done.4.r2, f32[3,32,1024]{2,1,0:T(8,128)} %collective-permute-done.5.r3, ...), custom_call_target="tpu_custom_call" | custom-call | flops 40000000000 | bytes 1000 | tf_op jit(solution)/shard_map/early/pallas_call | solution.py:158
  86.4 9.7 %all-to-all-done = f32[128,2,16,128]{3,2,1,0:T(8,128)S(1)} async-done(((f32[128,2,16,128]{3,2,1,0:T(8,128)}), f32[128,2,16,128]{3,2,1,0:T(8,128)S(1)}, u32[]{:S(2)}, u32[]{:S(2)}) %all-to-all-start) | async-done | bytes 2097184 | tf_op jit(solution)/shard_map/all_to_all | solution.py:397
  96.0 6.0 %all-to-all-start.1 = ((f32[128,1,16,128]{3,2,1,0:T(8,128)}), f32[128,1,16,128]{3,2,1,0:T(8,128)S(1)}, u32[]{:S(2)}, u32[]{:S(2)}) async-start(f32[128,1,16,128]{3,2,1,0:T(8,128)} %bitcast.157), calls=%async_computation.1 | async-start | bytes 2097152 | tf_op jit(solution)/shard_map/all_to_all | solution.py:397
  102.1 6.9 %late.3 = (f32[2,2,64,512]{3,2,1,0:T(8,128)}, f32[2,2,64,512]{3,2,1,0:T(8,128)}, f32[2,2,64,512]{3,2,1,0:T(8,128)}, f32[2,2,64,512]{3,2,1,0:T(8,128)}) custom-call(s32[1]{0:T(128)} %bitcast.yr, f32[4,4,8,2,16,128]{5,4,3,2,1,0:T(8,128)} %bitcast.156, f32[4,2,64,512]{3,2,1,0:T(8,128)} %get-tuple-element.183.a0, f32[4,2,64,512]{3,2,1,0:T(8,128)} %copy-done.2, ...), custom_call_target="tpu_custom_call" | custom-call | flops 8000000000 | bytes 1000 | tf_op jit(solution)/shard_map/late/pallas_call | solution.py:204
  108.9 1.0 collective-permute-start.15
  109.9 2.7 %collective-permute-start.16 = (f32[2,2,64,512]{3,2,1,0:T(8,128)}, f32[2,2,64,512]{3,2,1,0:T(8,128)S(1)}, u32[]{:S(2)}, u32[]{:S(2)}) collective-permute-start(f32[2,2,64,512]{3,2,1,0:T(8,128)} %get-tuple-element.205), channel_id=1, source_target_pairs={{0,64},{8,72},{16,80},{24,88},{32,96},{40,104},{48,112},{56,120},{... | collective-permute-start | bytes 1572872 | tf_op jit(solution)/shard_map/ppermute | solution.py:341
  112.6 1.4 collective-permute-start.17
  114.1 6.5 %collective-permute-done.10.r2 = f32[3,32,1024]{2,1,0:T(8,128)} collective-permute-done((f32[3,32,1024]{2,1,0:T(8,128)}, f32[3,32,1024]{2,1,0:T(8,128)}, u32[]{:S(2)}, u32[]{:S(2)}) %collective-permute-start.10) | collective-permute-done | bytes 393248 | tf_op jit(solution)/shard_map/ppermute | solution.py:341
  120.6 3.8 %early.5 = f32[4,4,8,1,16,128]{5,4,3,2,1,0:T(8,128)} custom-call(s32[1]{0:T(128)} %bitcast.1.zr, f32[3,32,1024]{2,1,0:T(8,128)} %get-tuple-element.194.r0, f32[3,32,1024]{2,1,0:T(8,128)} %collective-permute-done.9.r1, f32[3,32,1024]{2,1,0:T(8,128)} %collective-permute-done.10.r2, f32[3,32,1024]{2,1,0:T(8,128)} %collective-permute-done.11.r3, ...), custom_call_target="tpu_custom_call" | custom-call | flops 3000000000 | bytes 1000 | tf_op jit(solution)/shard_map/early/pallas_call | solution.py:158
  124.4 6.7 %all-to-all-start.2 = ((f32[128,1,16,128]{3,2,1,0:T(8,128)}), f32[128,1,16,128]{3,2,1,0:T(8,128)S(1)}, u32[]{:S(2)}, u32[]{:S(2)}) async-start(f32[128,1,16,128]{3,2,1,0:T(8,128)} %bitcast.158), calls=%async_computation.2 | async-start | bytes 2097152 | tf_op jit(solution)/shard_map/all_to_all | solution.py:397
  131.2 4.5 %late.4 = (f32[1,2,64,512]{3,2,1,0:T(8,128)}, f32[1,2,64,512]{3,2,1,0:T(8,128)}, f32[1,2,64,512]{3,2,1,0:T(8,128)}, f32[1,2,64,512]{3,2,1,0:T(8,128)}) custom-call(s32[1]{0:T(128)} %bitcast.yr, f32[4,4,8,1,16,128]{5,4,3,2,1,0:T(8,128)} %bitcast.154, f32[4,2,64,512]{3,2,1,0:T(8,128)} %get-tuple-element.183.a0, f32[4,2,64,512]{3,2,1,0:T(8,128)} %copy-done.2, ...), custom_call_target="tpu_custom_call" | custom-call | flops 1000 | bytes 1000 | tf_op jit(solution)/shard_map/late/pallas_call | solution.py:204
  135.7 1.0 collective-permute-start.12
  136.7 2.7 %collective-permute-start.13 = (f32[1,2,64,512]{3,2,1,0:T(8,128)}, f32[1,2,64,512]{3,2,1,0:T(8,128)S(1)}, u32[]{:S(2)}, u32[]{:S(2)}) collective-permute-start(f32[1,2,64,512]{3,2,1,0:T(8,128)} %get-tuple-element.201), channel_id=1, source_target_pairs={{0,64},{8,72},{16,80},{24,88},{32,96},{40,104},{48,112},{56,120},{... | collective-permute-start | bytes 786440 | tf_op jit(solution)/shard_map/ppermute | solution.py:341
  139.4 1.4 collective-permute-start.14
  140.8 7.1 %collective-permute-done.16.refs_2_ = f32[2,2,64,512]{3,2,1,0:T(8,128)S(1)} collective-permute-done((f32[2,2,64,512]{3,2,1,0:T(8,128)}, f32[2,2,64,512]{3,2,1,0:T(8,128)S(1)}, u32[]{:S(2)}, u32[]{:S(2)}) %collective-permute-start.16) | collective-permute-done | bytes 524320 | tf_op jit(solution)/shard_map/ppermute | solution.py:341
  147.9 0.8 copy-done.20
  148.7 3.2 %last.3.refs_4_ = f32[2,128,4096]{2,1,0:T(8,128)} custom-call(s32[1]{0:T(128)} %bitcast.yr, f32[2,2,64,512]{3,2,1,0:T(8,128)} %get-tuple-element.203.refs_0_, f32[2,2,64,512]{3,2,1,0:T(8,128)} %copy-done.19, f32[2,2,64,512]{3,2,1,0:T(8,128)} %copy-done.20, f32[2,2,64,512]{3,2,1,0:T(8,128)} %collective-permute-done.17.refs_3_), custom_call_target="tpu_custom_call" | custom-call | flops 10000000000 | bytes 1000 | tf_op jit(solution)/shard_map/last/pallas_call | solution.py:253
  151.9 1.4 all-to-all-done.2
  153.4 1.0 copy-done.1
  154.4 4.4 %late.5 = (f32[1,2,64,512]{3,2,1,0:T(8,128)}, f32[1,2,64,512]{3,2,1,0:T(8,128)}, f32[1,2,64,512]{3,2,1,0:T(8,128)}, f32[1,2,64,512]{3,2,1,0:T(8,128)}) custom-call(s32[1]{0:T(128)} %bitcast.yr, f32[4,4,8,1,16,128]{5,4,3,2,1,0:T(8,128)} %bitcast.155, f32[4,2,64,512]{3,2,1,0:T(8,128)} %get-tuple-element.183.a0, f32[4,2,64,512]{3,2,1,0:T(8,128)} %copy-done.2, ...), custom_call_target="tpu_custom_call" | custom-call | flops 1000 | bytes 1000 | tf_op jit(solution)/shard_map/late/pallas_call | solution.py:204
  158.8 2.9 %collective-permute-done.13.refs_2_ = f32[1,2,64,512]{3,2,1,0:T(8,128)S(1)} collective-permute-done((f32[1,2,64,512]{3,2,1,0:T(8,128)}, f32[1,2,64,512]{3,2,1,0:T(8,128)S(1)}, u32[]{:S(2)}, u32[]{:S(2)}) %collective-permute-start.13) | collective-permute-done | bytes 262176 | tf_op jit(solution)/shard_map/ppermute | solution.py:341
  162.1 2.1 %collective-permute-start.19 = (f32[1,2,64,512]{3,2,1,0:T(8,128)}, f32[1,2,64,512]{3,2,1,0:T(8,128)S(1)}, u32[]{:S(2)}, u32[]{:S(2)}) collective-permute-start(f32[1,2,64,512]{3,2,1,0:T(8,128)} %get-tuple-element.212), channel_id=1, source_target_pairs={{0,64},{8,72},{16,80},{24,88},{32,96},{40,104},{48,112},{56,120},{... | collective-permute-start | bytes 786440 | tf_op jit(solution)/shard_map/ppermute | solution.py:341
  164.2 1.6 collective-permute-start.20
  165.8 2.4 %last.4.refs_4_ = f32[2,128,4096]{2,1,0:T(8,128)} custom-call(s32[1]{0:T(128)} %bitcast.yr, f32[1,2,64,512]{3,2,1,0:T(8,128)} %get-tuple-element.214.refs_0_, f32[1,2,64,512]{3,2,1,0:T(8,128)} %copy-done.22, f32[1,2,64,512]{3,2,1,0:T(8,128)} %copy-done.23, f32[1,2,64,512]{3,2,1,0:T(8,128)} %copy-done.24, ...), custom_call_target="tpu_custom_call", output_to_operand_aliasing={{}: (5, {})} | custom-call | flops 5000000000 | bytes 1000 | tf_op jit(solution)/shard_map/last/pallas_call | solution.py:253
  168.3 8.6 %collective-permute-done.18.refs_1_ = f32[1,2,64,512]{3,2,1,0:T(8,128)S(1)} collective-permute-done((f32[1,2,64,512]{3,2,1,0:T(8,128)}, f32[1,2,64,512]{3,2,1,0:T(8,128)S(1)}, u32[]{:S(2)}, u32[]{:S(2)}) %collective-permute-start.18) | collective-permute-done | bytes 262176 | tf_op jit(solution)/shard_map/ppermute | solution.py:341
  176.9 0.6 collective-permute-done.20.refs_3_
  177.7 0.7 copy-done.12
  178.4 2.4 %last.5 = f32[2,128,4096]{2,1,0:T(8,128)} custom-call(s32[1]{0:T(128)} %bitcast.yr, f32[1,2,64,512]{3,2,1,0:T(8,128)} %get-tuple-element.210.refs_0_, f32[1,2,64,512]{3,2,1,0:T(8,128)} %copy-done.10, f32[1,2,64,512]{3,2,1,0:T(8,128)} %copy-done.11, f32[1,2,64,512]{3,2,1,0:T(8,128)} %copy-done.12, ...), custom_call_target="tpu_custom_call", output_to_operand_aliasing={{}: (5, {})} | custom-call | flops 1000 | bytes 1000 | tf_op jit(solution)/shard_map/last/pallas_call | solution.py:253
  (107 shorter events, 6.0 us)
Async XLA Ops:
  5.0 43.6 %collective-permute-start = (f32[3,32,2048]{2,1,0:T(8,128)}, f32[3,32,2048]{2,1,0:T(8,128)}, u32[]{:S(2)}, u32[]{:S(2)}) collective-permute-start(f32[3,32,2048]{2,1,0:T(8,128)} %get-tuple-element.117), channel_id=1, source_target_pairs={{0,8},{8,16},{16,24},{24,0},{32,40},{40,48},{48,56},{56,32},{64,72... | collective-permute-start | bytes 2359304 | tf_op jit(solution)/shard_map/ppermute | solution.py:341
  7.0 41.6 %collective-permute-start.1 = (f32[3,32,2048]{2,1,0:T(8,128)}, f32[3,32,2048]{2,1,0:T(8,128)}, u32[]{:S(2)}, u32[]{:S(2)}) collective-permute-start(f32[3,32,2048]{2,1,0:T(8,128)} %get-tuple-element.118), channel_id=1, source_target_pairs={{0,16},{8,24},{16,0},{24,8},{32,48},{40,56},{48,32},{56,40},{64,80... | collective-permute-start | bytes 2359304 | tf_op jit(solution)/shard_map/ppermute | solution.py:341
  10.6 38.0 %collective-permute-start.2 = (f32[3,32,2048]{2,1,0:T(8,128)}, f32[3,32,2048]{2,1,0:T(8,128)}, u32[]{:S(2)}, u32[]{:S(2)}) collective-permute-start(f32[3,32,2048]{2,1,0:T(8,128)} %get-tuple-element.119), channel_id=1, source_target_pairs={{0,24},{8,0},{16,8},{24,16},{32,56},{40,32},{48,40},{56,48},{64,88... | collective-permute-start | bytes 2359304 | tf_op jit(solution)/shard_map/ppermute | solution.py:341
  15.9 29.0 %collective-permute-start.6 = (f32[4,2,64,512]{3,2,1,0:T(8,128)}, f32[4,2,64,512]{3,2,1,0:T(8,128)S(1)}, u32[]{:S(2)}, u32[]{:S(2)}) collective-permute-start(f32[4,2,64,512]{3,2,1,0:T(8,128)} %get-tuple-element.173), channel_id=1, source_target_pairs={{0,32},{8,40},{16,48},{24,56},{32,64},{40,72},{48,80},{56,88},{64,... | collective-permute-start | bytes 3145736 | tf_op jit(solution)/shard_map/ppermute | solution.py:341
  17.5 27.4 %collective-permute-start.7 = (f32[4,2,64,512]{3,2,1,0:T(8,128)}, f32[4,2,64,512]{3,2,1,0:T(8,128)S(1)}, u32[]{:S(2)}, u32[]{:S(2)}) collective-permute-start(f32[4,2,64,512]{3,2,1,0:T(8,128)} %get-tuple-element.175), channel_id=1, source_target_pairs={{0,96},{8,104},{16,112},{24,120},{32,0},{40,8},{48,16},{56,24},{64... | collective-permute-start | bytes 3145736 | tf_op jit(solution)/shard_map/ppermute | solution.py:341
  19.2 9.0 %copy-start.18 = (pred[4]{0:T(512)(128)(4,1)}, pred[4]{0:T(512)(128)(4,1)S(1)}, u32[]{:S(2)}) copy-start(pred[4]{0:T(512)(128)(4,1)S(1)} %and_compare_fusion.2) | copy-start | bytes 16
  24.8 3.6 %copy-start.13 = (f32[2,16,16]{2,1,0:T(8,128)S(1)}, f32[2,16,16]{2,1,0:T(8,128)}, u32[]{:S(2)}) copy-start(f32[2,16,16]{2,1,0:T(8,128)} %param.8) | copy-start | bytes 6148
  24.8 3.6 %copy-start.14 = (s32[4,128]{1,0:T(4,128)S(1)}, s32[4,128]{1,0:T(4,128)}, u32[]{:S(2)}) copy-start(s32[4,128]{1,0:T(4,128)} %param.9) | copy-start | bytes 6148
  24.8 5.2 %copy-start.7 = (f32[4,4,2,2,16,16]{5,4,3,2,1,0:T(8,128)S(1)}, f32[4,4,2,2,16,16]{5,4,3,2,1,0:T(8,128)}, u32[]{:S(2)}) copy-start(f32[4,4,2,2,16,16]{5,4,3,2,1,0:T(8,128)} %param.7) | copy-start | bytes 196612
  33.4 3.8 %copy-start.6 = (f32[2,2,2,2,16,2,16]{6,5,4,3,0,1,2:T(2,128)S(1)}, f32[2,2,2,2,16,2,16]{6,5,4,3,0,1,2:T(2,128)}, u32[]{:S(2)}) copy-start(f32[2,2,2,2,16,2,16]{6,5,4,3,0,1,2:T(2,128)} %copy.38) | copy-start | bytes 98308
  33.4 4.8 %copy-start.17 = (pred[4]{0:T(512)(128)(4,1)S(1)}, pred[4]{0:T(512)(128)(4,1)}, u32[]{:S(2)}) copy-start(pred[4]{0:T(512)(128)(4,1)} %and_compare_fusion.1) | copy-start | bytes 16
  33.4 5.6 %copy-start.15 = (pred[2,2]{1,0:T(4,128)(4,1)S(1)}, pred[2,2]{1,0:T(4,128)(4,1)}, u32[]{:S(2)}) copy-start(pred[2,2]{1,0:T(4,128)(4,1)} %and_compare_fusion) | copy-start | bytes 16
  33.4 5.9 %copy-start.16 = (s32[4]{0:T(128)S(1)}, s32[4]{0:T(128)}, u32[]{:S(2)}) copy-start(s32[4]{0:T(128)} %iota_xor_fusion) | copy-start | bytes 52
  38.2 2.5 %copy-start.8 = (f32[4,4,16,16]{3,2,1,0:T(8,128)S(1)}, f32[4,4,16,16]{3,2,1,0:T(8,128)}, u32[]{:S(2)}) copy-start(f32[4,4,16,16]{3,2,1,0:T(8,128)} %get-tuple-element.219) | copy-start | bytes 49156
  38.2 2.5 %copy-start.9 = (f32[4,4,16,16]{3,2,1,0:T(8,128)S(1)}, f32[4,4,16,16]{3,2,1,0:T(8,128)}, u32[]{:S(2)}) copy-start(f32[4,4,16,16]{3,2,1,0:T(8,128)} %get-tuple-element.220) | copy-start | bytes 49156
  44.9 12.9 %copy-start.2 = (f32[4,2,64,512]{3,2,1,0:T(8,128)}, f32[4,2,64,512]{3,2,1,0:T(8,128)S(1)}, u32[]{:S(2)}) copy-start(f32[4,2,64,512]{3,2,1,0:T(8,128)S(1)} %collective-permute-done.6.a1) | copy-start | bytes 3145732
  44.9 12.9 %copy-start.3 = (f32[4,2,64,512]{3,2,1,0:T(8,128)}, f32[4,2,64,512]{3,2,1,0:T(8,128)S(1)}, u32[]{:S(2)}) copy-start(f32[4,2,64,512]{3,2,1,0:T(8,128)S(1)} %collective-permute-done.7.a3) | copy-start | bytes 3145732
  44.9 37.2 %collective-permute-start.8 = (f32[4,2,64,512]{3,2,1,0:T(8,128)}, f32[4,2,64,512]{3,2,1,0:T(8,128)S(1)}, u32[]{:S(2)}, u32[]{:S(2)}) collective-permute-start(f32[4,2,64,512]{3,2,1,0:T(8,128)} %get-tuple-element.176), channel_id=1, source_target_pairs={{0,64},{8,72},{16,80},{24,88},{32,96},{40,104},{48,112},{56,120},{... | collective-permute-start | bytes 3145736 | tf_op jit(solution)/shard_map/ppermute | solution.py:341
  48.6 19.2 %collective-permute-start.3 = (f32[3,32,1024]{2,1,0:T(8,128)}, f32[3,32,1024]{2,1,0:T(8,128)}, u32[]{:S(2)}, u32[]{:S(2)}) collective-permute-start(f32[3,32,1024]{2,1,0:T(8,128)} %get-tuple-element.162), channel_id=1, source_target_pairs={{0,8},{8,16},{16,24},{24,0},{32,40},{40,48},{48,56},{56,32},{64,72... | collective-permute-start | bytes 1179656 | tf_op jit(solution)/shard_map/ppermute | solution.py:341
  49.7 18.1 %collective-permute-start.4 = (f32[3,32,1024]{2,1,0:T(8,128)}, f32[3,32,1024]{2,1,0:T(8,128)}, u32[]{:S(2)}, u32[]{:S(2)}) collective-permute-start(f32[3,32,1024]{2,1,0:T(8,128)} %get-tuple-element.163), channel_id=1, source_target_pairs={{0,16},{8,24},{16,0},{24,8},{32,48},{40,56},{48,32},{56,40},{64,80... | collective-permute-start | bytes 1179656 | tf_op jit(solution)/shard_map/ppermute | solution.py:341
  50.1 20.0 %collective-permute-start.5 = (f32[3,32,1024]{2,1,0:T(8,128)}, f32[3,32,1024]{2,1,0:T(8,128)}, u32[]{:S(2)}, u32[]{:S(2)}) collective-permute-start(f32[3,32,1024]{2,1,0:T(8,128)} %get-tuple-element.164), channel_id=1, source_target_pairs={{0,24},{8,0},{16,8},{24,16},{32,56},{40,32},{48,40},{56,48},{64,88... | collective-permute-start | bytes 1179656 | tf_op jit(solution)/shard_map/ppermute | solution.py:341
  57.9 17.8 %copy-start.21 = (f32[3,32,1024]{2,1,0:T(8,128)S(1)}, f32[3,32,1024]{2,1,0:T(8,128)}, u32[]{:S(2)}) copy-start(f32[3,32,1024]{2,1,0:T(8,128)} %get-tuple-element.193) | copy-start | bytes 1179652
  57.9 38.2 %all-to-all-start = ((f32[128,2,16,128]{3,2,1,0:T(8,128)}), f32[128,2,16,128]{3,2,1,0:T(8,128)S(1)}, u32[]{:S(2)}, u32[]{:S(2)}) async-start(f32[128,2,16,128]{3,2,1,0:T(8,128)} %bitcast.153), calls=%async_computation | async-start | bytes 4194304 | tf_op jit(solution)/shard_map/all_to_all | solution.py:397
  70.1 42.5 %collective-permute-start.9 = (f32[3,32,1024]{2,1,0:T(8,128)}, f32[3,32,1024]{2,1,0:T(8,128)}, u32[]{:S(2)}, u32[]{:S(2)}) collective-permute-start(f32[3,32,1024]{2,1,0:T(8,128)} %get-tuple-element.191), channel_id=1, source_target_pairs={{0,8},{8,16},{16,24},{24,0},{32,40},{40,48},{48,56},{56,32},{64,72... | collective-permute-start | bytes 1179656 | tf_op jit(solution)/shard_map/ppermute | solution.py:341
  70.1 50.4 %collective-permute-start.10 = (f32[3,32,1024]{2,1,0:T(8,128)}, f32[3,32,1024]{2,1,0:T(8,128)}, u32[]{:S(2)}, u32[]{:S(2)}) collective-permute-start(f32[3,32,1024]{2,1,0:T(8,128)} %get-tuple-element.192), channel_id=1, source_target_pairs={{0,16},{8,24},{16,0},{24,8},{32,48},{40,56},{48,32},{56,40},{64,80... | collective-permute-start | bytes 1179656 | tf_op jit(solution)/shard_map/ppermute | solution.py:341
  75.7 44.9 %collective-permute-start.11 = (f32[3,32,1024]{2,1,0:T(8,128)S(1)}, f32[3,32,1024]{2,1,0:T(8,128)}, u32[]{:S(2)}, u32[]{:S(2)}) collective-permute-start(f32[3,32,1024]{2,1,0:T(8,128)S(1)} %copy-done.21), channel_id=1, source_target_pairs={{0,24},{8,0},{16,8},{24,16},{32,56},{40,32},{48,40},{56,48},{64,88... | collective-permute-start | bytes 1179656 | tf_op jit(solution)/shard_map/ppermute | solution.py:341
  82.2 4.2 %copy-start.4 = (f32[4,2,64,512]{3,2,1,0:T(8,128)}, f32[4,2,64,512]{3,2,1,0:T(8,128)S(1)}, u32[]{:S(2)}) copy-start(f32[4,2,64,512]{3,2,1,0:T(8,128)S(1)} %collective-permute-done.8.a2) | copy-start | bytes 3145732
  96.0 6.0 %copy-start.5 = (f32[128,2,16,128]{3,2,1,0:T(8,128)}, f32[128,2,16,128]{3,2,1,0:T(8,128)S(1)}, u32[]{:S(2)}) copy-start(f32[128,2,16,128]{3,2,1,0:T(8,128)S(1)} %all-to-all-done) | copy-start | bytes 6291460
  96.0 28.4 %all-to-all-start.1 = ((f32[128,1,16,128]{3,2,1,0:T(8,128)}), f32[128,1,16,128]{3,2,1,0:T(8,128)S(1)}, u32[]{:S(2)}, u32[]{:S(2)}) async-start(f32[128,1,16,128]{3,2,1,0:T(8,128)} %bitcast.157), calls=%async_computation.1 | async-start | bytes 2097152 | tf_op jit(solution)/shard_map/all_to_all | solution.py:397
  108.9 30.5 %collective-permute-start.15 = (f32[2,2,64,512]{3,2,1,0:T(8,128)}, f32[2,2,64,512]{3,2,1,0:T(8,128)S(1)}, u32[]{:S(2)}, u32[]{:S(2)}) collective-permute-start(f32[2,2,64,512]{3,2,1,0:T(8,128)} %get-tuple-element.204), channel_id=1, source_target_pairs={{0,32},{8,40},{16,48},{24,56},{32,64},{40,72},{48,80},{56,88},{64,... | collective-permute-start | bytes 1572872 | tf_op jit(solution)/shard_map/ppermute | solution.py:341
  109.9 38.0 %collective-permute-start.16 = (f32[2,2,64,512]{3,2,1,0:T(8,128)}, f32[2,2,64,512]{3,2,1,0:T(8,128)S(1)}, u32[]{:S(2)}, u32[]{:S(2)}) collective-permute-start(f32[2,2,64,512]{3,2,1,0:T(8,128)} %get-tuple-element.205), channel_id=1, source_target_pairs={{0,64},{8,72},{16,80},{24,88},{32,96},{40,104},{48,112},{56,120},{... | collective-permute-start | bytes 1572872 | tf_op jit(solution)/shard_map/ppermute | solution.py:341
  112.6 35.2 %collective-permute-start.17 = (f32[2,2,64,512]{3,2,1,0:T(8,128)}, f32[2,2,64,512]{3,2,1,0:T(8,128)}, u32[]{:S(2)}, u32[]{:S(2)}) collective-permute-start(f32[2,2,64,512]{3,2,1,0:T(8,128)} %get-tuple-element.206), channel_id=1, source_target_pairs={{0,96},{8,104},{16,112},{24,120},{32,0},{40,8},{48,16},{56,24},{64... | collective-permute-start | bytes 1572872 | tf_op jit(solution)/shard_map/ppermute | solution.py:341
  124.4 6.8 %copy-start = (f32[128,1,16,128]{3,2,1,0:T(8,128)}, f32[128,1,16,128]{3,2,1,0:T(8,128)S(1)}, u32[]{:S(2)}) copy-start(f32[128,1,16,128]{3,2,1,0:T(8,128)S(1)} %all-to-all-done.1) | copy-start | bytes 3145732
  124.4 28.9 %all-to-all-start.2 = ((f32[128,1,16,128]{3,2,1,0:T(8,128)}), f32[128,1,16,128]{3,2,1,0:T(8,128)S(1)}, u32[]{:S(2)}, u32[]{:S(2)}) async-start(f32[128,1,16,128]{3,2,1,0:T(8,128)} %bitcast.158), calls=%async_computation.2 | async-start | bytes 2097152 | tf_op jit(solution)/shard_map/all_to_all | solution.py:397
  135.7 23.1 %collective-permute-start.12 = (f32[1,2,64,512]{3,2,1,0:T(8,128)}, f32[1,2,64,512]{3,2,1,0:T(8,128)S(1)}, u32[]{:S(2)}, u32[]{:S(2)}) collective-permute-start(f32[1,2,64,512]{3,2,1,0:T(8,128)} %get-tuple-element.200), channel_id=1, source_target_pairs={{0,32},{8,40},{16,48},{24,56},{32,64},{40,72},{48,80},{56,88},{64,... | collective-permute-start | bytes 786440 | tf_op jit(solution)/shard_map/ppermute | solution.py:341
  136.7 25.0 %collective-permute-start.13 = (f32[1,2,64,512]{3,2,1,0:T(8,128)}, f32[1,2,64,512]{3,2,1,0:T(8,128)S(1)}, u32[]{:S(2)}, u32[]{:S(2)}) collective-permute-start(f32[1,2,64,512]{3,2,1,0:T(8,128)} %get-tuple-element.201), channel_id=1, source_target_pairs={{0,64},{8,72},{16,80},{24,88},{32,96},{40,104},{48,112},{56,120},{... | collective-permute-start | bytes 786440 | tf_op jit(solution)/shard_map/ppermute | solution.py:341
  139.4 8.5 %copy-start.19 = (f32[2,2,64,512]{3,2,1,0:T(8,128)}, f32[2,2,64,512]{3,2,1,0:T(8,128)S(1)}, u32[]{:S(2)}) copy-start(f32[2,2,64,512]{3,2,1,0:T(8,128)S(1)} %collective-permute-done.15.refs_1_) | copy-start | bytes 1572868
  139.4 22.3 %collective-permute-start.14 = (f32[1,2,64,512]{3,2,1,0:T(8,128)}, f32[1,2,64,512]{3,2,1,0:T(8,128)S(1)}, u32[]{:S(2)}, u32[]{:S(2)}) collective-permute-start(f32[1,2,64,512]{3,2,1,0:T(8,128)} %get-tuple-element.202), channel_id=1, source_target_pairs={{0,96},{8,104},{16,112},{24,120},{32,0},{40,8},{48,16},{56,24},{64... | collective-permute-start | bytes 786440 | tf_op jit(solution)/shard_map/ppermute | solution.py:341
  147.9 0.8 copy-start.20
  153.4 1.0 copy-start.1
  158.8 7.0 %copy-start.22 = (f32[1,2,64,512]{3,2,1,0:T(8,128)}, f32[1,2,64,512]{3,2,1,0:T(8,128)S(1)}, u32[]{:S(2)}) copy-start(f32[1,2,64,512]{3,2,1,0:T(8,128)S(1)} %collective-permute-done.12.refs_1_) | copy-start | bytes 786436
  161.7 4.1 %copy-start.23 = (f32[1,2,64,512]{3,2,1,0:T(8,128)}, f32[1,2,64,512]{3,2,1,0:T(8,128)S(1)}, u32[]{:S(2)}) copy-start(f32[1,2,64,512]{3,2,1,0:T(8,128)S(1)} %collective-permute-done.13.refs_2_) | copy-start | bytes 786436
  161.7 4.1 %copy-start.24 = (f32[1,2,64,512]{3,2,1,0:T(8,128)}, f32[1,2,64,512]{3,2,1,0:T(8,128)S(1)}, u32[]{:S(2)}) copy-start(f32[1,2,64,512]{3,2,1,0:T(8,128)S(1)} %collective-permute-done.14.refs_3_) | copy-start | bytes 786436
  161.7 15.2 %collective-permute-start.18 = (f32[1,2,64,512]{3,2,1,0:T(8,128)}, f32[1,2,64,512]{3,2,1,0:T(8,128)S(1)}, u32[]{:S(2)}, u32[]{:S(2)}) collective-permute-start(f32[1,2,64,512]{3,2,1,0:T(8,128)} %get-tuple-element.211), channel_id=1, source_target_pairs={{0,32},{8,40},{16,48},{24,56},{32,64},{40,72},{48,80},{56,88},{64,... | collective-permute-start | bytes 786440 | tf_op jit(solution)/shard_map/ppermute | solution.py:341
  162.1 14.8 %collective-permute-start.19 = (f32[1,2,64,512]{3,2,1,0:T(8,128)}, f32[1,2,64,512]{3,2,1,0:T(8,128)S(1)}, u32[]{:S(2)}, u32[]{:S(2)}) collective-permute-start(f32[1,2,64,512]{3,2,1,0:T(8,128)} %get-tuple-element.212), channel_id=1, source_target_pairs={{0,64},{8,72},{16,80},{24,88},{32,96},{40,104},{48,112},{56,120},{... | collective-permute-start | bytes 786440 | tf_op jit(solution)/shard_map/ppermute | solution.py:341
  164.2 13.4 %collective-permute-start.20 = (f32[1,2,64,512]{3,2,1,0:T(8,128)}, f32[1,2,64,512]{3,2,1,0:T(8,128)S(1)}, u32[]{:S(2)}, u32[]{:S(2)}) collective-permute-start(f32[1,2,64,512]{3,2,1,0:T(8,128)} %get-tuple-element.213), channel_id=1, source_target_pairs={{0,96},{8,104},{16,112},{24,120},{32,0},{40,8},{48,16},{56,24},{64... | collective-permute-start | bytes 786440 | tf_op jit(solution)/shard_map/ppermute | solution.py:341
  176.9 0.7 copy-start.10
  176.9 0.8 copy-start.11
  177.7 0.7 copy-start.12
